TPU v7x, 512 devices: a whole 4x8x8 slice. The times are simulated.
512 devices in a mesh: segment: 16 (over z_hi, y), ctx: 8 (over x, core), mp: 4 (over z_lo).
Axes of the slice: x: 4, y: 8, z: 8 (z_hi: 2, z_lo: 4; z = z_hi * 4 + z_lo), core: 2. Of those that a mesh axis runs over, the one named last changes fastest.
Arguments:
- queries: bfloat16 [16, 2, 1024, 2048], P('segment', None, 'ctx', 'mp')
- enc_states: bfloat16 [2, 2048, 4096], P(None, 'ctx', 'segment'), may hold values from -6 to 6
- key_weight: bfloat16 [16, 4096, 2048], P('segment', 'ctx', 'mp'), may hold values from -0.09375 to 0.09375
- value_weight: bfloat16 [16, 4096, 2048], P('segment', 'ctx', 'mp'), may hold values from -0.09375 to 0.09375
- enc_lengths: int32 [2], replicated, may hold values from 1025 to 2048, as said below
Outputs:
- context: bfloat16 [16, 2, 1024, 2048], P('segment', None, 'ctx', 'mp')
Inputs may be any that keep to these rules, and one draw needn't show every extreme that they name: `enc_lengths`: every document has more than half of 2048 valid positions, and at least one document is full.
All inputs are finite; a program needn't handle non-finite values.
Results may differ from a plain program's by a relative error of at most 0.012.
The roundings to bfloat16 on the way count: a program that leaves them out, or rounds other values in their place, can miss the bound.
Values may be sent and summed in bfloat16 or wider, within the bound.
No kernel may reach another device: no remote copies, remote signals or barrier semaphores. Data moves between devices by JAX's collectives and lax.ppermute only.
A program may use at most 64 MiB of HBM per device.

v0:
```python
import math

import jax
import jax.numpy as jnp
from jax import lax
from jax.sharding import Mesh
from jax.sharding import PartitionSpec as P

HEAD_DIM = 256
SEGMENT = ("segment_0", "segment_1")


def joined_along(blocks, dim):
    blocks = jnp.moveaxis(blocks, 0, dim)
    lengths = blocks.shape
    return blocks.reshape(*lengths[:dim], lengths[dim] * lengths[dim + 1], *lengths[dim + 2 :])


def all_blocks(array, axes, sequence):
    blocks = array
    for k in sequence:
        blocks = lax.all_gather(blocks, axes[k])
    done = sequence[::-1]
    back = [done.index(k) for k in range(len(axes))]
    blocks = blocks.transpose(*back, *range(len(axes), blocks.ndim))
    return blocks.reshape(-1, *array.shape)


def whole_of(array, axes, sequence, dim):
    return joined_along(all_blocks(array, axes, sequence), dim)


def in_one_piece(arrays, axis, dim, along):
    both = jnp.concatenate(arrays, axis=along)
    whole, at, finished = (lax.all_gather(both, axis, axis=dim, tiled=True), 0, [])
    for a in arrays:
        finished.append(lax.slice_in_dim(whole, at, at + a.shape[along], axis=along))
        at += a.shape[along]
    return tuple(finished)


def attend(query_heads, lengths, pieces, carry, scale):
    top, total, summed = carry
    key_piece, value_piece = pieces
    batch, rows, width = key_piece.shape
    heads = query_heads.shape[2]
    key_heads = key_piece.reshape(batch, rows, heads, width // heads)
    value_heads = value_piece.reshape(batch, rows, heads, width // heads)
    scores = (
        jnp.einsum("mthd,mlhd->mhtl", query_heads, key_heads, preferred_element_type=jnp.float32)
        * scale
    )
    places = lax.iota(jnp.int32, rows)
    valid = places[None, :] < lengths[:, None]
    scores = jnp.where(valid[:, None, None, :], scores, -jnp.inf)
    new_top = jnp.maximum(top, jnp.max(scores, axis=-1))
    weights = jnp.exp(scores - new_top[..., None])
    total = jnp.sum(weights, axis=-1)
    summed = jnp.einsum(
        "mhtl,mlhd->mhtd",
        weights.astype(jnp.bfloat16),
        value_heads,
        preferred_element_type=jnp.float32,
    )
    return (new_top, total, summed)


def start_carry(query_heads):
    batch, tokens, heads, depth = query_heads.shape
    top = jnp.full((batch, heads, tokens), -1e30, jnp.float32)
    total = jnp.zeros((batch, heads, tokens), jnp.float32)
    summed = jnp.zeros((batch, heads, tokens, depth), jnp.float32)
    return (top, total, summed)


def finish(carry):
    top, total, summed = carry
    mixed = summed / total[..., None]
    batch, heads, tokens, depth = mixed.shape
    return mixed.transpose(0, 2, 1, 3).reshape(batch, tokens, heads * depth)


def on_device(queries, enc_states, key_weight, value_weight, enc_lengths):
    w_key = key_weight[0]
    w_value = value_weight[0]
    batch, positions, _ = enc_states.shape
    width = w_key.shape[1]
    heads = width // HEAD_DIM
    scale = 1.0 / math.sqrt(HEAD_DIM)
    whole = whole_of(enc_states, SEGMENT, (0, 1), 2)
    pieces = in_one_piece((w_key, w_value), "ctx", 0, 1)
    keys_sum = jnp.einsum("mef,fh->meh", whole, pieces[0], preferred_element_type=jnp.float32)
    values_sum = jnp.einsum("mef,fh->meh", whole, pieces[1], preferred_element_type=jnp.float32)
    keys = keys_sum
    values = values_sum
    keys = keys.astype(jnp.bfloat16)
    values = values.astype(jnp.bfloat16)
    local_queries = queries[0]
    tokens = local_queries.shape[1]
    query_heads = local_queries.reshape(batch, tokens, heads, HEAD_DIM)
    carry = attend(
        query_heads,
        enc_lengths,
        in_one_piece((keys, values), "ctx", 1, 0),
        start_carry(query_heads),
        scale,
    )
    mixed = finish(carry)
    return mixed.astype(jnp.bfloat16)[None]


def solution(mesh):
    torus = Mesh(
        mesh.devices.reshape(2, 8, mesh.shape["ctx"], mesh.shape["mp"]),
        ("segment_0", "segment_1", "ctx", "mp"),
    )
    return jax.shard_map(
        on_device,
        mesh=torus,
        in_specs=(
            P(SEGMENT, None, "ctx", "mp"),
            P(None, "ctx", SEGMENT),
            P(SEGMENT, "ctx", "mp"),
            P(SEGMENT, "ctx", "mp"),
            P(),
        ),
        out_specs=P(SEGMENT, None, "ctx", "mp"),
        check_vma=False,
    )
```

profile of v0, /device:TPU:1, one launch (start us, length us, event | category | flops | bytes accessed | tf_op | source)
XLA Modules:
  0.0 232.8 jit_solution(11223218702413829260)
XLA Ops:
  6.5 0.0 all-gather.10.cloned.1.call-start
  6.5 19.6 %all-gather = bf16[4,256,256]{2,1,0:T(8,128)(2,1)} all-gather(bf16[2,256,256]{2,1,0:T(8,128)(2,1)} %param.6), channel_id=2, replica_groups=mesh['segment_0'=2,'segment_1'=8,'ctx'=8,'mp'=4] {'segment_0'}, dimensions={0}, use_global_device_ids=true | all-gather | bytes 786432 | tf_op jit(solution)/shard_map/all_gather | solution.py:22
  26.1 0.0 all-gather.10.cloned.1.call-update
  26.1 0.0 all-gather.6.cloned.1.call-start
  26.2 1.3 copy.22
  27.4 1.3 copy.23
  28.7 1.0 pad_maximum_fusion
  29.7 0.0 all-gather.6.cloned.1.call-update
  29.8 0.0 all-gather.8.cloned.1.call-start
  29.8 58.6 %all-gather.10.cloned.1.call-done = bf16[16,2,256,256]{3,2,1,0:T(8,128)(2,1)} async-done(((bf16[2,2,256,256]{3,2,1,0:T(8,128)(2,1)}), bf16[16,2,256,256]{3,2,1,0:T(8,128)(2,1)}) %all-gather.10.cloned.1.call-update) | async-done | bytes 4194320 | tf_op jit(solution)/shard_map/all_gather | solution.py:22
  88.4 6.5 %copy.39 = bf16[2,8,2,256,256]{4,1,0,3,2:T(8,128)(2,1)} copy(bf16[2,8,2,256,256]{4,3,2,0,1:T(8,128)(2,1)} %bitcast.64) | data formatting | bytes 8388608 | tf_op jit(solution)/shard_map/transpose | solution.py:25
  94.9 7.4 %reshape.46 = bf16[2,256,4096]{2,1,0:T(8,128)(2,1)} reshape(bf16[2,256,16,256]{3,2,1,0:T(8,128)(2,1)} %bitcast.63) | data formatting | bytes 8388608 | tf_op jit(solution)/shard_map/reshape | solution.py:16
  102.3 42.8 %all-gather.6.cloned.1.call-done = bf16[4096,1024]{0,1:T(8,128)(2,1)} async-done(((bf16[512,1024]{0,1:T(8,128)(2,1)}), bf16[4096,1024]{0,1:T(8,128)(2,1)}) %all-gather.6.cloned.1.call-update) | async-done | bytes 8388624 | tf_op jit(solution)/shard_map/all_gather | solution.py:35
  145.1 0.0 copy-start
  145.1 0.0 copy-start.3
  145.1 6.0 %fusion.16 = bf16[2,256,512]{1,2,0:T(8,128)(2,1)S(1)} fusion(bf16[2,256,4096]{2,1,0:T(8,128)(2,1)} %reshape.46, bf16[4096,1024]{0,1:T(8,128)(2,1)} %all-gather.6.cloned.1.call-done), kind=kOutput, calls=%fused_computation.19 | convolution fusion | flops 2147745792 | bytes 8912896 | tf_op jit(solution)/shard_map/mef,fh->meh/dot_general | solution.py:93
  151.0 0.0 copy-done
  151.0 1.1 copy-done.3
  152.2 0.0 copy-start.1
  152.2 0.0 copy-start.2
  152.2 2.4 %fusion.17 = bf16[2,256,512]{1,2,0:T(8,128)(2,1)S(1)} fusion(bf16[2,256,4096]{2,1,0:T(8,128)(2,1)S(1)} %copy-done, bf16[4096,1024]{0,1:T(8,128)(2,1)S(1)} %copy-done.3), kind=kOutput, calls=%fused_computation.20 | convolution fusion | flops 2147745792 | bytes 8912896 | tf_op jit(solution)/shard_map/mef,fh->meh/dot_general | solution.py:92
  154.5 1.1 pad_maximum_fusion.1
  155.7 0.0 all-gather.8.cloned.1.call-update
  155.7 0.0 copy-done.1
  155.7 0.1 reshape_squeeze.3
  155.8 0.0 copy-done.2
  155.8 0.1 iota_compare_fusion
  155.9 59.5 %all-gather.8.cloned.1.call-done = bf16[4,2048,512]{1,2,0:T(8,128)(2,1)} async-done(((bf16[4,256,512]{1,2,0:T(8,128)(2,1)}), bf16[4,2048,512]{1,2,0:T(8,128)(2,1)}) %all-gather.8.cloned.1.call-update) | async-done | bytes 8388624 | tf_op jit(solution)/shard_map/all_gather | solution.py:35
  215.4 4.0 %fusion.28 = (bf16[2,2048,512]{1,2,0:T(8,128)(2,1)S(1)}, bf16[2,2048,512]{1,2,0:T(8,128)(2,1)S(1)}) fusion(bf16[4,2048,512]{1,2,0:T(8,128)(2,1)} %all-gather.8.cloned.1.call-done), kind=kLoop, calls=%fused_computation.31 | loop fusion | bytes 16777216 | tf_op jit(solution)/shard_map/slice | solution.py:37
  219.4 2.1 bitcast_reduce_fusion
  221.5 1.2 fusion.3
  222.8 2.5 %fusion.21 = bf16[2,128,2,256]{3,1,2,0:T(8,128)(2,1)S(1)} fusion(bf16[2,2048,2,256]{1,3,2,0:T(8,128)(2,1)S(1)} %bitcast.65, f32[2,2,2048,128]{3,2,1,0:T(8,128)S(1)} %get-tuple-element.8, f32[2,2,128]{2,1,0:T(2,128)S(1)} %broadcast_maximum_fusion, pred[2,2048]{1,0:T(4,128)(4,1)S(1)} %iota_compare_fusion, f32[2,128,2]{1,2,0:T(2,128)S(1)} %bitcast.71), kind=kOutput, calls=%fused_computation.24 | convolution fusion | flops 541327360 | bytes 8658944 | tf_op jit(solution)/shard_map/mhtl,mlhd->mhtd/dot_general | solution.py:59
  225.3 0.2 copy.29
  225.5 0.9 copy.30
  (1 shorter events, 0.0 us)
Async XLA Ops:
  6.5 81.9 %all-gather.10.cloned.1.call-start = ((), (), s32[]{:S(2)}) async-start(), calls=%async_computation.2 | async-start | bytes 4718592 | tf_op jit(solution)/shard_map/all_gather | solution.py:22
  26.1 118.9 %all-gather.6.cloned.1.call-start = ((), (), s32[]{:S(2)}) async-start(), calls=%async_computation | async-start | bytes 9437184 | tf_op jit(solution)/shard_map/all_gather | solution.py:35
  29.8 185.6 %all-gather.8.cloned.1.call-start = ((), (), s32[]{:S(2)}) async-start(), calls=%async_computation.1 | async-start | bytes 9437184 | tf_op jit(solution)/shard_map/all_gather | solution.py:35
  145.1 6.0 %copy-start = (bf16[2,256,4096]{2,1,0:T(8,128)(2,1)S(1)}, bf16[2,256,4096]{2,1,0:T(8,128)(2,1)}, u32[]{:S(2)}) copy-start(bf16[2,256,4096]{2,1,0:T(8,128)(2,1)} %reshape.46) | copy-start | bytes 12582916
  145.1 7.1 %copy-start.3 = (bf16[4096,1024]{0,1:T(8,128)(2,1)S(1)}, bf16[4096,1024]{0,1:T(8,128)(2,1)}, u32[]{:S(2)}) copy-start(bf16[4096,1024]{0,1:T(8,128)(2,1)} %all-gather.6.cloned.1.call-done) | copy-start | bytes 25165828
  152.2 3.5 %copy-start.1 = (bf16[1,2,128,512]{3,2,1,0:T(8,128)(2,1)S(1)}, bf16[1,2,128,512]{3,2,1,0:T(8,128)(2,1)}, u32[]{:S(2)}) copy-start(bf16[1,2,128,512]{3,2,1,0:T(8,128)(2,1)} %param.5) | copy-start | bytes 786436
  152.2 3.6 %copy-start.2 = (s32[2]{0:T(128)S(1)}, s32[2]{0:T(128)}, u32[]{:S(2)}) copy-start(s32[2]{0:T(128)} %param.9) | copy-start | bytes 28
Sparse Core Ops, SparseCore 0:
  26.2 62.1 all-gather.9
  90.5 54.4 all-gather.5
  155.8 59.4 all-gather.7
where the time goes:
time: 233 us
  waiting for transfers between devices  161 us (69%)
  local copies, waits for them, and re-layouts  22.6 us (10%)
  blocking collectives  19.6 us (8%)
  between operations  13.2 us (6%)
  matrix products  12.9 us (6%)
  other arithmetic  3.52 us (2%)
    all_gather x2, waiting for transfers between devices, in_one_piece(): lax.all_gather(both, axis, axis=dim, tiled=True)  102 us
    all_gather x1, waiting for transfers between devices, all_blocks(): blocks = lax.all_gather(blocks, axes[k])  58.6 us
    all_gather x1, blocking collectives, all_blocks(): blocks = lax.all_gather(blocks, axes[k])  19.6 us
    reshape x1, local copies, waits for them, and re-layouts, joined_along(): blocks.reshape(*lengths[:dim], lengths[dim] * lengths[dim + 1], *lengths[...  7.39 us
    transpose x1, local copies, waits for them, and re-layouts, all_blocks(): blocks = blocks.transpose(*back, *range(len(axes), blocks.ndim))  6.49 us
    dot_general x1, matrix products, on_device(): jnp.einsum('mef,fh->meh', whole, pieces[1], preferred_element_type=jnp.fl...  5.96 us
  transfers between devices with their start and end apart: 3, of which 3 were waited for; matrix products, arithmetic and copies ran while one was open for 8% of the time, Pallas kernels for 0%

commit v1 on v0

v1 whole, which is shorter than its diff:
```python
import math

import jax
import jax.numpy as jnp
from jax import lax
from jax.experimental import pallas as pl
from jax.experimental.pallas import tpu as pltpu
from jax.sharding import Mesh
from jax.sharding import PartitionSpec as P

HEAD_DIM = 256
SEGMENT = ("zh", "y")
CTX = ("x", "c")
ROWS = 256
FEATS = 256
VMEM = pl.BlockSpec(memory_space=pltpu.VMEM)
SMEM = pl.BlockSpec(memory_space=pltpu.SMEM)
HBM = pl.BlockSpec(memory_space=pl.ANY)


def shift(array, axis, by):
    n = lax.axis_size(axis)
    return lax.ppermute(array, axis, [(i, (i + by) % n) for i in range(n)])


def ring_of_eight(block):
    up, down = block, block
    pieces = [block]
    for _ in range(3):
        up, down = shift(up, "y", 1), shift(down, "y", -1)
        pieces += [up, down]
    return pieces, (shift(up[0], "y", 1), shift(down[1], "y", -1))


def ring_of_four(block):
    half = block.shape[0] // 2
    right, left = shift(block, "x", 1), shift(block, "x", -1)
    return [block, right, left, shift(right[:half], "x", 1), shift(left[half:], "x", -1)]


Y_OFFSETS = (0, 7, 1, 6, 2, 5, 3)
X_OFFSETS = (0, 3, 1, 2, 2)


def store_heads(out, acc, n):
    kind, head = n // 2, n % 2
    for doc in range(2):
        out[doc * 2 + head, :, kind * HEAD_DIM : (kind + 1) * HEAD_DIM] = acc[doc * ROWS : (doc + 1) * ROWS]


def project_most_kernel(where, *refs):
    enc, own, other = refs[:7], refs[7:12], refs[12:17]
    out, w_left, enc_all, w_all, sem_e, sem_w = refs[17:]
    half, y, x, core = where[0], where[1], where[2], where[3]
    copies = []
    for side, blocks in enumerate((own, other)):
        for piece, ref in enumerate(blocks):
            block = lax.rem(x + X_OFFSETS[piece], 4)
            of_core = core if side == 0 else 1 - core
            row = block * 1024 + of_core * 512 + (256 if piece == 4 else 0)
            copies.append(
                pltpu.make_async_copy(
                    ref, w_all.at[pl.ds(pl.multiple_of(row, 256), ref.shape[0])], sem_w.at[len(copies)]
                )
            )
    halves = (half, 1 - half)
    for piece, ref in enumerate(enc):
        place = lax.rem(y + Y_OFFSETS[piece], 8)
        for near in range(2):
            column = pl.multiple_of((halves[near] * 8 + place) * FEATS, FEATS)
            copies.append(
                pltpu.make_async_copy(
                    ref.at[near], enc_all.at[:, :, pl.ds(column, FEATS)], sem_e.at[2 * piece + near]
                )
            )
    for copy in copies:
        copy.start()
    place = lax.rem(y + 4, 8)
    lefts = [pl.multiple_of((h * 8 + place) * FEATS, FEATS) for h in halves]
    for left in lefts:
        enc_all[:, :, pl.ds(left, FEATS)] = jnp.zeros((2, ROWS, FEATS), jnp.bfloat16)
    for copy in copies:
        copy.wait()
    for near in range(2):
        w_left[near] = w_all[pl.ds(lefts[near], FEATS), :]
    lhs = enc_all[...].reshape(2 * ROWS, 16 * FEATS)
    for n in range(4):
        cols = slice(n * HEAD_DIM, (n + 1) * HEAD_DIM)
        out[:, cols] = jnp.dot(lhs, w_all[:, cols], preferred_element_type=jnp.float32)


def project_most(where, enc, own, other):
    return pl.pallas_call(
        project_most_kernel,
        out_shape=(
            jax.ShapeDtypeStruct((2 * ROWS, 4 * HEAD_DIM), jnp.float32),
            jax.ShapeDtypeStruct((2, FEATS, 4 * HEAD_DIM), jnp.bfloat16),
        ),
        in_specs=[SMEM] + [HBM] * 17,
        out_specs=(VMEM, VMEM),
        scratch_shapes=[
            pltpu.VMEM((2, ROWS, 16 * FEATS), jnp.bfloat16),
            pltpu.VMEM((4096, 4 * HEAD_DIM), jnp.bfloat16),
            pltpu.SemaphoreType.DMA((14,)),
            pltpu.SemaphoreType.DMA((10,)),
        ],
        compiler_params=pltpu.CompilerParams(vmem_limit_bytes=60 * 2**20),
        cost_estimate=pl.CostEstimate(
            flops=2 * 512 * 4096 * 1024, bytes_accessed=14 * 2**20, transcendentals=0
        ),
        name="project_most",
    )(where, *enc, *own, *other)


def project_rest_kernel(near, far, partial, w_left, out):
    near_rows = near[...].reshape(2 * ROWS, FEATS)
    far_rows = far[...].reshape(2 * ROWS, FEATS)
    for n in range(4):
        cols = slice(n * HEAD_DIM, (n + 1) * HEAD_DIM)
        acc = jnp.dot(near_rows, w_left[0, :, cols], preferred_element_type=jnp.float32)
        acc += jnp.dot(far_rows, w_left[1, :, cols], preferred_element_type=jnp.float32)
        store_heads(out, (acc + partial[:, cols]).astype(jnp.bfloat16), n)


def project_rest(near, far, partial, w_left):
    return pl.pallas_call(
        project_rest_kernel,
        out_shape=jax.ShapeDtypeStruct((4, ROWS, 2 * HEAD_DIM), jnp.bfloat16),
        in_specs=[VMEM] * 4,
        out_specs=VMEM,
        compiler_params=pltpu.CompilerParams(vmem_limit_bytes=60 * 2**20),
        cost_estimate=pl.CostEstimate(
            flops=2 * 512 * 512 * 1024, bytes_accessed=5 * 2**20, transcendentals=0
        ),
        name="project_rest",
    )(near, far, partial, w_left)


def attend_kernel(where, lengths, query, mine, theirs, out):
    x, core = where[2], where[3]
    length = lengths[x // 2]
    scale = 1.0 / math.sqrt(HEAD_DIM)
    steps = [(ref, of, p) for of, ref in ((core, mine), (1 - core, theirs)) for p in range(4)]
    for chunk in range(4):
        q = query[chunk]
        scores = []
        for ref, of, p in steps:
            keys = ref[p, :, :HEAD_DIM]
            s = lax.dot_general(q, keys, (((1,), (1,)), ((), ())), preferred_element_type=jnp.float32)
            place = (p * 2 + of) * ROWS + lax.broadcasted_iota(jnp.int32, (1, ROWS), 1)
            scores.append(jnp.where(place < length, s * scale, -jnp.inf))
        top = scores[0]
        for s in scores[1:]:
            top = jnp.maximum(top, s)
        top = jnp.max(top, axis=1, keepdims=True)
        total, summed = None, None
        for s, (ref, _, p) in zip(scores, steps):
            w = jnp.exp(s - top)
            total = w if total is None else total + w
            o = jnp.dot(w.astype(jnp.bfloat16), ref[p, :, HEAD_DIM:], preferred_element_type=jnp.float32)
            summed = o if summed is None else summed + o
        total = jnp.sum(total, axis=1, keepdims=True)
        out[chunk] = (summed / total).astype(jnp.bfloat16)


def attend(where, lengths, query, mine, theirs):
    return pl.pallas_call(
        attend_kernel,
        out_shape=jax.ShapeDtypeStruct((4, 128, HEAD_DIM), jnp.bfloat16),
        in_specs=[SMEM, SMEM, VMEM, VMEM, VMEM],
        out_specs=VMEM,
        compiler_params=pltpu.CompilerParams(vmem_limit_bytes=60 * 2**20),
        cost_estimate=pl.CostEstimate(
            flops=4 * 512 * 2048 * 256, bytes_accessed=4 * 2**20, transcendentals=512 * 2048
        ),
        name="attend",
    )(where, lengths, query, mine, theirs)


def on_device(queries, enc_states, key_weight, value_weight, enc_lengths):
    zh, y = lax.axis_index("zh"), lax.axis_index("y")
    x, core = lax.axis_index("x"), lax.axis_index("c")
    where = jnp.stack([zh, y, x, core])

    far = shift(enc_states, "zh", 1)

    query = queries[0].reshape(2, 128, 2, HEAD_DIM).transpose(0, 2, 1, 3).reshape(4, 128, HEAD_DIM)
    query = lax.all_to_all(query, "x", 0, 0)

    weight = jnp.concatenate([key_weight[0], value_weight[0]], axis=1)
    weight, query = lax.optimization_barrier((weight, query))
    own = ring_of_four(weight)
    other = [shift(block, "c", 1) for block in own]
    enc, (rest_near, rest_far) = ring_of_eight(jnp.stack([enc_states, far]))

    most, w_left = project_most(where, enc, own, other)
    both = project_rest(rest_near, rest_far, most, w_left)
    mine = lax.all_to_all(both, "x", 0, 0)
    theirs = shift(mine, "c", 1)
    mixed = attend(where, enc_lengths, query, mine, theirs)
    mixed = lax.all_to_all(mixed, "x", 0, 0)
    mixed = mixed.reshape(2, 2, 128, HEAD_DIM).transpose(0, 2, 1, 3).reshape(2, 128, 2 * HEAD_DIM)
    return mixed[None]


def solution(mesh):
    torus = Mesh(mesh.devices.reshape(2, 8, 4, 2, 4), ("zh", "y", "x", "c", "mp"))
    return jax.shard_map(
        on_device,
        mesh=torus,
        in_specs=(
            P(SEGMENT, None, CTX, "mp"),
            P(None, CTX, SEGMENT),
            P(SEGMENT, CTX, "mp"),
            P(SEGMENT, CTX, "mp"),
            P(),
        ),
        out_specs=P(SEGMENT, None, CTX, "mp"),
        check_vma=False,
    )
```

time: 233 us -> 160 us (0.69)
  the two profiles are of different devices: /device:TPU:1 before, /device:TPU:152 now
where the time goes in v1:
time: 160 us; the launch traced here: 159 us
  starting transfers between devices  67.1 us (42%)
  waiting for transfers between devices  32.7 us (20%)
  blocking collectives  29.6 us (18%)
  Pallas kernels  20.6 us (13%)
  local copies, waits for them, and re-layouts  6.81 us (4%)
  other arithmetic  1.92 us (1%)
    ppermute x19, starting transfers between devices, shift(): return lax.ppermute(array, axis, [(i, (i + by) % n) for i in range(n)])  62.8 us
    ppermute x19, waiting for transfers between devices, shift(): return lax.ppermute(array, axis, [(i, (i + by) % n) for i in range(n)])  27.4 us
    all_to_all x1, blocking collectives, on_device(): mine = lax.all_to_all(both, 'x', 0, 0)  19 us
    pallas_call x1, Pallas kernels, project_most(): pl.pallas_call(project_most_kernel, out_shape=(jax.ShapeDtypeStruct((2 *...  11.5 us
    all_to_all x1, blocking collectives, on_device(): mixed = lax.all_to_all(mixed, 'x', 0, 0)  10.6 us
    pallas_call x1, Pallas kernels, attend(): pl.pallas_call(attend_kernel, out_shape=jax.ShapeDtypeStruct((4, 128, HEA...  5.37 us
    all_to_all x1, waiting for transfers between devices, on_device(): query = lax.all_to_all(query, 'x', 0, 0)  5.35 us
    all_to_all x1, starting transfers between devices, on_device(): query = lax.all_to_all(query, 'x', 0, 0)  4.29 us
  transfers between devices with their start and end apart: 20, of which 7 were waited for; matrix products, arithmetic and copies ran while one was open for 3% of the time, Pallas kernels for 7%

profile of v1, /device:TPU:152, one launch (start us, length us, event | category | flops | bytes accessed | tf_op | source)
XLA Modules:
  0.0 159.1 jit_solution(6841831876249381375)
XLA Ops:
  0.0 1.1 reshape_squeeze.3
  1.1 0.7 copy.6
  1.8 4.3 %all-to-all-start = ((bf16[4,128,256]{2,1,0:T(8,128)(2,1)}), bf16[4,128,256]{2,1,0:T(8,128)(2,1)S(1)}, u32[]{:S(2)}, u32[]{:S(2)}) async-start(bf16[4,128,256]{2,1,0:T(8,128)(2,1)} %bitcast.7), calls=%async_computation | async-start | bytes 524288 | tf_op jit(solution)/shard_map/all_to_all | solution.py:188
  6.1 1.3 pad_maximum_fusion.refs_7_
  7.4 0.0 copy-start
  7.4 5.4 %all-to-all-done.query = bf16[4,128,256]{2,1,0:T(8,128)(2,1)S(1)} async-done(((bf16[4,128,256]{2,1,0:T(8,128)(2,1)}), bf16[4,128,256]{2,1,0:T(8,128)(2,1)S(1)}, u32[]{:S(2)}, u32[]{:S(2)}) %all-to-all-start) | async-done | bytes 262176 | tf_op jit(solution)/shard_map/all_to_all | solution.py:188
  12.8 2.5 %collective-permute-start.9 = (bf16[512,1024]{1,0:T(8,128)(2,1)S(1)}, bf16[512,1024]{1,0:T(8,128)(2,1)S(1)}, u32[]{:S(2)}, u32[]{:S(2)}) collective-permute-start(bf16[512,1024]{1,0:T(8,128)(2,1)S(1)} %pad_maximum_fusion.refs_7_), channel_id=1, source_target_pairs={{0,8},{8,16},{16,24},{24,0},{1,9},{9,17},{17,25},{25,1},{2,10},{10... | collective-permute-start | bytes 3145736 | tf_op jit(solution)/shard_map/ppermute | solution.py:23
  15.2 4.6 %collective-permute-start.10 = (bf16[512,1024]{1,0:T(8,128)(2,1)S(1)}, bf16[512,1024]{1,0:T(8,128)(2,1)}, u32[]{:S(2)}, u32[]{:S(2)}) collective-permute-start(bf16[512,1024]{1,0:T(8,128)(2,1)S(1)} %pad_maximum_fusion.refs_7_), channel_id=1, source_target_pairs={{0,24},{8,0},{16,8},{24,16},{1,25},{9,1},{17,9},{25,17},{2,26},{10... | collective-permute-start | bytes 3145736 | tf_op jit(solution)/shard_map/ppermute | solution.py:23
  19.8 0.0 copy-done.7
  19.8 9.1 %collective-permute-start = (bf16[2,256,256]{2,1,0:T(8,128)(2,1)S(1)}, bf16[2,256,256]{2,1,0:T(8,128)(2,1)S(1)}, u32[]{:S(2)}, u32[]{:S(2)}) collective-permute-start(bf16[2,256,256]{2,1,0:T(8,128)(2,1)S(1)} %copy-done.7), channel_id=1, source_target_pairs={{0,256},{256,0},{1,257},{257,1},{2,258},{258,2},{3,259},{259,3},{4... | collective-permute-start | bytes 786440 | tf_op jit(solution)/shard_map/ppermute | solution.py:23
  29.0 9.9 %collective-permute-done = bf16[2,256,256]{2,1,0:T(8,128)(2,1)S(1)} collective-permute-done((bf16[2,256,256]{2,1,0:T(8,128)(2,1)S(1)}, bf16[2,256,256]{2,1,0:T(8,128)(2,1)S(1)}, u32[]{:S(2)}, u32[]{:S(2)}) %collective-permute-start) | collective-permute-done | bytes 262176 | tf_op jit(solution)/shard_map/ppermute | solution.py:23
  38.9 0.1 pad_maximum_fusion.1.refs_0_
  38.9 0.0 copy-start.2
  39.0 4.7 %collective-permute-start.1 = (bf16[2,2,256,256]{3,2,1,0:T(8,128)(2,1)S(1)}, bf16[2,2,256,256]{3,2,1,0:T(8,128)(2,1)S(1)}, u32[]{:S(2)}, u32[]{:S(2)}) collective-permute-start(bf16[2,2,256,256]{3,2,1,0:T(8,128)(2,1)S(1)} %pad_maximum_fusion.1.refs_0_), channel_id=1, source_target_pairs={{0,32},{32,64},{64,96},{96,128},{128,160},{160,192},{192,224},{224... | collective-permute-start | bytes 1572872 | tf_op jit(solution)/shard_map/ppermute | solution.py:23
  43.7 1.9 %collective-permute-start.5 = (bf16[2,2,256,256]{3,2,1,0:T(8,128)(2,1)S(1)}, bf16[2,2,256,256]{3,2,1,0:T(8,128)(2,1)S(1)}, u32[]{:S(2)}, u32[]{:S(2)}) collective-permute-start(bf16[2,2,256,256]{3,2,1,0:T(8,128)(2,1)S(1)} %pad_maximum_fusion.1.refs_0_), channel_id=1, source_target_pairs={{0,224},{32,0},{64,32},{96,64},{128,96},{160,128},{192,160},{224,1... | collective-permute-start | bytes 1572872 | tf_op jit(solution)/shard_map/ppermute | solution.py:23
  45.6 9.4 %collective-permute-done.1.refs_1_ = bf16[2,2,256,256]{3,2,1,0:T(8,128)(2,1)S(1)} collective-permute-done((bf16[2,2,256,256]{3,2,1,0:T(8,128)(2,1)S(1)}, bf16[2,2,256,256]{3,2,1,0:T(8,128)(2,1)S(1)}, u32[]{:S(2)}, u32[]{:S(2)}) %collective-permute-start.1) | collective-permute-done | bytes 524320 | tf_op jit(solution)/shard_map/ppermute | solution.py:23
  55.0 5.6 %collective-permute-start.2 = (bf16[2,2,256,256]{3,2,1,0:T(8,128)(2,1)S(1)}, bf16[2,2,256,256]{3,2,1,0:T(8,128)(2,1)}, u32[]{:S(2)}, u32[]{:S(2)}) collective-permute-start(bf16[2,2,256,256]{3,2,1,0:T(8,128)(2,1)S(1)} %collective-permute-done.1.refs_1_), channel_id=1, source_target_pairs={{0,32},{32,64},{64,96},{96,128},{128,160},{160,192},{192,224},{224... | collective-permute-start | bytes 1572872 | tf_op jit(solution)/shard_map/ppermute | solution.py:23
  60.6 0.0 collective-permute-done.5.refs_2_
  60.6 1.9 %collective-permute-start.6 = (bf16[2,2,256,256]{3,2,1,0:T(8,128)(2,1)S(1)}, bf16[2,2,256,256]{3,2,1,0:T(8,128)(2,1)}, u32[]{:S(2)}, u32[]{:S(2)}) collective-permute-start(bf16[2,2,256,256]{3,2,1,0:T(8,128)(2,1)S(1)} %collective-permute-done.5.refs_2_), channel_id=1, source_target_pairs={{0,224},{32,0},{64,32},{96,64},{128,96},{160,128},{192,160},{224,1... | collective-permute-start | bytes 1572872 | tf_op jit(solution)/shard_map/ppermute | solution.py:23
  62.5 0.0 collective-permute-done.9.refs_8_
  62.6 1.9 %collective-permute-start.11 = (bf16[256,1024]{1,0:T(8,128)(2,1)S(1)}, bf16[256,1024]{1,0:T(8,128)(2,1)}, u32[]{:S(2)}, u32[]{:S(2)}) collective-permute-start(bf16[256,1024]{1,0:T(8,128)(2,1)S(1)} %slice.18), channel_id=1, source_target_pairs={{0,8},{8,16},{16,24},{24,0},{1,9},{9,17},{17,25},{25,1},{2,10},{10... | collective-permute-start | bytes 1572872 | tf_op jit(solution)/shard_map/ppermute | solution.py:23
  64.5 0.0 collective-permute-done.10.refs_9_
  64.6 1.1 slice.19
  65.6 5.1 %collective-permute-start.12 = (bf16[256,1024]{1,0:T(8,128)(2,1)S(1)}, bf16[256,1024]{1,0:T(8,128)(2,1)}, u32[]{:S(2)}, u32[]{:S(2)}) collective-permute-start(bf16[256,1024]{1,0:T(8,128)(2,1)S(1)} %slice.19), channel_id=1, source_target_pairs={{0,24},{8,0},{16,8},{24,16},{1,25},{9,1},{17,9},{25,17},{2,26},{10... | collective-permute-start | bytes 1572872 | tf_op jit(solution)/shard_map/ppermute | solution.py:23
  70.8 0.3 collective-permute-done.2.refs_3_
  71.1 5.7 %collective-permute-start.3 = (bf16[2,2,256,256]{3,2,1,0:T(8,128)(2,1)}, bf16[2,2,256,256]{3,2,1,0:T(8,128)(2,1)S(1)}, u32[]{:S(2)}, u32[]{:S(2)}) collective-permute-start(bf16[2,2,256,256]{3,2,1,0:T(8,128)(2,1)} %collective-permute-done.2.refs_3_), channel_id=1, source_target_pairs={{0,32},{32,64},{64,96},{96,128},{128,160},{160,192},{192,224},{224... | collective-permute-start | bytes 1572872 | tf_op jit(solution)/shard_map/ppermute | solution.py:23
  76.8 0.0 collective-permute-done.6.refs_4_
  76.8 1.9 %collective-permute-start.7 = (bf16[2,2,256,256]{3,2,1,0:T(8,128)(2,1)}, bf16[2,2,256,256]{3,2,1,0:T(8,128)(2,1)}, u32[]{:S(2)}, u32[]{:S(2)}) collective-permute-start(bf16[2,2,256,256]{3,2,1,0:T(8,128)(2,1)} %collective-permute-done.6.refs_4_), channel_id=1, source_target_pairs={{0,224},{32,0},{64,32},{96,64},{128,96},{160,128},{192,160},{224,1... | collective-permute-start | bytes 1572872 | tf_op jit(solution)/shard_map/ppermute | solution.py:23
  78.7 1.9 %collective-permute-start.13 = (bf16[512,1024]{1,0:T(8,128)(2,1)S(1)}, bf16[512,1024]{1,0:T(8,128)(2,1)}, u32[]{:S(2)}, u32[]{:S(2)}) collective-permute-start(bf16[512,1024]{1,0:T(8,128)(2,1)S(1)} %pad_maximum_fusion.refs_7_), channel_id=1, source_target_pairs={{0,4},{4,0},{1,5},{5,1},{2,6},{6,2},{3,7},{7,3},{8,12},{12,8},{9,1... | collective-permute-start | bytes 3145736 | tf_op jit(solution)/shard_map/ppermute | solution.py:23
  80.7 0.0 collective-permute-done.11.refs_10_
  80.7 2.4 %collective-permute-start.14 = (bf16[512,1024]{1,0:T(8,128)(2,1)S(1)}, bf16[512,1024]{1,0:T(8,128)(2,1)}, u32[]{:S(2)}, u32[]{:S(2)}) collective-permute-start(bf16[512,1024]{1,0:T(8,128)(2,1)S(1)} %collective-permute-done.9.refs_8_), channel_id=1, source_target_pairs={{0,4},{4,0},{1,5},{5,1},{2,6},{6,2},{3,7},{7,3},{8,12},{12,8},{9,1... | collective-permute-start | bytes 3145736 | tf_op jit(solution)/shard_map/ppermute | solution.py:23
  83.1 0.0 collective-permute-done.12.refs_11_
  83.1 1.9 %collective-permute-start.15 = (bf16[512,1024]{1,0:T(8,128)(2,1)}, bf16[512,1024]{1,0:T(8,128)(2,1)}, u32[]{:S(2)}, u32[]{:S(2)}) collective-permute-start(bf16[512,1024]{1,0:T(8,128)(2,1)} %collective-permute-done.10.refs_9_), channel_id=1, source_target_pairs={{0,4},{4,0},{1,5},{5,1},{2,6},{6,2},{3,7},{7,3},{8,12},{12,8},{9,1... | collective-permute-start | bytes 3145736 | tf_op jit(solution)/shard_map/ppermute | solution.py:23
  85.1 1.6 %collective-permute-done.3.refs_5_ = bf16[2,2,256,256]{3,2,1,0:T(8,128)(2,1)S(1)} collective-permute-done((bf16[2,2,256,256]{3,2,1,0:T(8,128)(2,1)}, bf16[2,2,256,256]{3,2,1,0:T(8,128)(2,1)S(1)}, u32[]{:S(2)}, u32[]{:S(2)}) %collective-permute-start.3) | collective-permute-done | bytes 524320 | tf_op jit(solution)/shard_map/ppermute | solution.py:23
  86.7 1.9 %collective-permute-start.16 = (bf16[256,1024]{1,0:T(8,128)(2,1)}, bf16[256,1024]{1,0:T(8,128)(2,1)}, u32[]{:S(2)}, u32[]{:S(2)}) collective-permute-start(bf16[256,1024]{1,0:T(8,128)(2,1)} %collective-permute-done.11.refs_10_), channel_id=1, source_target_pairs={{0,4},{4,0},{1,5},{5,1},{2,6},{6,2},{3,7},{7,3},{8,12},{12,8},{9,1... | collective-permute-start | bytes 1572872 | tf_op jit(solution)/shard_map/ppermute | solution.py:23
  88.6 3.4 %collective-permute-done.7.refs_6_ = bf16[2,2,256,256]{3,2,1,0:T(8,128)(2,1)} collective-permute-done((bf16[2,2,256,256]{3,2,1,0:T(8,128)(2,1)}, bf16[2,2,256,256]{3,2,1,0:T(8,128)(2,1)}, u32[]{:S(2)}, u32[]{:S(2)}) %collective-permute-start.7) | collective-permute-done | bytes 524320 | tf_op jit(solution)/shard_map/ppermute | solution.py:23
  92.0 1.9 %collective-permute-start.17 = (bf16[256,1024]{1,0:T(8,128)(2,1)}, bf16[256,1024]{1,0:T(8,128)(2,1)}, u32[]{:S(2)}, u32[]{:S(2)}) collective-permute-start(bf16[256,1024]{1,0:T(8,128)(2,1)} %collective-permute-done.12.refs_11_), channel_id=1, source_target_pairs={{0,4},{4,0},{1,5},{5,1},{2,6},{6,2},{3,7},{7,3},{8,12},{12,8},{9,1... | collective-permute-start | bytes 1572872 | tf_op jit(solution)/shard_map/ppermute | solution.py:23
  93.9 0.6 pad_add_fusion.where
  94.5 1.0 slice_bitcast_fusion
  95.5 0.0 collective-permute-done.13.refs_12_
  95.5 2.6 %collective-permute-start.4 = (bf16[2,256,256]{2,1,0:T(8,128)(2,1)S(1)}, bf16[2,256,256]{2,1,0:T(8,128)(2,1)S(1)}, u32[]{:S(2)}, u32[]{:S(2)}) collective-permute-start(bf16[2,256,256]{2,1,0:T(8,128)(2,1)S(1)} %slice_bitcast_fusion.1), channel_id=1, source_target_pairs={{0,32},{32,64},{64,96},{96,128},{128,160},{160,192},{192,224},{224... | collective-permute-start | bytes 786440 | tf_op jit(solution)/shard_map/ppermute | solution.py:23
  98.1 0.0 collective-permute-done.14.refs_13_
  98.1 3.3 %collective-permute-start.8 = (bf16[2,256,256]{2,1,0:T(8,128)(2,1)S(1)}, bf16[2,256,256]{2,1,0:T(8,128)(2,1)S(1)}, u32[]{:S(2)}, u32[]{:S(2)}) collective-permute-start(bf16[2,256,256]{2,1,0:T(8,128)(2,1)S(1)} %slice_bitcast_fusion), channel_id=1, source_target_pairs={{0,224},{32,0},{64,32},{96,64},{128,96},{160,128},{192,160},{224,1... | collective-permute-start | bytes 786440 | tf_op jit(solution)/shard_map/ppermute | solution.py:23
  101.4 0.0 collective-permute-done.15.refs_14_
  101.4 0.0 collective-permute-done.16.refs_15_
  101.4 0.0 collective-permute-done.17.refs_16_
  101.4 0.0 copy-done.2
  101.4 0.0 copy-done.5
  101.5 0.0 copy-done.8
  101.5 11.5 %project_most.1 = (f32[512,1024]{1,0:T(8,128)}, bf16[2,256,1024]{2,1,0:T(8,128)(2,1)}) custom-call(s32[4]{0:T(128)} %pad_add_fusion.where, bf16[2,2,256,256]{3,2,1,0:T(8,128)(2,1)} %copy-done.2, bf16[2,2,256,256]{3,2,1,0:T(8,128)(2,1)} %copy-done.10, bf16[2,2,256,256]{3,2,1,0:T(8,128)(2,1)} %copy-done.11, ...), custom_call_target="tpu_custom_call" | custom-call | flops 4294967296 | bytes 14680064 | tf_op jit(solution)/shard_map/project_most/pallas_call | solution.py:93
  113.0 0.0 collective-permute-done.4.near
  113.0 0.0 collective-permute-done.8.far
  113.0 0.7 copy-done.3
  113.7 0.1 copy-done.4
  113.8 3.7 %project_rest.1 = bf16[4,256,512]{2,1,0:T(8,128)(2,1)} custom-call(bf16[2,256,256]{2,1,0:T(8,128)(2,1)} %copy-done.3, bf16[2,256,256]{2,1,0:T(8,128)(2,1)} %copy-done.4, f32[512,1024]{1,0:T(8,128)} %get-tuple-element.11.partial, bf16[2,256,1024]{2,1,0:T(8,128)(2,1)} %get-tuple-element.12.w_left), custom_call_target="tpu_custom_call" | custom-call | flops 536870912 | bytes 5242880 | tf_op jit(solution)/shard_map/project_rest/pallas_call | solution.py:126
  117.5 19.0 %all_to_all.15.mine = bf16[4,256,512]{2,1,0:T(8,128)(2,1)S(1)} all-to-all(bf16[4,256,512]{2,1,0:T(8,128)(2,1)} %project_rest.1), channel_id=1, replica_groups=mesh['zh'=2,'y'=8,'x'=4,'c'=2,'mp'=4] {'x'}, dimensions={0} | all-to-all | bytes 2097152 | tf_op jit(solution)/shard_map/all_to_all | solution.py:198
  136.5 1.9 %collective-permute-start.18 = (bf16[4,256,512]{2,1,0:T(8,128)(2,1)S(1)}, bf16[4,256,512]{2,1,0:T(8,128)(2,1)S(1)}, u32[]{:S(2)}, u32[]{:S(2)}) collective-permute-start(bf16[4,256,512]{2,1,0:T(8,128)(2,1)S(1)} %all_to_all.15.mine), channel_id=1, source_target_pairs={{0,4},{4,0},{1,5},{5,1},{2,6},{6,2},{3,7},{7,3},{8,12},{12,8},{9,1... | collective-permute-start | bytes 3145736 | tf_op jit(solution)/shard_map/ppermute | solution.py:23
  138.4 2.6 %collective-permute-done.18.theirs = bf16[4,256,512]{2,1,0:T(8,128)(2,1)S(1)} collective-permute-done((bf16[4,256,512]{2,1,0:T(8,128)(2,1)S(1)}, bf16[4,256,512]{2,1,0:T(8,128)(2,1)S(1)}, u32[]{:S(2)}, u32[]{:S(2)}) %collective-permute-start.18) | collective-permute-done | bytes 1048608 | tf_op jit(solution)/shard_map/ppermute | solution.py:23
  141.0 0.0 copy-done.1
  141.0 1.0 copy-done.9
  142.0 5.4 %attend.1 = bf16[4,128,256]{2,1,0:T(8,128)(2,1)} custom-call(s32[4]{0:T(128)} %pad_add_fusion.where, s32[2]{0:T(128)} %lengths.1, bf16[4,128,256]{2,1,0:T(8,128)(2,1)} %copy-done.6, bf16[4,256,512]{2,1,0:T(8,128)(2,1)} %copy-done.1, bf16[4,256,512]{2,1,0:T(8,128)(2,1)} %copy-done.9), custom_call_target="tpu_custom_call" | custom-call | flops 1073741824 | bytes 4194304 | tf_op jit(solution)/shard_map/attend/pallas_call | solution.py:167
  147.4 10.6 %all_to_all.16 = bf16[4,128,256]{2,1,0:T(8,128)(2,1)S(1)} all-to-all(bf16[4,128,256]{2,1,0:T(8,128)(2,1)} %attend.1), channel_id=1, replica_groups=mesh['zh'=2,'y'=8,'x'=4,'c'=2,'mp'=4] {'x'}, dimensions={0} | all-to-all | bytes 524288 | tf_op jit(solution)/shard_map/all_to_all | solution.py:201
  158.0 0.3 copy.7
  158.3 0.9 broadcast_in_dim_reshape.3
  (16 shorter events, 0.1 us)
Async XLA Ops:
  0.0 19.8 %copy-start.7 = (bf16[2,256,256]{2,1,0:T(8,128)(2,1)S(1)}, bf16[2,256,256]{2,1,0:T(8,128)(2,1)}, u32[]{:S(2)}) copy-start(bf16[2,256,256]{2,1,0:T(8,128)(2,1)} %param.6) | copy-start | bytes 786436
  1.8 11.0 %all-to-all-start = ((bf16[4,128,256]{2,1,0:T(8,128)(2,1)}), bf16[4,128,256]{2,1,0:T(8,128)(2,1)S(1)}, u32[]{:S(2)}, u32[]{:S(2)}) async-start(bf16[4,128,256]{2,1,0:T(8,128)(2,1)} %bitcast.7), calls=%async_computation | async-start | bytes 524288 | tf_op jit(solution)/shard_map/all_to_all | solution.py:188
  7.4 88.1 %copy-start = (bf16[512,1024]{1,0:T(8,128)(2,1)}, bf16[512,1024]{1,0:T(8,128)(2,1)S(1)}, u32[]{:S(2)}) copy-start(bf16[512,1024]{1,0:T(8,128)(2,1)S(1)} %pad_maximum_fusion.refs_7_) | copy-start | bytes 3145732
  12.8 82.7 %copy-start.6 = (bf16[4,128,256]{2,1,0:T(8,128)(2,1)}, bf16[4,128,256]{2,1,0:T(8,128)(2,1)S(1)}, u32[]{:S(2)}) copy-start(bf16[4,128,256]{2,1,0:T(8,128)(2,1)S(1)} %all-to-all-done.query) | copy-start | bytes 786436
  12.8 49.8 %collective-permute-start.9 = (bf16[512,1024]{1,0:T(8,128)(2,1)S(1)}, bf16[512,1024]{1,0:T(8,128)(2,1)S(1)}, u32[]{:S(2)}, u32[]{:S(2)}) collective-permute-start(bf16[512,1024]{1,0:T(8,128)(2,1)S(1)} %pad_maximum_fusion.refs_7_), channel_id=1, source_target_pairs={{0,8},{8,16},{16,24},{24,0},{1,9},{9,17},{17,25},{25,1},{2,10},{10... | collective-permute-start | bytes 3145736 | tf_op jit(solution)/shard_map/ppermute | solution.py:23
  15.2 49.3 %collective-permute-start.10 = (bf16[512,1024]{1,0:T(8,128)(2,1)S(1)}, bf16[512,1024]{1,0:T(8,128)(2,1)}, u32[]{:S(2)}, u32[]{:S(2)}) collective-permute-start(bf16[512,1024]{1,0:T(8,128)(2,1)S(1)} %pad_maximum_fusion.refs_7_), channel_id=1, source_target_pairs={{0,24},{8,0},{16,8},{24,16},{1,25},{9,1},{17,9},{25,17},{2,26},{10... | collective-permute-start | bytes 3145736 | tf_op jit(solution)/shard_map/ppermute | solution.py:23
  19.8 19.1 %collective-permute-start = (bf16[2,256,256]{2,1,0:T(8,128)(2,1)S(1)}, bf16[2,256,256]{2,1,0:T(8,128)(2,1)S(1)}, u32[]{:S(2)}, u32[]{:S(2)}) collective-permute-start(bf16[2,256,256]{2,1,0:T(8,128)(2,1)S(1)} %copy-done.7), channel_id=1, source_target_pairs={{0,256},{256,0},{1,257},{257,1},{2,258},{258,2},{3,259},{259,3},{4... | collective-permute-start | bytes 786440 | tf_op jit(solution)/shard_map/ppermute | solution.py:23
  38.9 62.5 %copy-start.2 = (bf16[2,2,256,256]{3,2,1,0:T(8,128)(2,1)}, bf16[2,2,256,256]{3,2,1,0:T(8,128)(2,1)S(1)}, u32[]{:S(2)}) copy-start(bf16[2,2,256,256]{3,2,1,0:T(8,128)(2,1)S(1)} %pad_maximum_fusion.1.refs_0_) | copy-start | bytes 1572868
  39.0 16.0 %collective-permute-start.1 = (bf16[2,2,256,256]{3,2,1,0:T(8,128)(2,1)S(1)}, bf16[2,2,256,256]{3,2,1,0:T(8,128)(2,1)S(1)}, u32[]{:S(2)}, u32[]{:S(2)}) collective-permute-start(bf16[2,2,256,256]{3,2,1,0:T(8,128)(2,1)S(1)} %pad_maximum_fusion.1.refs_0_), channel_id=1, source_target_pairs={{0,32},{32,64},{64,96},{96,128},{128,160},{160,192},{192,224},{224... | collective-permute-start | bytes 1572872 | tf_op jit(solution)/shard_map/ppermute | solution.py:23
  43.7 16.9 %collective-permute-start.5 = (bf16[2,2,256,256]{3,2,1,0:T(8,128)(2,1)S(1)}, bf16[2,2,256,256]{3,2,1,0:T(8,128)(2,1)S(1)}, u32[]{:S(2)}, u32[]{:S(2)}) collective-permute-start(bf16[2,2,256,256]{3,2,1,0:T(8,128)(2,1)S(1)} %pad_maximum_fusion.1.refs_0_), channel_id=1, source_target_pairs={{0,224},{32,0},{64,32},{96,64},{128,96},{160,128},{192,160},{224,1... | collective-permute-start | bytes 1572872 | tf_op jit(solution)/shard_map/ppermute | solution.py:23
  55.0 28.1 %copy-start.10 = (bf16[2,2,256,256]{3,2,1,0:T(8,128)(2,1)}, bf16[2,2,256,256]{3,2,1,0:T(8,128)(2,1)S(1)}, u32[]{:S(2)}) copy-start(bf16[2,2,256,256]{3,2,1,0:T(8,128)(2,1)S(1)} %collective-permute-done.1.refs_1_) | copy-start | bytes 1572868
  55.0 16.1 %collective-permute-start.2 = (bf16[2,2,256,256]{3,2,1,0:T(8,128)(2,1)S(1)}, bf16[2,2,256,256]{3,2,1,0:T(8,128)(2,1)}, u32[]{:S(2)}, u32[]{:S(2)}) collective-permute-start(bf16[2,2,256,256]{3,2,1,0:T(8,128)(2,1)S(1)} %collective-permute-done.1.refs_1_), channel_id=1, source_target_pairs={{0,32},{32,64},{64,96},{96,128},{128,160},{160,192},{192,224},{224... | collective-permute-start | bytes 1572872 | tf_op jit(solution)/shard_map/ppermute | solution.py:23
  60.6 24.4 %copy-start.11 = (bf16[2,2,256,256]{3,2,1,0:T(8,128)(2,1)}, bf16[2,2,256,256]{3,2,1,0:T(8,128)(2,1)S(1)}, u32[]{:S(2)}) copy-start(bf16[2,2,256,256]{3,2,1,0:T(8,128)(2,1)S(1)} %collective-permute-done.5.refs_2_) | copy-start | bytes 1572868
  60.6 16.2 %collective-permute-start.6 = (bf16[2,2,256,256]{3,2,1,0:T(8,128)(2,1)S(1)}, bf16[2,2,256,256]{3,2,1,0:T(8,128)(2,1)}, u32[]{:S(2)}, u32[]{:S(2)}) collective-permute-start(bf16[2,2,256,256]{3,2,1,0:T(8,128)(2,1)S(1)} %collective-permute-done.5.refs_2_), channel_id=1, source_target_pairs={{0,224},{32,0},{64,32},{96,64},{128,96},{160,128},{192,160},{224,1... | collective-permute-start | bytes 1572872 | tf_op jit(solution)/shard_map/ppermute | solution.py:23
  62.6 38.9 %copy-start.5 = (bf16[512,1024]{1,0:T(8,128)(2,1)}, bf16[512,1024]{1,0:T(8,128)(2,1)S(1)}, u32[]{:S(2)}) copy-start(bf16[512,1024]{1,0:T(8,128)(2,1)S(1)} %collective-permute-done.9.refs_8_) | copy-start | bytes 3145732
  62.6 18.1 %collective-permute-start.11 = (bf16[256,1024]{1,0:T(8,128)(2,1)S(1)}, bf16[256,1024]{1,0:T(8,128)(2,1)}, u32[]{:S(2)}, u32[]{:S(2)}) collective-permute-start(bf16[256,1024]{1,0:T(8,128)(2,1)S(1)} %slice.18), channel_id=1, source_target_pairs={{0,8},{8,16},{16,24},{24,0},{1,9},{9,17},{17,25},{25,1},{2,10},{10... | collective-permute-start | bytes 1572872 | tf_op jit(solution)/shard_map/ppermute | solution.py:23
  65.6 17.5 %collective-permute-start.12 = (bf16[256,1024]{1,0:T(8,128)(2,1)S(1)}, bf16[256,1024]{1,0:T(8,128)(2,1)}, u32[]{:S(2)}, u32[]{:S(2)}) collective-permute-start(bf16[256,1024]{1,0:T(8,128)(2,1)S(1)} %slice.19), channel_id=1, source_target_pairs={{0,24},{8,0},{16,8},{24,16},{1,25},{9,1},{17,9},{25,17},{2,26},{10... | collective-permute-start | bytes 1572872 | tf_op jit(solution)/shard_map/ppermute | solution.py:23
  71.1 15.6 %collective-permute-start.3 = (bf16[2,2,256,256]{3,2,1,0:T(8,128)(2,1)}, bf16[2,2,256,256]{3,2,1,0:T(8,128)(2,1)S(1)}, u32[]{:S(2)}, u32[]{:S(2)}) collective-permute-start(bf16[2,2,256,256]{3,2,1,0:T(8,128)(2,1)} %collective-permute-done.2.refs_3_), channel_id=1, source_target_pairs={{0,32},{32,64},{64,96},{96,128},{128,160},{160,192},{192,224},{224... | collective-permute-start | bytes 1572872 | tf_op jit(solution)/shard_map/ppermute | solution.py:23
  76.8 15.2 %collective-permute-start.7 = (bf16[2,2,256,256]{3,2,1,0:T(8,128)(2,1)}, bf16[2,2,256,256]{3,2,1,0:T(8,128)(2,1)}, u32[]{:S(2)}, u32[]{:S(2)}) collective-permute-start(bf16[2,2,256,256]{3,2,1,0:T(8,128)(2,1)} %collective-permute-done.6.refs_4_), channel_id=1, source_target_pairs={{0,224},{32,0},{64,32},{96,64},{128,96},{160,128},{192,160},{224,1... | collective-permute-start | bytes 1572872 | tf_op jit(solution)/shard_map/ppermute | solution.py:23
  78.7 16.8 %collective-permute-start.13 = (bf16[512,1024]{1,0:T(8,128)(2,1)S(1)}, bf16[512,1024]{1,0:T(8,128)(2,1)}, u32[]{:S(2)}, u32[]{:S(2)}) collective-permute-start(bf16[512,1024]{1,0:T(8,128)(2,1)S(1)} %pad_maximum_fusion.refs_7_), channel_id=1, source_target_pairs={{0,4},{4,0},{1,5},{5,1},{2,6},{6,2},{3,7},{7,3},{8,12},{12,8},{9,1... | collective-permute-start | bytes 3145736 | tf_op jit(solution)/shard_map/ppermute | solution.py:23
  80.7 17.4 %collective-permute-start.14 = (bf16[512,1024]{1,0:T(8,128)(2,1)S(1)}, bf16[512,1024]{1,0:T(8,128)(2,1)}, u32[]{:S(2)}, u32[]{:S(2)}) collective-permute-start(bf16[512,1024]{1,0:T(8,128)(2,1)S(1)} %collective-permute-done.9.refs_8_), channel_id=1, source_target_pairs={{0,4},{4,0},{1,5},{5,1},{2,6},{6,2},{3,7},{7,3},{8,12},{12,8},{9,1... | collective-permute-start | bytes 3145736 | tf_op jit(solution)/shard_map/ppermute | solution.py:23
  83.1 18.3 %collective-permute-start.15 = (bf16[512,1024]{1,0:T(8,128)(2,1)}, bf16[512,1024]{1,0:T(8,128)(2,1)}, u32[]{:S(2)}, u32[]{:S(2)}) collective-permute-start(bf16[512,1024]{1,0:T(8,128)(2,1)} %collective-permute-done.10.refs_9_), channel_id=1, source_target_pairs={{0,4},{4,0},{1,5},{5,1},{2,6},{6,2},{3,7},{7,3},{8,12},{12,8},{9,1... | collective-permute-start | bytes 3145736 | tf_op jit(solution)/shard_map/ppermute | solution.py:23
  86.7 14.8 %copy-start.8 = (bf16[2,2,256,256]{3,2,1,0:T(8,128)(2,1)}, bf16[2,2,256,256]{3,2,1,0:T(8,128)(2,1)S(1)}, u32[]{:S(2)}) copy-start(bf16[2,2,256,256]{3,2,1,0:T(8,128)(2,1)S(1)} %collective-permute-done.3.refs_5_) | copy-start | bytes 1572868
  86.7 14.7 %collective-permute-start.16 = (bf16[256,1024]{1,0:T(8,128)(2,1)}, bf16[256,1024]{1,0:T(8,128)(2,1)}, u32[]{:S(2)}, u32[]{:S(2)}) collective-permute-start(bf16[256,1024]{1,0:T(8,128)(2,1)} %collective-permute-done.11.refs_10_), channel_id=1, source_target_pairs={{0,4},{4,0},{1,5},{5,1},{2,6},{6,2},{3,7},{7,3},{8,12},{12,8},{9,1... | collective-permute-start | bytes 1572872 | tf_op jit(solution)/shard_map/ppermute | solution.py:23
  92.0 9.4 %collective-permute-start.17 = (bf16[256,1024]{1,0:T(8,128)(2,1)}, bf16[256,1024]{1,0:T(8,128)(2,1)}, u32[]{:S(2)}, u32[]{:S(2)}) collective-permute-start(bf16[256,1024]{1,0:T(8,128)(2,1)} %collective-permute-done.12.refs_11_), channel_id=1, source_target_pairs={{0,4},{4,0},{1,5},{5,1},{2,6},{6,2},{3,7},{7,3},{8,12},{12,8},{9,1... | collective-permute-start | bytes 1572872 | tf_op jit(solution)/shard_map/ppermute | solution.py:23
  95.5 17.5 %collective-permute-start.4 = (bf16[2,256,256]{2,1,0:T(8,128)(2,1)S(1)}, bf16[2,256,256]{2,1,0:T(8,128)(2,1)S(1)}, u32[]{:S(2)}, u32[]{:S(2)}) collective-permute-start(bf16[2,256,256]{2,1,0:T(8,128)(2,1)S(1)} %slice_bitcast_fusion.1), channel_id=1, source_target_pairs={{0,32},{32,64},{64,96},{96,128},{128,160},{160,192},{192,224},{224... | collective-permute-start | bytes 786440 | tf_op jit(solution)/shard_map/ppermute | solution.py:23
  98.1 14.9 %collective-permute-start.8 = (bf16[2,256,256]{2,1,0:T(8,128)(2,1)S(1)}, bf16[2,256,256]{2,1,0:T(8,128)(2,1)S(1)}, u32[]{:S(2)}, u32[]{:S(2)}) collective-permute-start(bf16[2,256,256]{2,1,0:T(8,128)(2,1)S(1)} %slice_bitcast_fusion), channel_id=1, source_target_pairs={{0,224},{32,0},{64,32},{96,64},{128,96},{160,128},{192,160},{224,1... | collective-permute-start | bytes 786440 | tf_op jit(solution)/shard_map/ppermute | solution.py:23
  113.0 0.7 copy-start.3
  113.0 0.8 copy-start.4
  136.5 4.5 %copy-start.1 = (bf16[4,256,512]{2,1,0:T(8,128)(2,1)}, bf16[4,256,512]{2,1,0:T(8,128)(2,1)S(1)}, u32[]{:S(2)}) copy-start(bf16[4,256,512]{2,1,0:T(8,128)(2,1)S(1)} %all_to_all.15.mine) | copy-start | bytes 3145732
  136.5 4.5 %collective-permute-start.18 = (bf16[4,256,512]{2,1,0:T(8,128)(2,1)S(1)}, bf16[4,256,512]{2,1,0:T(8,128)(2,1)S(1)}, u32[]{:S(2)}, u32[]{:S(2)}) collective-permute-start(bf16[4,256,512]{2,1,0:T(8,128)(2,1)S(1)} %all_to_all.15.mine), channel_id=1, source_target_pairs={{0,4},{4,0},{1,5},{5,1},{2,6},{6,2},{3,7},{7,3},{8,12},{12,8},{9,1... | collective-permute-start | bytes 3145736 | tf_op jit(solution)/shard_map/ppermute | solution.py:23
  141.0 1.0 copy-start.9

commit v2 on v1

v2 whole, which is shorter than its diff:
```python
import math

import jax
import jax.numpy as jnp
from jax import lax
from jax.experimental import pallas as pl
from jax.experimental.pallas import tpu as pltpu
from jax.sharding import Mesh
from jax.sharding import PartitionSpec as P

HEAD_DIM = 256
SEGMENT = ("zh", "y")
X = ("xh", "xl")
CTX = ("xh", "xl", "c")
ROWS = 256
FEATS = 256
VMEM = pl.BlockSpec(memory_space=pltpu.VMEM)
SMEM = pl.BlockSpec(memory_space=pltpu.SMEM)
ANY = pl.BlockSpec(memory_space=pl.ANY)


def shift(array, axis, by):
    n = lax.axis_size(axis)
    by %= n
    return lax.ppermute(array, axis, [(i, (i + by) % n) for i in range(n)])


def ring_of_eight(block):
    up, down = block, block
    pieces = [block]
    for _ in range(3):
        up, down = shift(up, "y", 1), shift(down, "y", -1)
        pieces += [up, down]
    return pieces, (shift(up[0], "y", 1), shift(down[1], "y", -1))


X_OFFSETS = (0, 3, 1, 2)


def slot_of(relative):
    odd_even = jnp.where(relative < 4, 2 * relative, 2 * (8 - relative) - 1)
    return jnp.where(relative == 4, 7, jnp.where(relative == 0, 0, odd_even))


def project_early_kernel(where, *refs):
    enc, own, other = refs[:5], refs[5:9], refs[9:13]
    out, w_left, enc_all, w_all, sem_e, sem_w = refs[13:]
    y, x, core = where[0], where[1], where[2]
    copies = []
    for side, blocks in enumerate((own, other)):
        of_core = core if side == 0 else 1 - core
        for ref, offset in zip(blocks, X_OFFSETS):
            block = lax.rem(x + offset, 4)
            for part in range(2):
                segment = (block * 2 + of_core) * 2 + part
                relative = lax.rem(lax.rem(segment, 8) - y + 8, 8)
                row = (slot_of(relative) * 2 + block // 2) * FEATS
                copies.append(
                    pltpu.make_async_copy(
                        ref.at[pl.ds(part * FEATS, FEATS)],
                        w_all.at[pl.ds(pl.multiple_of(row, FEATS), FEATS)],
                        sem_w.at[len(copies)],
                    )
                )
    for piece, ref in enumerate(enc):
        for high in range(2):
            n = 2 * piece + high
            copies.append(
                pltpu.make_async_copy(
                    ref.at[high], enc_all.at[:, :, pl.ds(n * FEATS, FEATS)], sem_e.at[n]
                )
            )
    for copy in copies:
        copy.start()
    for copy in copies:
        copy.wait()
    depth = 2 * len(enc) * FEATS
    lhs = enc_all[...].reshape(2 * ROWS, depth)
    for n in range(4):
        cols = slice(n * HEAD_DIM, (n + 1) * HEAD_DIM)
        out[:, cols] = jnp.dot(lhs, w_all[:depth, cols], preferred_element_type=jnp.float32)
    for n in range(6):
        w_left[n] = w_all[depth + n * FEATS : depth + (n + 1) * FEATS, :]


def project_early(where, enc, own, other):
    return pl.pallas_call(
        project_early_kernel,
        out_shape=(
            jax.ShapeDtypeStruct((2 * ROWS, 4 * HEAD_DIM), jnp.float32),
            jax.ShapeDtypeStruct((6, FEATS, 4 * HEAD_DIM), jnp.bfloat16),
        ),
        in_specs=[SMEM] + [ANY] * 13,
        out_specs=(VMEM, VMEM),
        scratch_shapes=[
            pltpu.VMEM((2, ROWS, 10 * FEATS), jnp.bfloat16),
            pltpu.VMEM((4096, 4 * HEAD_DIM), jnp.bfloat16),
            pltpu.SemaphoreType.DMA((10,)),
            pltpu.SemaphoreType.DMA((16,)),
        ],
        compiler_params=pltpu.CompilerParams(vmem_limit_bytes=32 * 2**20),
        cost_estimate=pl.CostEstimate(
            flops=2 * 512 * 2560 * 1024, bytes_accessed=14 * 2**20, transcendentals=0
        ),
        name="project_early",
    )(where, *enc, *own, *other)


def project_next_kernel(up, down, partial, w_left, out):
    for n in range(4):
        cols = slice(n * HEAD_DIM, (n + 1) * HEAD_DIM)
        acc = partial[:, cols]
        for k, (ref, high) in enumerate(((up, 0), (up, 1), (down, 0), (down, 1))):
            rows = ref[high].reshape(2 * ROWS, FEATS)
            acc += jnp.dot(rows, w_left[k, :, cols], preferred_element_type=jnp.float32)
        out[:, cols] = acc


def project_next(up, down, partial, w_left):
    return pl.pallas_call(
        project_next_kernel,
        out_shape=jax.ShapeDtypeStruct((2 * ROWS, 4 * HEAD_DIM), jnp.float32),
        in_specs=[VMEM] * 4,
        out_specs=VMEM,
        compiler_params=pltpu.CompilerParams(vmem_limit_bytes=32 * 2**20),
        cost_estimate=pl.CostEstimate(
            flops=2 * 512 * 1024 * 1024, bytes_accessed=8 * 2**20, transcendentals=0
        ),
        name="project_next",
    )(up, down, partial, w_left)


def project_rest_kernel(first, second, partial, w_left, out):
    first_rows = first[...].reshape(2 * ROWS, FEATS)
    second_rows = second[...].reshape(2 * ROWS, FEATS)
    for n in range(4):
        cols = slice(n * HEAD_DIM, (n + 1) * HEAD_DIM)
        acc = jnp.dot(first_rows, w_left[4, :, cols], preferred_element_type=jnp.float32)
        acc += jnp.dot(second_rows, w_left[5, :, cols], preferred_element_type=jnp.float32)
        out[:, cols] = (acc + partial[:, cols]).astype(jnp.bfloat16)


def project_rest(first, second, partial, w_left):
    return pl.pallas_call(
        project_rest_kernel,
        out_shape=jax.ShapeDtypeStruct((2 * ROWS, 4 * HEAD_DIM), jnp.bfloat16),
        in_specs=[VMEM] * 4,
        out_specs=VMEM,
        compiler_params=pltpu.CompilerParams(vmem_limit_bytes=32 * 2**20),
        cost_estimate=pl.CostEstimate(
            flops=2 * 512 * 512 * 1024, bytes_accessed=5 * 2**20, transcendentals=0
        ),
        name="project_rest",
    )(first, second, partial, w_left)


def attend_kernel(where, lengths, query, mine, theirs, out):
    x, core = where[1], where[2]
    length = lengths[lax.rem(x, 2)]
    scale = 1.0 / math.sqrt(HEAD_DIM)
    steps = []
    for of, ref in ((core, mine), (1 - core, theirs)):
        index = lax.broadcasted_iota(jnp.int32, (1, 2 * ROWS), 1)
        first = (x // 2 * 4 + of) * ROWS
        place = index + jnp.where(index < ROWS, first, first + ROWS)
        steps.append((ref, place < length))
    lane = lax.broadcasted_iota(jnp.int32, (128, 128), 1)
    for chunk in range(2):
        tables = [jnp.zeros((128, 128), jnp.float32)] * 2
        for head in range(2):
            key_cols = slice(head * HEAD_DIM, (head + 1) * HEAD_DIM)
            value_cols = slice((2 + head) * HEAD_DIM, (3 + head) * HEAD_DIM)
            q = query[2 * chunk : 2 * chunk + 2, :, key_cols].reshape(256, HEAD_DIM)
            scores = []
            for ref, valid in steps:
                s = lax.dot_general(
                    q, ref[:, key_cols], (((1,), (1,)), ((), ())), preferred_element_type=jnp.float32
                )
                scores.append(jnp.where(valid, s * scale, -1e30))
            top = jnp.max(jnp.maximum(scores[0], scores[1]), axis=1, keepdims=True)
            weights = [jnp.exp(s - top) for s in scores]
            total = jnp.sum(weights[0] + weights[1], axis=1, keepdims=True)
            summed = sum(
                jnp.dot(w.astype(jnp.bfloat16), ref[:, value_cols], preferred_element_type=jnp.float32)
                for w, (ref, _) in zip(weights, steps)
            )
            mixed = (summed / total).astype(jnp.bfloat16)
            log_total = top + jnp.log(total)
            high = log_total.astype(jnp.bfloat16).astype(jnp.float32)
            middle = (log_total - high).astype(jnp.bfloat16).astype(jnp.float32)
            low = log_total - high - middle
            for half in range(2):
                rows = slice(half * 128, (half + 1) * 128)
                out[2 * chunk + half, :128, key_cols] = mixed[rows]
                for at, part in enumerate((high, middle, low)):
                    tables[half] = jnp.where(lane == 3 * head + at, part[rows], tables[half])
        for half in range(2):
            out[2 * chunk + half, 128:, :128] = jnp.transpose(tables[half])[:16].astype(jnp.bfloat16)
            out[2 * chunk + half, 128:, 128:] = jnp.zeros((16, 2 * HEAD_DIM - 128), jnp.bfloat16)


def attend(where, lengths, query, mine, theirs):
    return pl.pallas_call(
        attend_kernel,
        out_shape=jax.ShapeDtypeStruct((4, 144, 2 * HEAD_DIM), jnp.bfloat16),
        in_specs=[SMEM, SMEM, VMEM, VMEM, VMEM],
        out_specs=VMEM,
        compiler_params=pltpu.CompilerParams(vmem_limit_bytes=32 * 2**20),
        cost_estimate=pl.CostEstimate(
            flops=4 * 1024 * 1024 * 256, bytes_accessed=4 * 2**20, transcendentals=1024 * 1024
        ),
        name="attend",
    )(where, lengths, query, mine, theirs)


def merge_kernel(parts, out):
    for doc in range(2):
        tables = [parts[doc + 2 * xh, 128:, :128].astype(jnp.float32) for xh in range(2)]
        for head in range(2):
            cols = slice(head * HEAD_DIM, (head + 1) * HEAD_DIM)
            logs = []
            for table in tables:
                row = sum(table[3 * head + at : 3 * head + at + 1] for at in range(3))
                logs.append(jnp.transpose(jnp.broadcast_to(row, (128, 128)))[:, :1])
            top = jnp.maximum(logs[0], logs[1])
            shares = [jnp.exp(log - top) for log in logs]
            mixed = sum(
                share * parts[doc + 2 * xh, :128, cols].astype(jnp.float32) for xh, share in enumerate(shares)
            )
            out[0, doc, :, cols] = (mixed / (shares[0] + shares[1])).astype(jnp.bfloat16)


def merge(parts):
    return pl.pallas_call(
        merge_kernel,
        out_shape=jax.ShapeDtypeStruct((1, 2, 128, 2 * HEAD_DIM), jnp.bfloat16),
        in_specs=[VMEM],
        out_specs=VMEM,
        name="merge",
    )(parts)


def on_device(queries, enc_states, key_weight, value_weight, enc_lengths):
    x = lax.axis_index("xh") * 2 + lax.axis_index("xl")
    where = jnp.stack([lax.axis_index("y"), x, lax.axis_index("c")])

    states = jnp.broadcast_to(enc_states[None], (2, *enc_states.shape)).reshape(4, ROWS, FEATS)
    states = lax.all_to_all(states, ("zh", "xl"), 0, 0).reshape(2, 2, ROWS, FEATS)

    weight = jnp.concatenate([key_weight[0], value_weight[0]], axis=1)
    late, states = lax.optimization_barrier((weight, states))
    own = [weight, shift(weight, X, 1), shift(weight, X, -1), shift(late, X, 2)]
    other = [shift(block, "c", 1) for block in own]
    enc, (first, second) = ring_of_eight(states)

    query = jnp.broadcast_to(queries, (2, *queries.shape[1:])).reshape(4, *queries.shape[2:])
    query, own[3] = lax.optimization_barrier((query, own[3]))
    query = lax.all_to_all(query, X, 0, 0)

    partial, w_left = project_early(where, enc[:5], own, other)
    partial = project_next(enc[5], enc[6], partial, w_left)
    mine = project_rest(first, second, partial, w_left)
    mine, query = lax.optimization_barrier((mine, query))
    theirs = shift(mine, "c", 1)
    parts = attend(where, enc_lengths, query, mine, theirs)
    return merge(lax.all_to_all(parts, X, 0, 0))


def solution(mesh):
    torus = Mesh(mesh.devices.reshape(2, 8, 2, 2, 2, 4), ("zh", "y", "xh", "xl", "c", "mp"))
    return jax.shard_map(
        on_device,
        mesh=torus,
        in_specs=(
            P(SEGMENT, None, CTX, "mp"),
            P(None, CTX, SEGMENT),
            P(SEGMENT, CTX, "mp"),
            P(SEGMENT, CTX, "mp"),
            P(),
        ),
        out_specs=P(SEGMENT, None, CTX, "mp"),
        check_vma=False,
    )
```

time: 160 us -> 152 us (0.950)
  the two profiles are of different devices: /device:TPU:152 before, /device:TPU:88 now
where the time goes in v2:
time: 152 us; the launch traced here: 151 us
  starting transfers between devices  67.3 us (44%)
  waiting for transfers between devices  42.3 us (28%)
  blocking collectives  19.9 us (13%)
  Pallas kernels  14.6 us (10%)
  local copies, waits for them, and re-layouts  6.51 us (4%)
    ppermute x16, starting transfers between devices, shift(): return lax.ppermute(array, axis, [(i, (i + by) % n) for i in range(n)])  47.5 us
    ppermute x16, waiting for transfers between devices, shift(): return lax.ppermute(array, axis, [(i, (i + by) % n) for i in range(n)])  25 us
    all_to_all x1, blocking collectives, on_device(): return merge(lax.all_to_all(parts, X, 0, 0))  19.9 us
    all_to_all x1, waiting for transfers between devices, on_device(): lax.all_to_all(states, ('zh', 'xl'), 0, 0).reshape(2, 2, ROWS, FEATS)  17.2 us
    all_to_all x1, starting transfers between devices, on_device(): lax.all_to_all(states, ('zh', 'xl'), 0, 0).reshape(2, 2, ROWS, FEATS)  10.3 us
    all_to_all x1, starting transfers between devices, on_device(): query = lax.all_to_all(query, X, 0, 0)  9.49 us
    pallas_call x1, Pallas kernels, project_early(): pl.pallas_call(project_early_kernel, out_shape=(jax.ShapeDtypeStruct((2 *...  7.31 us
    unnamed x16, local copies, waits for them, and re-layouts  3.67 us
  transfers between devices with their start and end apart: 18, of which 6 were waited for; matrix products, arithmetic and copies ran while one was open for 1% of the time, Pallas kernels for 6%

profile of v2, /device:TPU:88, one launch (start us, length us, event | category | flops | bytes accessed | tf_op | source)
XLA Modules:
  0.0 151.1 jit_solution(12922674993752249866)
XLA Ops:
  0.0 0.0 copy-start.6
  0.0 0.0 copy-start.5
  0.0 0.0 copy-start.7
  0.0 1.9 %broadcast_in_dim.6 = bf16[2,2,256,256]{3,2,1,0:T(8,128)(2,1)} broadcast(bf16[2,256,256]{2,1,0:T(8,128)(2,1)} %param.6), dimensions={1,2,3} | broadcast | bytes 786432 | tf_op jit(solution)/shard_map/broadcast_in_dim | solution.py:247
  1.9 10.3 %all-to-all-start = ((bf16[4,256,256]{2,1,0:T(8,128)(2,1)}), bf16[4,256,256]{2,1,0:T(8,128)(2,1)S(1)}, u32[]{:S(2)}, u32[]{:S(2)}) async-start(bf16[4,256,256]{2,1,0:T(8,128)(2,1)} %bitcast.5), calls=%async_computation | async-start | bytes 1048576 | tf_op jit(solution)/shard_map/all_to_all | solution.py:248
  12.2 0.0 copy-done.6
  12.2 0.0 copy-done.5
  12.2 0.1 pad_maximum_fusion.refs_5_
  12.4 17.2 %all-to-all-done = bf16[4,256,256]{2,1,0:T(8,128)(2,1)S(1)} async-done(((bf16[4,256,256]{2,1,0:T(8,128)(2,1)}), bf16[4,256,256]{2,1,0:T(8,128)(2,1)S(1)}, u32[]{:S(2)}, u32[]{:S(2)}) %all-to-all-start) | async-done | bytes 524320 | tf_op jit(solution)/shard_map/all_to_all | solution.py:248
  29.6 4.7 %collective-permute-start = (bf16[2,2,256,256]{3,2,1,0:T(8,128)(2,1)S(1)}, bf16[2,2,256,256]{3,2,1,0:T(8,128)(2,1)S(1)}, u32[]{:S(2)}, u32[]{:S(2)}) collective-permute-start(bf16[2,2,256,256]{3,2,1,0:T(8,128)(2,1)S(1)} %bitcast.13), channel_id=1, source_target_pairs={{0,32},{32,64},{64,96},{96,128},{128,160},{160,192},{192,224},{224... | collective-permute-start | bytes 1572872 | tf_op jit(solution)/shard_map/ppermute | solution.py:25
  34.3 3.5 %collective-permute-start.8 = (bf16[512,1024]{1,0:T(8,128)(2,1)S(1)}, bf16[512,1024]{1,0:T(8,128)(2,1)}, u32[]{:S(2)}, u32[]{:S(2)}) collective-permute-start(bf16[512,1024]{1,0:T(8,128)(2,1)S(1)} %pad_maximum_fusion.refs_5_), channel_id=1, source_target_pairs={{0,8},{8,16},{16,24},{24,0},{1,9},{9,17},{17,25},{25,1},{2,10},{10... | collective-permute-start | bytes 3145736 | tf_op jit(solution)/shard_map/ppermute | solution.py:25
  37.8 3.6 %collective-permute-start.9 = (bf16[512,1024]{1,0:T(8,128)(2,1)S(1)}, bf16[512,1024]{1,0:T(8,128)(2,1)}, u32[]{:S(2)}, u32[]{:S(2)}) collective-permute-start(bf16[512,1024]{1,0:T(8,128)(2,1)S(1)} %pad_maximum_fusion.refs_5_), channel_id=1, source_target_pairs={{0,24},{8,0},{16,8},{24,16},{1,25},{9,1},{17,9},{25,17},{2,26},{10... | collective-permute-start | bytes 3145736 | tf_op jit(solution)/shard_map/ppermute | solution.py:25
  41.4 1.9 %collective-permute-start.4 = (bf16[2,2,256,256]{3,2,1,0:T(8,128)(2,1)S(1)}, bf16[2,2,256,256]{3,2,1,0:T(8,128)(2,1)S(1)}, u32[]{:S(2)}, u32[]{:S(2)}) collective-permute-start(bf16[2,2,256,256]{3,2,1,0:T(8,128)(2,1)S(1)} %bitcast.14), channel_id=1, source_target_pairs={{0,224},{32,0},{64,32},{96,64},{128,96},{160,128},{192,160},{224,1... | collective-permute-start | bytes 1572872 | tf_op jit(solution)/shard_map/ppermute | solution.py:25
  43.3 3.4 %collective-permute-start.10 = (bf16[512,1024]{1,0:T(8,128)(2,1)S(1)}, bf16[512,1024]{1,0:T(8,128)(2,1)}, u32[]{:S(2)}, u32[]{:S(2)}) collective-permute-start(bf16[512,1024]{1,0:T(8,128)(2,1)S(1)} %pad_maximum_fusion.refs_5_), channel_id=1, source_target_pairs={{0,16},{8,24},{16,0},{24,8},{1,17},{9,25},{17,1},{25,9},{2,18},{10... | collective-permute-start | bytes 3145736 | tf_op jit(solution)/shard_map/ppermute | solution.py:25
  46.7 0.0 collective-permute-done.refs_1_
  46.8 5.1 %collective-permute-start.1 = (bf16[2,2,256,256]{3,2,1,0:T(8,128)(2,1)S(1)}, bf16[2,2,256,256]{3,2,1,0:T(8,128)(2,1)S(1)}, u32[]{:S(2)}, u32[]{:S(2)}) collective-permute-start(bf16[2,2,256,256]{3,2,1,0:T(8,128)(2,1)S(1)} %collective-permute-done.refs_1_), channel_id=1, source_target_pairs={{0,32},{32,64},{64,96},{96,128},{128,160},{160,192},{192,224},{224... | collective-permute-start | bytes 1572872 | tf_op jit(solution)/shard_map/ppermute | solution.py:25
  51.9 4.2 %collective-permute-done.4.refs_2_ = bf16[2,2,256,256]{3,2,1,0:T(8,128)(2,1)S(1)} collective-permute-done((bf16[2,2,256,256]{3,2,1,0:T(8,128)(2,1)S(1)}, bf16[2,2,256,256]{3,2,1,0:T(8,128)(2,1)S(1)}, u32[]{:S(2)}, u32[]{:S(2)}) %collective-permute-start.4) | collective-permute-done | bytes 524320 | tf_op jit(solution)/shard_map/ppermute | solution.py:25
  56.1 1.9 %collective-permute-start.5 = (bf16[2,2,256,256]{3,2,1,0:T(8,128)(2,1)S(1)}, bf16[2,2,256,256]{3,2,1,0:T(8,128)(2,1)}, u32[]{:S(2)}, u32[]{:S(2)}) collective-permute-start(bf16[2,2,256,256]{3,2,1,0:T(8,128)(2,1)S(1)} %collective-permute-done.4.refs_2_), channel_id=1, source_target_pairs={{0,224},{32,0},{64,32},{96,64},{128,96},{160,128},{192,160},{224,1... | collective-permute-start | bytes 1572872 | tf_op jit(solution)/shard_map/ppermute | solution.py:25
  58.0 0.0 copy-start
  58.0 0.8 copy-done
  58.8 1.6 %collective-permute-done.1.refs_3_ = bf16[2,2,256,256]{3,2,1,0:T(8,128)(2,1)S(1)} collective-permute-done((bf16[2,2,256,256]{3,2,1,0:T(8,128)(2,1)S(1)}, bf16[2,2,256,256]{3,2,1,0:T(8,128)(2,1)S(1)}, u32[]{:S(2)}, u32[]{:S(2)}) %collective-permute-start.1) | collective-permute-done | bytes 524320 | tf_op jit(solution)/shard_map/ppermute | solution.py:25
  60.5 5.6 %collective-permute-start.2 = (bf16[2,2,256,256]{3,2,1,0:T(8,128)(2,1)S(1)}, bf16[2,2,256,256]{3,2,1,0:T(8,128)(2,1)S(1)}, u32[]{:S(2)}, u32[]{:S(2)}) collective-permute-start(bf16[2,2,256,256]{3,2,1,0:T(8,128)(2,1)S(1)} %collective-permute-done.1.refs_3_), channel_id=1, source_target_pairs={{0,32},{32,64},{64,96},{96,128},{128,160},{160,192},{192,224},{224... | collective-permute-start | bytes 1572872 | tf_op jit(solution)/shard_map/ppermute | solution.py:25
  66.0 0.0 copy-start.2
  66.1 0.8 copy-done.2
  66.8 0.0 collective-permute-done.8.refs_6_
  66.8 1.9 %collective-permute-start.11 = (bf16[512,1024]{1,0:T(8,128)(2,1)S(1)}, bf16[512,1024]{1,0:T(8,128)(2,1)}, u32[]{:S(2)}, u32[]{:S(2)}) collective-permute-start(bf16[512,1024]{1,0:T(8,128)(2,1)S(1)} %pad_maximum_fusion.refs_5_), channel_id=1, source_target_pairs={{0,4},{4,0},{1,5},{5,1},{2,6},{6,2},{3,7},{7,3},{8,12},{12,8},{9,1... | collective-permute-start | bytes 3145736 | tf_op jit(solution)/shard_map/ppermute | solution.py:25
  68.8 0.0 collective-permute-done.9.refs_7_
  68.8 2.4 %collective-permute-start.12 = (bf16[512,1024]{1,0:T(8,128)(2,1)}, bf16[512,1024]{1,0:T(8,128)(2,1)}, u32[]{:S(2)}, u32[]{:S(2)}) collective-permute-start(bf16[512,1024]{1,0:T(8,128)(2,1)} %collective-permute-done.8.refs_6_), channel_id=1, source_target_pairs={{0,4},{4,0},{1,5},{5,1},{2,6},{6,2},{3,7},{7,3},{8,12},{12,8},{9,1... | collective-permute-start | bytes 3145736 | tf_op jit(solution)/shard_map/ppermute | solution.py:25
  71.2 0.0 collective-permute-done.5.refs_4_
  71.2 1.9 %collective-permute-start.13 = (bf16[512,1024]{1,0:T(8,128)(2,1)}, bf16[512,1024]{1,0:T(8,128)(2,1)}, u32[]{:S(2)}, u32[]{:S(2)}) collective-permute-start(bf16[512,1024]{1,0:T(8,128)(2,1)} %collective-permute-done.9.refs_7_), channel_id=1, source_target_pairs={{0,4},{4,0},{1,5},{5,1},{2,6},{6,2},{3,7},{7,3},{8,12},{12,8},{9,1... | collective-permute-start | bytes 3145736 | tf_op jit(solution)/shard_map/ppermute | solution.py:25
  73.1 11.3 %collective-permute-done.10.refs_8_ = bf16[512,1024]{1,0:T(8,128)(2,1)} collective-permute-done((bf16[512,1024]{1,0:T(8,128)(2,1)S(1)}, bf16[512,1024]{1,0:T(8,128)(2,1)}, u32[]{:S(2)}, u32[]{:S(2)}) %collective-permute-start.10) | collective-permute-done | bytes 1048608 | tf_op jit(solution)/shard_map/ppermute | solution.py:25
  84.4 1.9 %collective-permute-start.14 = (bf16[512,1024]{1,0:T(8,128)(2,1)}, bf16[512,1024]{1,0:T(8,128)(2,1)}, u32[]{:S(2)}, u32[]{:S(2)}) collective-permute-start(bf16[512,1024]{1,0:T(8,128)(2,1)} %collective-permute-done.10.refs_8_), channel_id=1, source_target_pairs={{0,4},{4,0},{1,5},{5,1},{2,6},{6,2},{3,7},{7,3},{8,12},{12,8},{9,1... | collective-permute-start | bytes 3145736 | tf_op jit(solution)/shard_map/ppermute | solution.py:25
  86.3 0.0 collective-permute-done.2.up
  86.4 1.9 %collective-permute-start.6 = (bf16[2,2,256,256]{3,2,1,0:T(8,128)(2,1)}, bf16[2,2,256,256]{3,2,1,0:T(8,128)(2,1)S(1)}, u32[]{:S(2)}, u32[]{:S(2)}) collective-permute-start(bf16[2,2,256,256]{3,2,1,0:T(8,128)(2,1)} %collective-permute-done.5.refs_4_), channel_id=1, source_target_pairs={{0,224},{32,0},{64,32},{96,64},{128,96},{160,128},{192,160},{224,1... | collective-permute-start | bytes 1572872 | tf_op jit(solution)/shard_map/ppermute | solution.py:25
  88.3 0.1 pad_add_fusion.where
  88.4 0.0 copy-done.7
  88.4 0.9 broadcast_in_dim.15
  89.3 9.5 %all-to-all-start.1 = ((bf16[4,128,512]{2,1,0:T(8,128)(2,1)}), bf16[4,128,512]{2,1,0:T(8,128)(2,1)}, u32[]{:S(2)}, u32[]{:S(2)}) async-start(bf16[4,128,512]{2,1,0:T(8,128)(2,1)} %bitcast.16), calls=%async_computation.1 | async-start | bytes 1048576 | tf_op jit(solution)/shard_map/all_to_all | solution.py:258
  98.8 5.2 %collective-permute-done.6.down = bf16[2,2,256,256]{3,2,1,0:T(8,128)(2,1)S(1)} collective-permute-done((bf16[2,2,256,256]{3,2,1,0:T(8,128)(2,1)}, bf16[2,2,256,256]{3,2,1,0:T(8,128)(2,1)S(1)}, u32[]{:S(2)}, u32[]{:S(2)}) %collective-permute-start.6) | collective-permute-done | bytes 524320 | tf_op jit(solution)/shard_map/ppermute | solution.py:25
  104.0 1.9 %collective-permute-start.3 = (bf16[2,256,256]{2,1,0:T(8,128)(2,1)S(1)}, bf16[2,256,256]{2,1,0:T(8,128)(2,1)S(1)}, u32[]{:S(2)}, u32[]{:S(2)}) collective-permute-start(bf16[2,256,256]{2,1,0:T(8,128)(2,1)S(1)} %slice_bitcast_fusion.1), channel_id=1, source_target_pairs={{0,32},{32,64},{64,96},{96,128},{128,160},{160,192},{192,224},{224... | collective-permute-start | bytes 786440 | tf_op jit(solution)/shard_map/ppermute | solution.py:25
  105.9 0.0 collective-permute-done.11.refs_9_
  106.0 3.9 %collective-permute-start.7 = (bf16[2,256,256]{2,1,0:T(8,128)(2,1)S(1)}, bf16[2,256,256]{2,1,0:T(8,128)(2,1)S(1)}, u32[]{:S(2)}, u32[]{:S(2)}) collective-permute-start(bf16[2,256,256]{2,1,0:T(8,128)(2,1)S(1)} %slice_bitcast_fusion), channel_id=1, source_target_pairs={{0,224},{32,0},{64,32},{96,64},{128,96},{160,128},{192,160},{224,1... | collective-permute-start | bytes 786440 | tf_op jit(solution)/shard_map/ppermute | solution.py:25
  109.9 0.0 collective-permute-done.12.refs_10_
  109.9 0.0 collective-permute-done.13.refs_11_
  109.9 0.0 collective-permute-done.14.refs_12_
  109.9 0.0 copy-start.1
  109.9 1.0 copy-done.1
  111.0 0.0 copy-start.3
  111.0 1.0 copy-done.3
  112.0 7.3 %project_early.1 = (f32[512,1024]{1,0:T(8,128)S(1)}, bf16[6,256,1024]{2,1,0:T(8,128)(2,1)S(1)}) custom-call(s32[3]{0:T(128)S(1)} %pad_add_fusion.where, bf16[2,2,256,256]{3,2,1,0:T(8,128)(2,1)S(1)} %bitcast.15, bf16[2,2,256,256]{3,2,1,0:T(8,128)(2,1)S(1)} %collective-permute-done.refs_1_, bf16[2,2,256,256]{3,2,1,0:T(8,128)(2,1)S(1)} %copy-done.1, ...), custom_call_target="tpu_custom_call" | custom-call | flops 2684354560 | bytes 14680064 | tf_op jit(solution)/shard_map/project_early/pallas_call | solution.py:87
  119.3 1.3 project_next.1.partial
  120.6 0.0 copy-start.4
  120.6 0.0 collective-permute-done.3.first
  120.6 0.0 collective-permute-done.7.second
  120.6 0.7 project_rest.1.mine
  121.3 0.0 all-to-all-done.1.query
  121.3 1.9 %collective-permute-start.15 = (bf16[512,1024]{1,0:T(8,128)(2,1)S(1)}, bf16[512,1024]{1,0:T(8,128)(2,1)S(1)}, u32[]{:S(2)}, u32[]{:S(2)}) collective-permute-start(bf16[512,1024]{1,0:T(8,128)(2,1)S(1)} %project_rest.1.mine), channel_id=1, source_target_pairs={{0,4},{4,0},{1,5},{5,1},{2,6},{6,2},{3,7},{7,3},{8,12},{12,8},{9,1... | collective-permute-start | bytes 3145736 | tf_op jit(solution)/shard_map/ppermute | solution.py:25
  123.3 2.6 %collective-permute-done.15.theirs = bf16[512,1024]{1,0:T(8,128)(2,1)S(1)} collective-permute-done((bf16[512,1024]{1,0:T(8,128)(2,1)S(1)}, bf16[512,1024]{1,0:T(8,128)(2,1)S(1)}, u32[]{:S(2)}, u32[]{:S(2)}) %collective-permute-start.15) | collective-permute-done | bytes 1048608 | tf_op jit(solution)/shard_map/ppermute | solution.py:25
  125.9 0.0 copy-done.4
  125.9 3.2 %attend.1 = bf16[4,144,512]{2,1,0:T(8,128)(2,1)S(1)} custom-call(s32[3]{0:T(128)S(1)} %pad_add_fusion.where, s32[2]{0:T(128)S(1)} %copy-done.4, bf16[4,128,512]{2,1,0:T(8,128)(2,1)} %all-to-all-done.1.query, bf16[512,1024]{1,0:T(8,128)(2,1)S(1)} %project_rest.1.mine, bf16[512,1024]{1,0:T(8,128)(2,1)S(1)} %collective-permute-done.15.theirs), custom_call_target="tpu_custom_call" | custom-call | flops 1073741824 | bytes 4194304 | tf_op jit(solution)/shard_map/attend/pallas_call | solution.py:203
  129.1 19.9 %all_to_all.15.parts = bf16[4,144,512]{2,1,0:T(8,128)(2,1)} all-to-all(bf16[4,144,512]{2,1,0:T(8,128)(2,1)S(1)} %attend.1), channel_id=1, replica_groups=mesh['zh'=2,'y'=8,'xh'=2,'xl'=2,'c'=2,'mp'=4] {'xh','xl'}, dimensions={0} | all-to-all | bytes 1179648 | tf_op jit(solution)/shard_map/all_to_all | solution.py:266
  148.9 2.2 %merge.1 = bf16[1,2,128,512]{3,2,1,0:T(8,128)(2,1)} custom-call(bf16[4,144,512]{2,1,0:T(8,128)(2,1)} %all_to_all.15.parts), custom_call_target="tpu_custom_call" | custom-call | tf_op jit(solution)/shard_map/merge/pallas_call | solution.py:234
  (2 shorter events, 0.0 us)
Async XLA Ops:
  0.0 12.2 %copy-start.6 = (bf16[1,512,512]{2,1,0:T(8,128)(2,1)S(1)}, bf16[1,512,512]{2,1,0:T(8,128)(2,1)}, u32[]{:S(2)}) copy-start(bf16[1,512,512]{2,1,0:T(8,128)(2,1)} %param.7) | copy-start | bytes 1572868
  0.0 12.2 %copy-start.5 = (bf16[1,512,512]{2,1,0:T(8,128)(2,1)S(1)}, bf16[1,512,512]{2,1,0:T(8,128)(2,1)}, u32[]{:S(2)}) copy-start(bf16[1,512,512]{2,1,0:T(8,128)(2,1)} %param.8) | copy-start | bytes 1572868
  0.0 88.4 %copy-start.7 = (bf16[1,2,128,512]{3,2,1,0:T(8,128)(2,1)S(1)}, bf16[1,2,128,512]{3,2,1,0:T(8,128)(2,1)}, u32[]{:S(2)}) copy-start(bf16[1,2,128,512]{3,2,1,0:T(8,128)(2,1)} %param.5) | copy-start | bytes 786436
  1.9 27.7 %all-to-all-start = ((bf16[4,256,256]{2,1,0:T(8,128)(2,1)}), bf16[4,256,256]{2,1,0:T(8,128)(2,1)S(1)}, u32[]{:S(2)}, u32[]{:S(2)}) async-start(bf16[4,256,256]{2,1,0:T(8,128)(2,1)} %bitcast.5), calls=%async_computation | async-start | bytes 1048576 | tf_op jit(solution)/shard_map/all_to_all | solution.py:248
  29.6 17.1 %collective-permute-start = (bf16[2,2,256,256]{3,2,1,0:T(8,128)(2,1)S(1)}, bf16[2,2,256,256]{3,2,1,0:T(8,128)(2,1)S(1)}, u32[]{:S(2)}, u32[]{:S(2)}) collective-permute-start(bf16[2,2,256,256]{3,2,1,0:T(8,128)(2,1)S(1)} %bitcast.13), channel_id=1, source_target_pairs={{0,32},{32,64},{64,96},{96,128},{128,160},{160,192},{192,224},{224... | collective-permute-start | bytes 1572872 | tf_op jit(solution)/shard_map/ppermute | solution.py:25
  34.3 32.5 %collective-permute-start.8 = (bf16[512,1024]{1,0:T(8,128)(2,1)S(1)}, bf16[512,1024]{1,0:T(8,128)(2,1)}, u32[]{:S(2)}, u32[]{:S(2)}) collective-permute-start(bf16[512,1024]{1,0:T(8,128)(2,1)S(1)} %pad_maximum_fusion.refs_5_), channel_id=1, source_target_pairs={{0,8},{8,16},{16,24},{24,0},{1,9},{9,17},{17,25},{25,1},{2,10},{10... | collective-permute-start | bytes 3145736 | tf_op jit(solution)/shard_map/ppermute | solution.py:25
  37.8 31.0 %collective-permute-start.9 = (bf16[512,1024]{1,0:T(8,128)(2,1)S(1)}, bf16[512,1024]{1,0:T(8,128)(2,1)}, u32[]{:S(2)}, u32[]{:S(2)}) collective-permute-start(bf16[512,1024]{1,0:T(8,128)(2,1)S(1)} %pad_maximum_fusion.refs_5_), channel_id=1, source_target_pairs={{0,24},{8,0},{16,8},{24,16},{1,25},{9,1},{17,9},{25,17},{2,26},{10... | collective-permute-start | bytes 3145736 | tf_op jit(solution)/shard_map/ppermute | solution.py:25
  41.4 14.7 %collective-permute-start.4 = (bf16[2,2,256,256]{3,2,1,0:T(8,128)(2,1)S(1)}, bf16[2,2,256,256]{3,2,1,0:T(8,128)(2,1)S(1)}, u32[]{:S(2)}, u32[]{:S(2)}) collective-permute-start(bf16[2,2,256,256]{3,2,1,0:T(8,128)(2,1)S(1)} %bitcast.14), channel_id=1, source_target_pairs={{0,224},{32,0},{64,32},{96,64},{128,96},{160,128},{192,160},{224,1... | collective-permute-start | bytes 1572872 | tf_op jit(solution)/shard_map/ppermute | solution.py:25
  43.3 41.1 %collective-permute-start.10 = (bf16[512,1024]{1,0:T(8,128)(2,1)S(1)}, bf16[512,1024]{1,0:T(8,128)(2,1)}, u32[]{:S(2)}, u32[]{:S(2)}) collective-permute-start(bf16[512,1024]{1,0:T(8,128)(2,1)S(1)} %pad_maximum_fusion.refs_5_), channel_id=1, source_target_pairs={{0,16},{8,24},{16,0},{24,8},{1,17},{9,25},{17,1},{25,9},{2,18},{10... | collective-permute-start | bytes 3145736 | tf_op jit(solution)/shard_map/ppermute | solution.py:25
  46.8 13.7 %collective-permute-start.1 = (bf16[2,2,256,256]{3,2,1,0:T(8,128)(2,1)S(1)}, bf16[2,2,256,256]{3,2,1,0:T(8,128)(2,1)S(1)}, u32[]{:S(2)}, u32[]{:S(2)}) collective-permute-start(bf16[2,2,256,256]{3,2,1,0:T(8,128)(2,1)S(1)} %collective-permute-done.refs_1_), channel_id=1, source_target_pairs={{0,32},{32,64},{64,96},{96,128},{128,160},{160,192},{192,224},{224... | collective-permute-start | bytes 1572872 | tf_op jit(solution)/shard_map/ppermute | solution.py:25
  56.1 15.1 %collective-permute-start.5 = (bf16[2,2,256,256]{3,2,1,0:T(8,128)(2,1)S(1)}, bf16[2,2,256,256]{3,2,1,0:T(8,128)(2,1)}, u32[]{:S(2)}, u32[]{:S(2)}) collective-permute-start(bf16[2,2,256,256]{3,2,1,0:T(8,128)(2,1)S(1)} %collective-permute-done.4.refs_2_), channel_id=1, source_target_pairs={{0,224},{32,0},{64,32},{96,64},{128,96},{160,128},{192,160},{224,1... | collective-permute-start | bytes 1572872 | tf_op jit(solution)/shard_map/ppermute | solution.py:25
  58.0 0.8 copy-start
  60.5 25.9 %collective-permute-start.2 = (bf16[2,2,256,256]{3,2,1,0:T(8,128)(2,1)S(1)}, bf16[2,2,256,256]{3,2,1,0:T(8,128)(2,1)S(1)}, u32[]{:S(2)}, u32[]{:S(2)}) collective-permute-start(bf16[2,2,256,256]{3,2,1,0:T(8,128)(2,1)S(1)} %collective-permute-done.1.refs_3_), channel_id=1, source_target_pairs={{0,32},{32,64},{64,96},{96,128},{128,160},{160,192},{192,224},{224... | collective-permute-start | bytes 1572872 | tf_op jit(solution)/shard_map/ppermute | solution.py:25
  66.0 0.8 copy-start.2
  66.8 39.1 %collective-permute-start.11 = (bf16[512,1024]{1,0:T(8,128)(2,1)S(1)}, bf16[512,1024]{1,0:T(8,128)(2,1)}, u32[]{:S(2)}, u32[]{:S(2)}) collective-permute-start(bf16[512,1024]{1,0:T(8,128)(2,1)S(1)} %pad_maximum_fusion.refs_5_), channel_id=1, source_target_pairs={{0,4},{4,0},{1,5},{5,1},{2,6},{6,2},{3,7},{7,3},{8,12},{12,8},{9,1... | collective-permute-start | bytes 3145736 | tf_op jit(solution)/shard_map/ppermute | solution.py:25
  68.8 41.1 %collective-permute-start.12 = (bf16[512,1024]{1,0:T(8,128)(2,1)}, bf16[512,1024]{1,0:T(8,128)(2,1)}, u32[]{:S(2)}, u32[]{:S(2)}) collective-permute-start(bf16[512,1024]{1,0:T(8,128)(2,1)} %collective-permute-done.8.refs_6_), channel_id=1, source_target_pairs={{0,4},{4,0},{1,5},{5,1},{2,6},{6,2},{3,7},{7,3},{8,12},{12,8},{9,1... | collective-permute-start | bytes 3145736 | tf_op jit(solution)/shard_map/ppermute | solution.py:25
  71.2 38.7 %collective-permute-start.13 = (bf16[512,1024]{1,0:T(8,128)(2,1)}, bf16[512,1024]{1,0:T(8,128)(2,1)}, u32[]{:S(2)}, u32[]{:S(2)}) collective-permute-start(bf16[512,1024]{1,0:T(8,128)(2,1)} %collective-permute-done.9.refs_7_), channel_id=1, source_target_pairs={{0,4},{4,0},{1,5},{5,1},{2,6},{6,2},{3,7},{7,3},{8,12},{12,8},{9,1... | collective-permute-start | bytes 3145736 | tf_op jit(solution)/shard_map/ppermute | solution.py:25
  84.4 25.5 %collective-permute-start.14 = (bf16[512,1024]{1,0:T(8,128)(2,1)}, bf16[512,1024]{1,0:T(8,128)(2,1)}, u32[]{:S(2)}, u32[]{:S(2)}) collective-permute-start(bf16[512,1024]{1,0:T(8,128)(2,1)} %collective-permute-done.10.refs_8_), channel_id=1, source_target_pairs={{0,4},{4,0},{1,5},{5,1},{2,6},{6,2},{3,7},{7,3},{8,12},{12,8},{9,1... | collective-permute-start | bytes 3145736 | tf_op jit(solution)/shard_map/ppermute | solution.py:25
  86.4 17.6 %collective-permute-start.6 = (bf16[2,2,256,256]{3,2,1,0:T(8,128)(2,1)}, bf16[2,2,256,256]{3,2,1,0:T(8,128)(2,1)S(1)}, u32[]{:S(2)}, u32[]{:S(2)}) collective-permute-start(bf16[2,2,256,256]{3,2,1,0:T(8,128)(2,1)} %collective-permute-done.5.refs_4_), channel_id=1, source_target_pairs={{0,224},{32,0},{64,32},{96,64},{128,96},{160,128},{192,160},{224,1... | collective-permute-start | bytes 1572872 | tf_op jit(solution)/shard_map/ppermute | solution.py:25
  89.3 32.0 %all-to-all-start.1 = ((bf16[4,128,512]{2,1,0:T(8,128)(2,1)}), bf16[4,128,512]{2,1,0:T(8,128)(2,1)}, u32[]{:S(2)}, u32[]{:S(2)}) async-start(bf16[4,128,512]{2,1,0:T(8,128)(2,1)} %bitcast.16), calls=%async_computation.1 | async-start | bytes 1048576 | tf_op jit(solution)/shard_map/all_to_all | solution.py:258
  104.0 16.6 %collective-permute-start.3 = (bf16[2,256,256]{2,1,0:T(8,128)(2,1)S(1)}, bf16[2,256,256]{2,1,0:T(8,128)(2,1)S(1)}, u32[]{:S(2)}, u32[]{:S(2)}) collective-permute-start(bf16[2,256,256]{2,1,0:T(8,128)(2,1)S(1)} %slice_bitcast_fusion.1), channel_id=1, source_target_pairs={{0,32},{32,64},{64,96},{96,128},{128,160},{160,192},{192,224},{224... | collective-permute-start | bytes 786440 | tf_op jit(solution)/shard_map/ppermute | solution.py:25
  106.0 14.6 %collective-permute-start.7 = (bf16[2,256,256]{2,1,0:T(8,128)(2,1)S(1)}, bf16[2,256,256]{2,1,0:T(8,128)(2,1)S(1)}, u32[]{:S(2)}, u32[]{:S(2)}) collective-permute-start(bf16[2,256,256]{2,1,0:T(8,128)(2,1)S(1)} %slice_bitcast_fusion), channel_id=1, source_target_pairs={{0,224},{32,0},{64,32},{96,64},{128,96},{160,128},{192,160},{224,1... | collective-permute-start | bytes 786440 | tf_op jit(solution)/shard_map/ppermute | solution.py:25
  109.9 1.0 copy-start.1
  111.0 1.0 copy-start.3
  120.6 5.3 %copy-start.4 = (s32[2]{0:T(128)S(1)}, s32[2]{0:T(128)}, u32[]{:S(2)}) copy-start(s32[2]{0:T(128)} %lengths.1) | copy-start | bytes 28
  121.3 4.6 %collective-permute-start.15 = (bf16[512,1024]{1,0:T(8,128)(2,1)S(1)}, bf16[512,1024]{1,0:T(8,128)(2,1)S(1)}, u32[]{:S(2)}, u32[]{:S(2)}) collective-permute-start(bf16[512,1024]{1,0:T(8,128)(2,1)S(1)} %project_rest.1.mine), channel_id=1, source_target_pairs={{0,4},{4,0},{1,5},{5,1},{2,6},{6,2},{3,7},{7,3},{8,12},{12,8},{9,1... | collective-permute-start | bytes 3145736 | tf_op jit(solution)/shard_map/ppermute | solution.py:25

commit v3 on v1

v3 whole, which is shorter than its diff:
```python
import math

import jax
import jax.numpy as jnp
from jax import lax
from jax.experimental import pallas as pl
from jax.experimental.pallas import tpu as pltpu
from jax.sharding import Mesh
from jax.sharding import PartitionSpec as P

HEAD_DIM = 256
SEGMENT = ("zh", "y")
CTX = ("x", "c")
ROWS = 256
FEATS = 256
VMEM = pl.BlockSpec(memory_space=pltpu.VMEM)
SMEM = pl.BlockSpec(memory_space=pltpu.SMEM)
ANY = pl.BlockSpec(memory_space=pl.ANY)


def shift(array, axis, by):
    n = lax.axis_size(axis)
    return lax.ppermute(array, axis, [(i, (i + by) % n) for i in range(n)])


def ring_of_eight(block):
    up, down = block, block
    pieces = [block]
    for _ in range(3):
        up, down = shift(up, "y", 1), shift(down, "y", -1)
        pieces += [up, down]
    return pieces, (shift(up[0], "y", 1), shift(down[1], "y", -1))


def ring_of_four(block):
    half = block.shape[0] // 2
    right, left = shift(block, "x", 1), shift(block, "x", -1)
    return [block, right, left, shift(right[:half], "x", 1), shift(left[half:], "x", -1)]


X_OFFSETS = (0, 3, 1, 2, 2)


def slot_of(relative):
    odd_even = jnp.where(relative < 4, 2 * relative, 2 * (8 - relative) - 1)
    return jnp.where(relative == 4, 7, jnp.where(relative == 0, 0, odd_even))


def store_heads(out, acc, n):
    kind, head = n // 2, n % 2
    for doc in range(2):
        out[doc * 2 + head, :ROWS, kind * HEAD_DIM : (kind + 1) * HEAD_DIM] = acc[doc * ROWS : (doc + 1) * ROWS]


def project_most_kernel(where, *refs):
    enc, own, other = refs[:7], refs[7:12], refs[12:17]
    out, w_left, enc_all, w_all, sem_e, sem_w = refs[17:]
    y, x, core = where[0], where[1], where[2]
    parts = []
    for side, blocks in enumerate((own, other)):
        of_core = core if side == 0 else 1 - core
        for piece, ref in enumerate(blocks):
            block = lax.rem(x + X_OFFSETS[piece], 4)
            for part in range(ref.shape[0] // FEATS):
                within = 1 if piece == 4 else part
                segment = (block * 2 + of_core) * 2 + within
                relative = lax.rem(lax.rem(segment, 8) - y + 8, 8)
                row = (slot_of(relative) * 2 + segment // 8) * FEATS
                parts.append((ref, part * FEATS, pl.multiple_of(row, FEATS)))
    enc_copies = [
        pltpu.make_async_copy(
            ref.at[high],
            enc_all.at[:, :, pl.ds((2 * piece + high) * FEATS, FEATS)],
            sem_e.at[2 * piece + high],
        )
        for piece, ref in enumerate(enc)
        for high in range(2)
    ]
    half = 2 * HEAD_DIM
    w_copies = [
        [
            pltpu.make_async_copy(
                ref.at[pl.ds(start, FEATS), pl.ds(kind * half, half)],
                w_all.at[pl.ds(row, FEATS), pl.ds(kind * half, half)],
                sem_w.at[kind, n],
            )
            for n, (ref, start, row) in enumerate(parts)
        ]
        for kind in range(2)
    ]
    for copy in enc_copies + w_copies[0] + w_copies[1]:
        copy.start()
    for copy in enc_copies:
        copy.wait()
    depth = 2 * len(enc) * FEATS
    lhs = enc_all[...].reshape(2 * ROWS, depth)
    for kind in range(2):
        for copy in w_copies[kind]:
            copy.wait()
        for head in range(2):
            n = 2 * kind + head
            cols = slice(n * HEAD_DIM, (n + 1) * HEAD_DIM)
            out[:, cols] = jnp.dot(lhs, w_all[:depth, cols], preferred_element_type=jnp.float32)
    for high in range(2):
        w_left[high] = w_all[depth + high * FEATS : depth + (high + 1) * FEATS, :]


def project_most(where, enc, own, other):
    return pl.pallas_call(
        project_most_kernel,
        out_shape=(
            jax.ShapeDtypeStruct((2 * ROWS, 4 * HEAD_DIM), jnp.float32),
            jax.ShapeDtypeStruct((2, FEATS, 4 * HEAD_DIM), jnp.bfloat16),
        ),
        in_specs=[SMEM] + [ANY] * 17,
        out_specs=(VMEM, VMEM),
        scratch_shapes=[
            pltpu.VMEM((2, ROWS, 14 * FEATS), jnp.bfloat16),
            pltpu.VMEM((4096, 4 * HEAD_DIM), jnp.bfloat16),
            pltpu.SemaphoreType.DMA((14,)),
            pltpu.SemaphoreType.DMA((2, 16)),
        ],
        compiler_params=pltpu.CompilerParams(vmem_limit_bytes=32 * 2**20),
        cost_estimate=pl.CostEstimate(
            flops=2 * 512 * 3584 * 1024, bytes_accessed=14 * 2**20, transcendentals=0
        ),
        name="project_most",
    )(where, *enc, *own, *other)


def project_rest_kernel(first, second, partial, w_left, queries, out):
    first_rows = first[...].reshape(2 * ROWS, FEATS)
    second_rows = second[...].reshape(2 * ROWS, FEATS)
    for n in range(4):
        cols = slice(n * HEAD_DIM, (n + 1) * HEAD_DIM)
        acc = jnp.dot(first_rows, w_left[0, :, cols], preferred_element_type=jnp.float32)
        acc += jnp.dot(second_rows, w_left[1, :, cols], preferred_element_type=jnp.float32)
        store_heads(out, (acc + partial[:, cols]).astype(jnp.bfloat16), n)
    for doc in range(2):
        for head in range(2):
            cols = slice(head * HEAD_DIM, (head + 1) * HEAD_DIM)
            for part in range(2):
                out[doc * 2 + head, ROWS:, part * HEAD_DIM : (part + 1) * HEAD_DIM] = queries[
                    0, doc, part * 64 : (part + 1) * 64, cols
                ]


def project_rest(first, second, partial, w_left, queries):
    return pl.pallas_call(
        project_rest_kernel,
        out_shape=jax.ShapeDtypeStruct((4, ROWS + 64, 2 * HEAD_DIM), jnp.bfloat16),
        in_specs=[VMEM] * 5,
        out_specs=VMEM,
        compiler_params=pltpu.CompilerParams(vmem_limit_bytes=32 * 2**20),
        cost_estimate=pl.CostEstimate(
            flops=2 * 512 * 512 * 1024, bytes_accessed=5 * 2**20, transcendentals=0
        ),
        name="project_rest",
    )(first, second, partial, w_left, queries)


def attend_kernel(where, lengths, mine, theirs, out):
    x, core = where[1], where[2]
    length = lengths[x // 2]
    scale = 1.0 / math.sqrt(HEAD_DIM)
    steps = [(ref, of, p) for of, ref in ((core, mine), (1 - core, theirs)) for p in range(4)]
    for chunk in range(4):
        q = jnp.concatenate([mine[chunk, ROWS:, :HEAD_DIM], mine[chunk, ROWS:, HEAD_DIM:]], axis=0)
        scores = []
        for ref, of, p in steps:
            keys = ref[p, :ROWS, :HEAD_DIM]
            s = lax.dot_general(q, keys, (((1,), (1,)), ((), ())), preferred_element_type=jnp.float32)
            place = (p * 2 + of) * ROWS + lax.broadcasted_iota(jnp.int32, (1, ROWS), 1)
            scores.append(jnp.where(place < length, s * scale, -jnp.inf))
        top = scores[0]
        for s in scores[1:]:
            top = jnp.maximum(top, s)
        top = jnp.max(top, axis=1, keepdims=True)
        total, summed = None, None
        for s, (ref, _, p) in zip(scores, steps):
            w = jnp.exp(s - top)
            total = w if total is None else total + w
            o = jnp.dot(w.astype(jnp.bfloat16), ref[p, :ROWS, HEAD_DIM:], preferred_element_type=jnp.float32)
            summed = o if summed is None else summed + o
        total = jnp.sum(total, axis=1, keepdims=True)
        out[chunk] = (summed / total).astype(jnp.bfloat16)


def attend(where, lengths, mine, theirs):
    return pl.pallas_call(
        attend_kernel,
        out_shape=jax.ShapeDtypeStruct((4, 128, HEAD_DIM), jnp.bfloat16),
        in_specs=[SMEM, SMEM, VMEM, VMEM],
        out_specs=VMEM,
        compiler_params=pltpu.CompilerParams(vmem_limit_bytes=32 * 2**20),
        cost_estimate=pl.CostEstimate(
            flops=4 * 512 * 2048 * 256, bytes_accessed=4 * 2**20, transcendentals=512 * 2048
        ),
        name="attend",
    )(where, lengths, mine, theirs)


def on_device(queries, enc_states, key_weight, value_weight, enc_lengths):
    where = jnp.stack([lax.axis_index("y"), lax.axis_index("x"), lax.axis_index("c")])
    weight = jnp.concatenate([key_weight[0], value_weight[0]], axis=1)
    own = ring_of_four(weight)
    other = [shift(block, "c", 1) for block in own]
    enc, (first, second) = ring_of_eight(lax.all_gather(enc_states, "zh"))

    partial, w_left = project_most(where, enc, own, other)
    both = project_rest(first, second, partial, w_left, queries)
    mine = lax.all_to_all(both, "x", 0, 0)
    theirs = shift(mine, "c", 1)
    mixed = attend(where, enc_lengths, mine, theirs)
    mixed = lax.all_to_all(mixed, "x", 0, 0)
    mixed = mixed.reshape(2, 2, 128, HEAD_DIM).transpose(0, 2, 1, 3).reshape(2, 128, 2 * HEAD_DIM)
    return mixed[None]


def solution(mesh):
    torus = Mesh(mesh.devices.reshape(2, 8, 4, 2, 4), ("zh", "y", "x", "c", "mp"))
    return jax.shard_map(
        on_device,
        mesh=torus,
        in_specs=(
            P(SEGMENT, None, CTX, "mp"),
            P(None, CTX, SEGMENT),
            P(SEGMENT, CTX, "mp"),
            P(SEGMENT, CTX, "mp"),
            P(),
        ),
        out_specs=P(SEGMENT, None, CTX, "mp"),
        check_vma=False,
    )
```

time: 160 us -> 143 us (0.89)
  blocking collectives: 29.6 us -> 49.8 us
  waiting for transfers between devices: 32.7 us -> 16.7 us
  starting transfers between devices: 67.1 us -> 53.8 us
  Pallas kernels: 20.6 us -> 11.8 us
    all_gather x0 -> x1, blocking collectives: none -> 19.3 us  [on_device(): enc, (first, second) = ring_of_eight(lax.all_gather(enc_states, 'zh'))]
    ppermute x19 -> x18, waiting for transfers between devices: 27.4 us -> 16.7 us  [shift(): return lax.ppermute(array, axis, [(i, (i + by) % n) for i in range(n)])]
    ppermute x19 -> x18, starting transfers between devices: 62.8 us -> 53.8 us  [shift(): return lax.ppermute(array, axis, [(i, (i + by) % n) for i in range(n)])]
    all_to_all x1 -> x0, waiting for transfers between devices: 5.35 us -> none  [on_device(): query = lax.all_to_all(query, 'x', 0, 0)]
    all_to_all x1 -> x0, starting transfers between devices: 4.29 us -> none  [on_device(): query = lax.all_to_all(query, 'x', 0, 0)]
    pallas_call x1, Pallas kernels: 11.5 us -> 7.47 us  [project_most(): pl.pallas_call(project_most_kernel, out_shape=(jax.ShapeDtypeStruct((2 *...]
    unnamed x24 -> x22, local copies, waits for them, and re-layouts: 1.78 us -> 4.98 us
    pallas_call x1, Pallas kernels: 3.72 us -> 0.71 us  [project_rest(): pl.pallas_call(project_rest_kernel, out_shape=jax.ShapeDtypeStruct((4, RO...]
  transfers between devices with their start and end apart: 20 -> 18, of which waited for: 7 -> 5; matrix products, arithmetic and copies ran while one was open for 3% -> 2% of each run, Pallas kernels for 7% -> 5%
where the time goes in v3:
time: 143 us; the launch traced here: 142 us
  starting transfers between devices  53.8 us (38%)
  blocking collectives  49.8 us (35%)
  waiting for transfers between devices  16.7 us (12%)
  Pallas kernels  11.8 us (8%)
  local copies, waits for them, and re-layouts  8.22 us (6%)
  other arithmetic  1.43 us (1%)
    ppermute x18, starting transfers between devices, shift(): return lax.ppermute(array, axis, [(i, (i + by) % n) for i in range(n)])  53.8 us
    all_to_all x1, blocking collectives, on_device(): mine = lax.all_to_all(both, 'x', 0, 0)  20.9 us
    all_gather x1, blocking collectives, on_device(): enc, (first, second) = ring_of_eight(lax.all_gather(enc_states, 'zh'))  19.3 us
    ppermute x18, waiting for transfers between devices, shift(): return lax.ppermute(array, axis, [(i, (i + by) % n) for i in range(n)])  16.7 us
    all_to_all x1, blocking collectives, on_device(): mixed = lax.all_to_all(mixed, 'x', 0, 0)  9.63 us
    pallas_call x1, Pallas kernels, project_most(): pl.pallas_call(project_most_kernel, out_shape=(jax.ShapeDtypeStruct((2 *...  7.47 us
    unnamed x22, local copies, waits for them, and re-layouts  4.98 us
    pallas_call x1, Pallas kernels, attend(): pl.pallas_call(attend_kernel, out_shape=jax.ShapeDtypeStruct((4, 128, HEA...  3.58 us
  transfers between devices with their start and end apart: 18, of which 5 were waited for; matrix products, arithmetic and copies ran while one was open for 2% of the time, Pallas kernels for 5%

profile of v3, /device:TPU:152, one launch (start us, length us, event | category | flops | bytes accessed | tf_op | source)
XLA Modules:
  0.0 142.1 jit_solution(6187073717374917810)
XLA Ops:
  0.0 1.4 pad_maximum_fusion.refs_7_
  1.4 3.4 %collective-permute-start.8 = (bf16[512,1024]{1,0:T(8,128)(2,1)S(1)}, bf16[512,1024]{1,0:T(8,128)(2,1)S(1)}, u32[]{:S(2)}, u32[]{:S(2)}) collective-permute-start(bf16[512,1024]{1,0:T(8,128)(2,1)S(1)} %pad_maximum_fusion.refs_7_), channel_id=1, source_target_pairs={{0,8},{8,16},{16,24},{24,0},{1,9},{9,17},{17,25},{25,1},{2,10},{10... | collective-permute-start | bytes 3145736 | tf_op jit(solution)/shard_map/ppermute | solution.py:23
  4.8 3.7 %collective-permute-start.9 = (bf16[512,1024]{1,0:T(8,128)(2,1)S(1)}, bf16[512,1024]{1,0:T(8,128)(2,1)}, u32[]{:S(2)}, u32[]{:S(2)}) collective-permute-start(bf16[512,1024]{1,0:T(8,128)(2,1)S(1)} %pad_maximum_fusion.refs_7_), channel_id=1, source_target_pairs={{0,24},{8,0},{16,8},{24,16},{1,25},{9,1},{17,9},{25,17},{2,26},{10... | collective-permute-start | bytes 3145736 | tf_op jit(solution)/shard_map/ppermute | solution.py:23
  8.4 0.0 copy-done.10
  8.4 19.3 %all-gather = bf16[4,256,256]{2,1,0:T(8,128)(2,1)S(1)} all-gather(bf16[2,256,256]{2,1,0:T(8,128)(2,1)S(1)} %copy-done.10), channel_id=2, replica_groups=mesh['zh'=2,'y'=8,'x'=4,'c'=2,'mp'=4] {'zh'}, dimensions={0}, use_global_device_ids=true | all-gather | bytes 786432 | tf_op jit(solution)/shard_map/all_gather | solution.py:208
  27.8 4.7 %collective-permute-start = (bf16[2,2,256,256]{3,2,1,0:T(8,128)(2,1)S(1)}, bf16[2,2,256,256]{3,2,1,0:T(8,128)(2,1)S(1)}, u32[]{:S(2)}, u32[]{:S(2)}) collective-permute-start(bf16[2,2,256,256]{3,2,1,0:T(8,128)(2,1)S(1)} %bitcast.13), channel_id=1, source_target_pairs={{0,32},{32,64},{64,96},{96,128},{128,160},{160,192},{192,224},{224... | collective-permute-start | bytes 1572872 | tf_op jit(solution)/shard_map/ppermute | solution.py:23
  32.4 1.9 %collective-permute-start.4 = (bf16[2,2,256,256]{3,2,1,0:T(8,128)(2,1)S(1)}, bf16[2,2,256,256]{3,2,1,0:T(8,128)(2,1)S(1)}, u32[]{:S(2)}, u32[]{:S(2)}) collective-permute-start(bf16[2,2,256,256]{3,2,1,0:T(8,128)(2,1)S(1)} %bitcast.14), channel_id=1, source_target_pairs={{0,224},{32,0},{64,32},{96,64},{128,96},{160,128},{192,160},{224,1... | collective-permute-start | bytes 1572872 | tf_op jit(solution)/shard_map/ppermute | solution.py:23
  34.4 9.3 %collective-permute-done.refs_1_ = bf16[2,2,256,256]{3,2,1,0:T(8,128)(2,1)S(1)} collective-permute-done((bf16[2,2,256,256]{3,2,1,0:T(8,128)(2,1)S(1)}, bf16[2,2,256,256]{3,2,1,0:T(8,128)(2,1)S(1)}, u32[]{:S(2)}, u32[]{:S(2)}) %collective-permute-start) | collective-permute-done | bytes 524320 | tf_op jit(solution)/shard_map/ppermute | solution.py:23
  43.7 5.6 %collective-permute-start.1 = (bf16[2,2,256,256]{3,2,1,0:T(8,128)(2,1)S(1)}, bf16[2,2,256,256]{3,2,1,0:T(8,128)(2,1)}, u32[]{:S(2)}, u32[]{:S(2)}) collective-permute-start(bf16[2,2,256,256]{3,2,1,0:T(8,128)(2,1)S(1)} %collective-permute-done.refs_1_), channel_id=1, source_target_pairs={{0,32},{32,64},{64,96},{96,128},{128,160},{160,192},{192,224},{224... | collective-permute-start | bytes 1572872 | tf_op jit(solution)/shard_map/ppermute | solution.py:23
  49.3 0.0 collective-permute-done.4.refs_2_
  49.3 0.0 copy-start.3
  49.3 1.9 %collective-permute-start.5 = (bf16[2,2,256,256]{3,2,1,0:T(8,128)(2,1)S(1)}, bf16[2,2,256,256]{3,2,1,0:T(8,128)(2,1)}, u32[]{:S(2)}, u32[]{:S(2)}) collective-permute-start(bf16[2,2,256,256]{3,2,1,0:T(8,128)(2,1)S(1)} %collective-permute-done.4.refs_2_), channel_id=1, source_target_pairs={{0,224},{32,0},{64,32},{96,64},{128,96},{160,128},{192,160},{224,1... | collective-permute-start | bytes 1572872 | tf_op jit(solution)/shard_map/ppermute | solution.py:23
  51.2 0.0 collective-permute-done.8.refs_8_
  51.3 2.2 %collective-permute-start.10 = (bf16[256,1024]{1,0:T(8,128)(2,1)S(1)}, bf16[256,1024]{1,0:T(8,128)(2,1)S(1)}, u32[]{:S(2)}, u32[]{:S(2)}) collective-permute-start(bf16[256,1024]{1,0:T(8,128)(2,1)S(1)} %slice.18), channel_id=1, source_target_pairs={{0,8},{8,16},{16,24},{24,0},{1,9},{9,17},{17,25},{25,1},{2,10},{10... | collective-permute-start | bytes 1572872 | tf_op jit(solution)/shard_map/ppermute | solution.py:23
  53.5 0.0 collective-permute-done.9.refs_9_
  53.5 1.1 slice.19
  54.6 4.9 %collective-permute-start.11 = (bf16[256,1024]{1,0:T(8,128)(2,1)S(1)}, bf16[256,1024]{1,0:T(8,128)(2,1)S(1)}, u32[]{:S(2)}, u32[]{:S(2)}) collective-permute-start(bf16[256,1024]{1,0:T(8,128)(2,1)S(1)} %slice.19), channel_id=1, source_target_pairs={{0,24},{8,0},{16,8},{24,16},{1,25},{9,1},{17,9},{25,17},{2,26},{10... | collective-permute-start | bytes 1572872 | tf_op jit(solution)/shard_map/ppermute | solution.py:23
  59.5 0.2 collective-permute-done.1.refs_3_
  59.7 5.7 %collective-permute-start.2 = (bf16[2,2,256,256]{3,2,1,0:T(8,128)(2,1)}, bf16[2,2,256,256]{3,2,1,0:T(8,128)(2,1)S(1)}, u32[]{:S(2)}, u32[]{:S(2)}) collective-permute-start(bf16[2,2,256,256]{3,2,1,0:T(8,128)(2,1)} %collective-permute-done.1.refs_3_), channel_id=1, source_target_pairs={{0,32},{32,64},{64,96},{96,128},{128,160},{160,192},{192,224},{224... | collective-permute-start | bytes 1572872 | tf_op jit(solution)/shard_map/ppermute | solution.py:23
  65.4 0.0 collective-permute-done.5.refs_4_
  65.4 1.9 %collective-permute-start.6 = (bf16[2,2,256,256]{3,2,1,0:T(8,128)(2,1)}, bf16[2,2,256,256]{3,2,1,0:T(8,128)(2,1)}, u32[]{:S(2)}, u32[]{:S(2)}) collective-permute-start(bf16[2,2,256,256]{3,2,1,0:T(8,128)(2,1)} %collective-permute-done.5.refs_4_), channel_id=1, source_target_pairs={{0,224},{32,0},{64,32},{96,64},{128,96},{160,128},{192,160},{224,1... | collective-permute-start | bytes 1572872 | tf_op jit(solution)/shard_map/ppermute | solution.py:23
  67.3 1.9 %collective-permute-start.12 = (bf16[512,1024]{1,0:T(8,128)(2,1)S(1)}, bf16[512,1024]{1,0:T(8,128)(2,1)}, u32[]{:S(2)}, u32[]{:S(2)}) collective-permute-start(bf16[512,1024]{1,0:T(8,128)(2,1)S(1)} %pad_maximum_fusion.refs_7_), channel_id=1, source_target_pairs={{0,4},{4,0},{1,5},{5,1},{2,6},{6,2},{3,7},{7,3},{8,12},{12,8},{9,1... | collective-permute-start | bytes 3145736 | tf_op jit(solution)/shard_map/ppermute | solution.py:23
  69.2 0.0 copy-done.1
  69.3 0.0 collective-permute-done.10.refs_10_
  69.3 0.0 copy-done.3
  69.3 0.0 copy-start.5
  69.3 2.4 %collective-permute-start.13 = (bf16[512,1024]{1,0:T(8,128)(2,1)S(1)}, bf16[512,1024]{1,0:T(8,128)(2,1)}, u32[]{:S(2)}, u32[]{:S(2)}) collective-permute-start(bf16[512,1024]{1,0:T(8,128)(2,1)S(1)} %collective-permute-done.8.refs_8_), channel_id=1, source_target_pairs={{0,4},{4,0},{1,5},{5,1},{2,6},{6,2},{3,7},{7,3},{8,12},{12,8},{9,1... | collective-permute-start | bytes 3145736 | tf_op jit(solution)/shard_map/ppermute | solution.py:23
  71.7 0.0 copy-done.5
  71.7 0.0 collective-permute-done.11.refs_11_
  71.7 0.0 copy-start.7
  71.7 0.8 copy-done.7
  72.5 1.9 %collective-permute-start.14 = (bf16[512,1024]{1,0:T(8,128)(2,1)}, bf16[512,1024]{1,0:T(8,128)(2,1)}, u32[]{:S(2)}, u32[]{:S(2)}) collective-permute-start(bf16[512,1024]{1,0:T(8,128)(2,1)} %collective-permute-done.9.refs_9_), channel_id=1, source_target_pairs={{0,4},{4,0},{1,5},{5,1},{2,6},{6,2},{3,7},{7,3},{8,12},{12,8},{9,1... | collective-permute-start | bytes 3145736 | tf_op jit(solution)/shard_map/ppermute | solution.py:23
  74.4 0.7 collective-permute-done.2.refs_5_
  75.2 1.9 %collective-permute-start.15 = (bf16[256,1024]{1,0:T(8,128)(2,1)}, bf16[256,1024]{1,0:T(8,128)(2,1)S(1)}, u32[]{:S(2)}, u32[]{:S(2)}) collective-permute-start(bf16[256,1024]{1,0:T(8,128)(2,1)} %copy-done.5), channel_id=1, source_target_pairs={{0,4},{4,0},{1,5},{5,1},{2,6},{6,2},{3,7},{7,3},{8,12},{12,8},{9,1... | collective-permute-start | bytes 1572872 | tf_op jit(solution)/shard_map/ppermute | solution.py:23
  77.1 3.4 %collective-permute-done.6.refs_6_ = bf16[2,2,256,256]{3,2,1,0:T(8,128)(2,1)} collective-permute-done((bf16[2,2,256,256]{3,2,1,0:T(8,128)(2,1)}, bf16[2,2,256,256]{3,2,1,0:T(8,128)(2,1)}, u32[]{:S(2)}, u32[]{:S(2)}) %collective-permute-start.6) | collective-permute-done | bytes 524320 | tf_op jit(solution)/shard_map/ppermute | solution.py:23
  80.5 1.9 %collective-permute-start.16 = (bf16[256,1024]{1,0:T(8,128)(2,1)}, bf16[256,1024]{1,0:T(8,128)(2,1)S(1)}, u32[]{:S(2)}, u32[]{:S(2)}) collective-permute-start(bf16[256,1024]{1,0:T(8,128)(2,1)} %copy-done.7), channel_id=1, source_target_pairs={{0,4},{4,0},{1,5},{5,1},{2,6},{6,2},{3,7},{7,3},{8,12},{12,8},{9,1... | collective-permute-start | bytes 1572872 | tf_op jit(solution)/shard_map/ppermute | solution.py:23
  82.4 0.1 pad_add_fusion.where
  82.5 1.0 slice_bitcast_fusion
  83.5 0.0 copy-start
  83.5 0.0 collective-permute-done.12.refs_12_
  83.5 2.7 %collective-permute-start.3 = (bf16[2,256,256]{2,1,0:T(8,128)(2,1)S(1)}, bf16[2,256,256]{2,1,0:T(8,128)(2,1)S(1)}, u32[]{:S(2)}, u32[]{:S(2)}) collective-permute-start(bf16[2,256,256]{2,1,0:T(8,128)(2,1)S(1)} %slice_bitcast_fusion.1), channel_id=1, source_target_pairs={{0,32},{32,64},{64,96},{96,128},{128,160},{160,192},{192,224},{224... | collective-permute-start | bytes 786440 | tf_op jit(solution)/shard_map/ppermute | solution.py:23
  86.2 0.0 collective-permute-done.15.refs_15_
  86.2 3.3 %collective-permute-start.7 = (bf16[2,256,256]{2,1,0:T(8,128)(2,1)S(1)}, bf16[2,256,256]{2,1,0:T(8,128)(2,1)S(1)}, u32[]{:S(2)}, u32[]{:S(2)}) collective-permute-start(bf16[2,256,256]{2,1,0:T(8,128)(2,1)S(1)} %slice_bitcast_fusion), channel_id=1, source_target_pairs={{0,224},{32,0},{64,32},{96,64},{128,96},{160,128},{192,160},{224,1... | collective-permute-start | bytes 786440 | tf_op jit(solution)/shard_map/ppermute | solution.py:23
  89.5 0.0 collective-permute-done.16.refs_16_
  89.5 0.0 collective-permute-done.13.refs_13_
  89.5 0.0 collective-permute-done.14.refs_14_
  89.5 0.0 copy-start.2
  89.5 1.0 copy-done.2
  90.6 1.0 copy-done.4
  91.6 1.0 copy-done.6
  92.7 1.0 copy-done.8
  93.7 7.5 %project_most.1 = (f32[512,1024]{1,0:T(8,128)S(1)}, bf16[2,256,1024]{2,1,0:T(8,128)(2,1)S(1)}) custom-call(s32[3]{0:T(128)S(1)} %pad_add_fusion.where, bf16[2,2,256,256]{3,2,1,0:T(8,128)(2,1)S(1)} %bitcast.15, bf16[2,2,256,256]{3,2,1,0:T(8,128)(2,1)S(1)} %copy-done.2, bf16[2,2,256,256]{3,2,1,0:T(8,128)(2,1)S(1)} %copy-done.4, ...), custom_call_target="tpu_custom_call" | custom-call | flops 3758096384 | bytes 14680064 | tf_op jit(solution)/shard_map/project_most/pallas_call | solution.py:109
  101.2 0.0 collective-permute-done.3.first
  101.2 0.0 collective-permute-done.7.second
  101.2 0.0 copy-done
  101.2 0.7 project_rest.1
  101.9 0.0 copy-start.9
  101.9 20.9 %all_to_all.10.mine = bf16[4,320,512]{2,1,0:T(8,128)(2,1)S(1)} all-to-all(bf16[4,320,512]{2,1,0:T(8,128)(2,1)S(1)} %project_rest.1), channel_id=1, replica_groups=mesh['zh'=2,'y'=8,'x'=4,'c'=2,'mp'=4] {'x'}, dimensions={0} | all-to-all | bytes 2621440 | tf_op jit(solution)/shard_map/all_to_all | solution.py:212
  122.8 1.9 %collective-permute-start.17 = (bf16[4,320,512]{2,1,0:T(8,128)(2,1)S(1)}, bf16[4,320,512]{2,1,0:T(8,128)(2,1)S(1)}, u32[]{:S(2)}, u32[]{:S(2)}) collective-permute-start(bf16[4,320,512]{2,1,0:T(8,128)(2,1)S(1)} %all_to_all.10.mine), channel_id=1, source_target_pairs={{0,4},{4,0},{1,5},{5,1},{2,6},{6,2},{3,7},{7,3},{8,12},{12,8},{9,1... | collective-permute-start | bytes 3932168 | tf_op jit(solution)/shard_map/ppermute | solution.py:23
  124.8 3.0 %collective-permute-done.17.theirs = bf16[4,320,512]{2,1,0:T(8,128)(2,1)S(1)} collective-permute-done((bf16[4,320,512]{2,1,0:T(8,128)(2,1)S(1)}, bf16[4,320,512]{2,1,0:T(8,128)(2,1)S(1)}, u32[]{:S(2)}, u32[]{:S(2)}) %collective-permute-start.17) | collective-permute-done | bytes 1310752 | tf_op jit(solution)/shard_map/ppermute | solution.py:23
  127.8 3.6 %attend.1 = bf16[4,128,256]{2,1,0:T(8,128)(2,1)S(1)} custom-call(s32[3]{0:T(128)S(1)} %pad_add_fusion.where, s32[2]{0:T(128)S(1)} %copy-done.9, bf16[4,320,512]{2,1,0:T(8,128)(2,1)S(1)} %all_to_all.10.mine, bf16[4,320,512]{2,1,0:T(8,128)(2,1)S(1)} %collective-permute-done.17.theirs), custom_call_target="tpu_custom_call" | custom-call | flops 1073741824 | bytes 4194304 | tf_op jit(solution)/shard_map/attend/pallas_call | solution.py:190
  131.3 9.6 %all_to_all.11 = bf16[4,128,256]{2,1,0:T(8,128)(2,1)S(1)} all-to-all(bf16[4,128,256]{2,1,0:T(8,128)(2,1)S(1)} %attend.1), channel_id=1, replica_groups=mesh['zh'=2,'y'=8,'x'=4,'c'=2,'mp'=4] {'x'}, dimensions={0} | all-to-all | bytes 524288 | tf_op jit(solution)/shard_map/all_to_all | solution.py:215
  141.0 0.3 copy.7
  141.2 0.9 broadcast_in_dim_reshape.3
  (8 shorter events, 0.1 us)
Async XLA Ops:
  0.0 8.4 %copy-start.10 = (bf16[2,256,256]{2,1,0:T(8,128)(2,1)S(1)}, bf16[2,256,256]{2,1,0:T(8,128)(2,1)}, u32[]{:S(2)}) copy-start(bf16[2,256,256]{2,1,0:T(8,128)(2,1)} %param.6) | copy-start | bytes 786436
  1.4 49.9 %collective-permute-start.8 = (bf16[512,1024]{1,0:T(8,128)(2,1)S(1)}, bf16[512,1024]{1,0:T(8,128)(2,1)S(1)}, u32[]{:S(2)}, u32[]{:S(2)}) collective-permute-start(bf16[512,1024]{1,0:T(8,128)(2,1)S(1)} %pad_maximum_fusion.refs_7_), channel_id=1, source_target_pairs={{0,8},{8,16},{16,24},{24,0},{1,9},{9,17},{17,25},{25,1},{2,10},{10... | collective-permute-start | bytes 3145736 | tf_op jit(solution)/shard_map/ppermute | solution.py:23
  4.8 48.7 %collective-permute-start.9 = (bf16[512,1024]{1,0:T(8,128)(2,1)S(1)}, bf16[512,1024]{1,0:T(8,128)(2,1)}, u32[]{:S(2)}, u32[]{:S(2)}) collective-permute-start(bf16[512,1024]{1,0:T(8,128)(2,1)S(1)} %pad_maximum_fusion.refs_7_), channel_id=1, source_target_pairs={{0,24},{8,0},{16,8},{24,16},{1,25},{9,1},{17,9},{25,17},{2,26},{10... | collective-permute-start | bytes 3145736 | tf_op jit(solution)/shard_map/ppermute | solution.py:23
  27.8 15.9 %collective-permute-start = (bf16[2,2,256,256]{3,2,1,0:T(8,128)(2,1)S(1)}, bf16[2,2,256,256]{3,2,1,0:T(8,128)(2,1)S(1)}, u32[]{:S(2)}, u32[]{:S(2)}) collective-permute-start(bf16[2,2,256,256]{3,2,1,0:T(8,128)(2,1)S(1)} %bitcast.13), channel_id=1, source_target_pairs={{0,32},{32,64},{64,96},{96,128},{128,160},{160,192},{192,224},{224... | collective-permute-start | bytes 1572872 | tf_op jit(solution)/shard_map/ppermute | solution.py:23
  32.4 16.8 %collective-permute-start.4 = (bf16[2,2,256,256]{3,2,1,0:T(8,128)(2,1)S(1)}, bf16[2,2,256,256]{3,2,1,0:T(8,128)(2,1)S(1)}, u32[]{:S(2)}, u32[]{:S(2)}) collective-permute-start(bf16[2,2,256,256]{3,2,1,0:T(8,128)(2,1)S(1)} %bitcast.14), channel_id=1, source_target_pairs={{0,224},{32,0},{64,32},{96,64},{128,96},{160,128},{192,160},{224,1... | collective-permute-start | bytes 1572872 | tf_op jit(solution)/shard_map/ppermute | solution.py:23
  43.7 25.6 %copy-start.1 = (bf16[2,2,256,256]{3,2,1,0:T(8,128)(2,1)}, bf16[2,2,256,256]{3,2,1,0:T(8,128)(2,1)S(1)}, u32[]{:S(2)}) copy-start(bf16[2,2,256,256]{3,2,1,0:T(8,128)(2,1)S(1)} %collective-permute-done.refs_1_) | copy-start | bytes 1572868
  43.7 16.0 %collective-permute-start.1 = (bf16[2,2,256,256]{3,2,1,0:T(8,128)(2,1)S(1)}, bf16[2,2,256,256]{3,2,1,0:T(8,128)(2,1)}, u32[]{:S(2)}, u32[]{:S(2)}) collective-permute-start(bf16[2,2,256,256]{3,2,1,0:T(8,128)(2,1)S(1)} %collective-permute-done.refs_1_), channel_id=1, source_target_pairs={{0,32},{32,64},{64,96},{96,128},{128,160},{160,192},{192,224},{224... | collective-permute-start | bytes 1572872 | tf_op jit(solution)/shard_map/ppermute | solution.py:23
  49.3 20.0 %copy-start.3 = (bf16[2,2,256,256]{3,2,1,0:T(8,128)(2,1)}, bf16[2,2,256,256]{3,2,1,0:T(8,128)(2,1)S(1)}, u32[]{:S(2)}) copy-start(bf16[2,2,256,256]{3,2,1,0:T(8,128)(2,1)S(1)} %collective-permute-done.4.refs_2_) | copy-start | bytes 1572868
  49.3 16.1 %collective-permute-start.5 = (bf16[2,2,256,256]{3,2,1,0:T(8,128)(2,1)S(1)}, bf16[2,2,256,256]{3,2,1,0:T(8,128)(2,1)}, u32[]{:S(2)}, u32[]{:S(2)}) collective-permute-start(bf16[2,2,256,256]{3,2,1,0:T(8,128)(2,1)S(1)} %collective-permute-done.4.refs_2_), channel_id=1, source_target_pairs={{0,224},{32,0},{64,32},{96,64},{128,96},{160,128},{192,160},{224,1... | collective-permute-start | bytes 1572872 | tf_op jit(solution)/shard_map/ppermute | solution.py:23
  51.3 18.0 %collective-permute-start.10 = (bf16[256,1024]{1,0:T(8,128)(2,1)S(1)}, bf16[256,1024]{1,0:T(8,128)(2,1)S(1)}, u32[]{:S(2)}, u32[]{:S(2)}) collective-permute-start(bf16[256,1024]{1,0:T(8,128)(2,1)S(1)} %slice.18), channel_id=1, source_target_pairs={{0,8},{8,16},{16,24},{24,0},{1,9},{9,17},{17,25},{25,1},{2,10},{10... | collective-permute-start | bytes 1572872 | tf_op jit(solution)/shard_map/ppermute | solution.py:23
  54.6 17.1 %collective-permute-start.11 = (bf16[256,1024]{1,0:T(8,128)(2,1)S(1)}, bf16[256,1024]{1,0:T(8,128)(2,1)S(1)}, u32[]{:S(2)}, u32[]{:S(2)}) collective-permute-start(bf16[256,1024]{1,0:T(8,128)(2,1)S(1)} %slice.19), channel_id=1, source_target_pairs={{0,24},{8,0},{16,8},{24,16},{1,25},{9,1},{17,9},{25,17},{2,26},{10... | collective-permute-start | bytes 1572872 | tf_op jit(solution)/shard_map/ppermute | solution.py:23
  59.7 15.5 %collective-permute-start.2 = (bf16[2,2,256,256]{3,2,1,0:T(8,128)(2,1)}, bf16[2,2,256,256]{3,2,1,0:T(8,128)(2,1)S(1)}, u32[]{:S(2)}, u32[]{:S(2)}) collective-permute-start(bf16[2,2,256,256]{3,2,1,0:T(8,128)(2,1)} %collective-permute-done.1.refs_3_), channel_id=1, source_target_pairs={{0,32},{32,64},{64,96},{96,128},{128,160},{160,192},{192,224},{224... | collective-permute-start | bytes 1572872 | tf_op jit(solution)/shard_map/ppermute | solution.py:23
  65.4 15.1 %collective-permute-start.6 = (bf16[2,2,256,256]{3,2,1,0:T(8,128)(2,1)}, bf16[2,2,256,256]{3,2,1,0:T(8,128)(2,1)}, u32[]{:S(2)}, u32[]{:S(2)}) collective-permute-start(bf16[2,2,256,256]{3,2,1,0:T(8,128)(2,1)} %collective-permute-done.5.refs_4_), channel_id=1, source_target_pairs={{0,224},{32,0},{64,32},{96,64},{128,96},{160,128},{192,160},{224,1... | collective-permute-start | bytes 1572872 | tf_op jit(solution)/shard_map/ppermute | solution.py:23
  67.3 16.2 %collective-permute-start.12 = (bf16[512,1024]{1,0:T(8,128)(2,1)S(1)}, bf16[512,1024]{1,0:T(8,128)(2,1)}, u32[]{:S(2)}, u32[]{:S(2)}) collective-permute-start(bf16[512,1024]{1,0:T(8,128)(2,1)S(1)} %pad_maximum_fusion.refs_7_), channel_id=1, source_target_pairs={{0,4},{4,0},{1,5},{5,1},{2,6},{6,2},{3,7},{7,3},{8,12},{12,8},{9,1... | collective-permute-start | bytes 3145736 | tf_op jit(solution)/shard_map/ppermute | solution.py:23
  69.3 2.4 %copy-start.5 = (bf16[256,1024]{1,0:T(8,128)(2,1)}, bf16[256,1024]{1,0:T(8,128)(2,1)S(1)}, u32[]{:S(2)}) copy-start(bf16[256,1024]{1,0:T(8,128)(2,1)S(1)} %collective-permute-done.10.refs_10_) | copy-start | bytes 1572868
  69.3 20.2 %collective-permute-start.13 = (bf16[512,1024]{1,0:T(8,128)(2,1)S(1)}, bf16[512,1024]{1,0:T(8,128)(2,1)}, u32[]{:S(2)}, u32[]{:S(2)}) collective-permute-start(bf16[512,1024]{1,0:T(8,128)(2,1)S(1)} %collective-permute-done.8.refs_8_), channel_id=1, source_target_pairs={{0,4},{4,0},{1,5},{5,1},{2,6},{6,2},{3,7},{7,3},{8,12},{12,8},{9,1... | collective-permute-start | bytes 3145736 | tf_op jit(solution)/shard_map/ppermute | solution.py:23
  71.7 0.8 copy-start.7
  72.5 17.0 %collective-permute-start.14 = (bf16[512,1024]{1,0:T(8,128)(2,1)}, bf16[512,1024]{1,0:T(8,128)(2,1)}, u32[]{:S(2)}, u32[]{:S(2)}) collective-permute-start(bf16[512,1024]{1,0:T(8,128)(2,1)} %collective-permute-done.9.refs_9_), channel_id=1, source_target_pairs={{0,4},{4,0},{1,5},{5,1},{2,6},{6,2},{3,7},{7,3},{8,12},{12,8},{9,1... | collective-permute-start | bytes 3145736 | tf_op jit(solution)/shard_map/ppermute | solution.py:23
  75.2 11.1 %collective-permute-start.15 = (bf16[256,1024]{1,0:T(8,128)(2,1)}, bf16[256,1024]{1,0:T(8,128)(2,1)S(1)}, u32[]{:S(2)}, u32[]{:S(2)}) collective-permute-start(bf16[256,1024]{1,0:T(8,128)(2,1)} %copy-done.5), channel_id=1, source_target_pairs={{0,4},{4,0},{1,5},{5,1},{2,6},{6,2},{3,7},{7,3},{8,12},{12,8},{9,1... | collective-permute-start | bytes 1572872 | tf_op jit(solution)/shard_map/ppermute | solution.py:23
  80.5 9.0 %collective-permute-start.16 = (bf16[256,1024]{1,0:T(8,128)(2,1)}, bf16[256,1024]{1,0:T(8,128)(2,1)S(1)}, u32[]{:S(2)}, u32[]{:S(2)}) collective-permute-start(bf16[256,1024]{1,0:T(8,128)(2,1)} %copy-done.7), channel_id=1, source_target_pairs={{0,4},{4,0},{1,5},{5,1},{2,6},{6,2},{3,7},{7,3},{8,12},{12,8},{9,1... | collective-permute-start | bytes 1572872 | tf_op jit(solution)/shard_map/ppermute | solution.py:23
  83.5 17.7 %copy-start = (bf16[1,2,128,512]{3,2,1,0:T(8,128)(2,1)S(1)}, bf16[1,2,128,512]{3,2,1,0:T(8,128)(2,1)}, u32[]{:S(2)}) copy-start(bf16[1,2,128,512]{3,2,1,0:T(8,128)(2,1)} %queries.1) | copy-start | bytes 786436
  83.5 17.7 %collective-permute-start.3 = (bf16[2,256,256]{2,1,0:T(8,128)(2,1)S(1)}, bf16[2,256,256]{2,1,0:T(8,128)(2,1)S(1)}, u32[]{:S(2)}, u32[]{:S(2)}) collective-permute-start(bf16[2,256,256]{2,1,0:T(8,128)(2,1)S(1)} %slice_bitcast_fusion.1), channel_id=1, source_target_pairs={{0,32},{32,64},{64,96},{96,128},{128,160},{160,192},{192,224},{224... | collective-permute-start | bytes 786440 | tf_op jit(solution)/shard_map/ppermute | solution.py:23
  86.2 15.0 %collective-permute-start.7 = (bf16[2,256,256]{2,1,0:T(8,128)(2,1)S(1)}, bf16[2,256,256]{2,1,0:T(8,128)(2,1)S(1)}, u32[]{:S(2)}, u32[]{:S(2)}) collective-permute-start(bf16[2,256,256]{2,1,0:T(8,128)(2,1)S(1)} %slice_bitcast_fusion), channel_id=1, source_target_pairs={{0,224},{32,0},{64,32},{96,64},{128,96},{160,128},{192,160},{224,1... | collective-permute-start | bytes 786440 | tf_op jit(solution)/shard_map/ppermute | solution.py:23
  89.5 1.0 copy-start.2
  90.6 1.0 copy-start.4
  91.6 1.0 copy-start.6
  92.7 1.0 copy-start.8
  101.9 25.8 %copy-start.9 = (s32[2]{0:T(128)S(1)}, s32[2]{0:T(128)}, u32[]{:S(2)}) copy-start(s32[2]{0:T(128)} %lengths.1) | copy-start | bytes 28
  122.8 4.9 %collective-permute-start.17 = (bf16[4,320,512]{2,1,0:T(8,128)(2,1)S(1)}, bf16[4,320,512]{2,1,0:T(8,128)(2,1)S(1)}, u32[]{:S(2)}, u32[]{:S(2)}) collective-permute-start(bf16[4,320,512]{2,1,0:T(8,128)(2,1)S(1)} %all_to_all.10.mine), channel_id=1, source_target_pairs={{0,4},{4,0},{1,5},{5,1},{2,6},{6,2},{3,7},{7,3},{8,12},{12,8},{9,1... | collective-permute-start | bytes 3932168 | tf_op jit(solution)/shard_map/ppermute | solution.py:23

commit v4 on v3

--- a/solution.py
+++ b/solution.py
@@ -21,6 +21,10 @@
 def shift(array, axis, by):
     n = lax.axis_size(axis)
     return lax.ppermute(array, axis, [(i, (i + by) % n) for i in range(n)])
+
+
+def in_hbm(array):
+    return pltpu.with_memory_space_constraint(array, pltpu.HBM)
 
 
 def ring_of_eight(block):
@@ -207,6 +211,8 @@
     other = [shift(block, "c", 1) for block in own]
     enc, (first, second) = ring_of_eight(lax.all_gather(enc_states, "zh"))
 
+    enc[1], enc[2] = in_hbm(enc[1]), in_hbm(enc[2])
+    own = own[:3] + [in_hbm(own[3]), in_hbm(own[4])]
     partial, w_left = project_most(where, enc, own, other)
     both = project_rest(first, second, partial, w_left, queries)
     mine = lax.all_to_all(both, "x", 0, 0)

time: 143 us -> 139 us (0.972)
  local copies, waits for them, and re-layouts: 8.22 us -> 3.28 us
    unnamed x22 -> x14, local copies, waits for them, and re-layouts: 4.98 us -> 0.03 us
  transfers between devices with their start and end apart: 18 -> 18, of which waited for: 5 -> 5; matrix products, arithmetic and copies ran while one was open for 2% -> 2% of each run, Pallas kernels for 5% -> 6%
where the time goes in v4:
time: 139 us; the launch traced here: 138 us
  starting transfers between devices  53.8 us (39%)
  blocking collectives  49.8 us (36%)
  waiting for transfers between devices  17.5 us (13%)
  Pallas kernels  12.3 us (9%)
  local copies, waits for them, and re-layouts  3.28 us (2%)
  other arithmetic  1.43 us (1%)
    ppermute x18, starting transfers between devices, shift(): return lax.ppermute(array, axis, [(i, (i + by) % n) for i in range(n)])  53.8 us
    all_to_all x1, blocking collectives, on_device(): mine = lax.all_to_all(both, 'x', 0, 0)  20.9 us
    all_gather x1, blocking collectives, on_device(): enc, (first, second) = ring_of_eight(lax.all_gather(enc_states, 'zh'))  19.3 us
    ppermute x18, waiting for transfers between devices, shift(): return lax.ppermute(array, axis, [(i, (i + by) % n) for i in range(n)])  17.5 us
    all_to_all x1, blocking collectives, on_device(): mixed = lax.all_to_all(mixed, 'x', 0, 0)  9.64 us
    pallas_call x1, Pallas kernels, project_most(): pl.pallas_call(project_most_kernel, out_shape=(jax.ShapeDtypeStruct((2 *...  7.87 us
    pallas_call x1, Pallas kernels, attend(): pl.pallas_call(attend_kernel, out_shape=jax.ShapeDtypeStruct((4, 128, HEA...  3.68 us
  transfers between devices with their start and end apart: 18, of which 5 were waited for; matrix products, arithmetic and copies ran while one was open for 2% of the time, Pallas kernels for 6%

profile of v4, /device:TPU:152, one launch (start us, length us, event | category | flops | bytes accessed | tf_op | source)
XLA Modules:
  0.0 138.5 jit_solution(5881955360017080807)
XLA Ops:
  0.0 0.0 copy-start.2
  0.0 1.4 pad_maximum_fusion.refs_7_
  1.4 3.4 %collective-permute-start.8 = (bf16[512,1024]{1,0:T(8,128)(2,1)S(1)}, bf16[512,1024]{1,0:T(8,128)(2,1)S(1)}, u32[]{:S(2)}, u32[]{:S(2)}) collective-permute-start(bf16[512,1024]{1,0:T(8,128)(2,1)S(1)} %pad_maximum_fusion.refs_7_), channel_id=1, source_target_pairs={{0,8},{8,16},{16,24},{24,0},{1,9},{9,17},{17,25},{25,1},{2,10},{10... | collective-permute-start | bytes 3145736 | tf_op jit(solution)/shard_map/ppermute | solution.py:23
  4.8 3.7 %collective-permute-start.9 = (bf16[512,1024]{1,0:T(8,128)(2,1)S(1)}, bf16[512,1024]{1,0:T(8,128)(2,1)}, u32[]{:S(2)}, u32[]{:S(2)}) collective-permute-start(bf16[512,1024]{1,0:T(8,128)(2,1)S(1)} %pad_maximum_fusion.refs_7_), channel_id=1, source_target_pairs={{0,24},{8,0},{16,8},{24,16},{1,25},{9,1},{17,9},{25,17},{2,26},{10... | collective-permute-start | bytes 3145736 | tf_op jit(solution)/shard_map/ppermute | solution.py:23
  8.4 0.0 copy-done.2
  8.4 19.3 %all-gather = bf16[4,256,256]{2,1,0:T(8,128)(2,1)S(1)} all-gather(bf16[2,256,256]{2,1,0:T(8,128)(2,1)S(1)} %copy-done.2), channel_id=2, replica_groups=mesh['zh'=2,'y'=8,'x'=4,'c'=2,'mp'=4] {'zh'}, dimensions={0}, use_global_device_ids=true | all-gather | bytes 786432 | tf_op jit(solution)/shard_map/all_gather | solution.py:212
  27.8 4.7 %collective-permute-start = (bf16[2,2,256,256]{3,2,1,0:T(8,128)(2,1)S(1)}, bf16[2,2,256,256]{3,2,1,0:T(8,128)(2,1)S(1)}, u32[]{:S(2)}, u32[]{:S(2)}) collective-permute-start(bf16[2,2,256,256]{3,2,1,0:T(8,128)(2,1)S(1)} %bitcast.13), channel_id=1, source_target_pairs={{0,32},{32,64},{64,96},{96,128},{128,160},{160,192},{192,224},{224... | collective-permute-start | bytes 1572872 | tf_op jit(solution)/shard_map/ppermute | solution.py:23
  32.4 1.9 %collective-permute-start.4 = (bf16[2,2,256,256]{3,2,1,0:T(8,128)(2,1)S(1)}, bf16[2,2,256,256]{3,2,1,0:T(8,128)(2,1)S(1)}, u32[]{:S(2)}, u32[]{:S(2)}) collective-permute-start(bf16[2,2,256,256]{3,2,1,0:T(8,128)(2,1)S(1)} %bitcast.14), channel_id=1, source_target_pairs={{0,224},{32,0},{64,32},{96,64},{128,96},{160,128},{192,160},{224,1... | collective-permute-start | bytes 1572872 | tf_op jit(solution)/shard_map/ppermute | solution.py:23
  34.4 9.3 %collective-permute-done.refs_1_ = bf16[2,2,256,256]{3,2,1,0:T(8,128)(2,1)S(1)} collective-permute-done((bf16[2,2,256,256]{3,2,1,0:T(8,128)(2,1)S(1)}, bf16[2,2,256,256]{3,2,1,0:T(8,128)(2,1)S(1)}, u32[]{:S(2)}, u32[]{:S(2)}) %collective-permute-start) | collective-permute-done | bytes 524320 | tf_op jit(solution)/shard_map/ppermute | solution.py:23
  43.7 0.0 copy-start.3
  43.7 5.6 %collective-permute-start.1 = (bf16[2,2,256,256]{3,2,1,0:T(8,128)(2,1)S(1)}, bf16[2,2,256,256]{3,2,1,0:T(8,128)(2,1)}, u32[]{:S(2)}, u32[]{:S(2)}) collective-permute-start(bf16[2,2,256,256]{3,2,1,0:T(8,128)(2,1)S(1)} %collective-permute-done.refs_1_), channel_id=1, source_target_pairs={{0,32},{32,64},{64,96},{96,128},{128,160},{160,192},{192,224},{224... | collective-permute-start | bytes 1572872 | tf_op jit(solution)/shard_map/ppermute | solution.py:23
  49.3 0.0 collective-permute-done.4.refs_2_
  49.3 0.0 copy-start.4
  49.3 1.9 %collective-permute-start.5 = (bf16[2,2,256,256]{3,2,1,0:T(8,128)(2,1)S(1)}, bf16[2,2,256,256]{3,2,1,0:T(8,128)(2,1)}, u32[]{:S(2)}, u32[]{:S(2)}) collective-permute-start(bf16[2,2,256,256]{3,2,1,0:T(8,128)(2,1)S(1)} %collective-permute-done.4.refs_2_), channel_id=1, source_target_pairs={{0,224},{32,0},{64,32},{96,64},{128,96},{160,128},{192,160},{224,1... | collective-permute-start | bytes 1572872 | tf_op jit(solution)/shard_map/ppermute | solution.py:23
  51.2 0.0 collective-permute-done.8.refs_8_
  51.3 2.2 %collective-permute-start.10 = (bf16[256,1024]{1,0:T(8,128)(2,1)S(1)}, bf16[256,1024]{1,0:T(8,128)(2,1)S(1)}, u32[]{:S(2)}, u32[]{:S(2)}) collective-permute-start(bf16[256,1024]{1,0:T(8,128)(2,1)S(1)} %slice.18), channel_id=1, source_target_pairs={{0,8},{8,16},{16,24},{24,0},{1,9},{9,17},{17,25},{25,1},{2,10},{10... | collective-permute-start | bytes 1572872 | tf_op jit(solution)/shard_map/ppermute | solution.py:23
  53.5 0.0 collective-permute-done.9.refs_9_
  53.5 1.1 slice.19
  54.6 4.9 %collective-permute-start.11 = (bf16[256,1024]{1,0:T(8,128)(2,1)S(1)}, bf16[256,1024]{1,0:T(8,128)(2,1)S(1)}, u32[]{:S(2)}, u32[]{:S(2)}) collective-permute-start(bf16[256,1024]{1,0:T(8,128)(2,1)S(1)} %slice.19), channel_id=1, source_target_pairs={{0,24},{8,0},{16,8},{24,16},{1,25},{9,1},{17,9},{25,17},{2,26},{10... | collective-permute-start | bytes 1572872 | tf_op jit(solution)/shard_map/ppermute | solution.py:23
  59.5 0.2 collective-permute-done.1.refs_3_
  59.7 5.7 %collective-permute-start.2 = (bf16[2,2,256,256]{3,2,1,0:T(8,128)(2,1)}, bf16[2,2,256,256]{3,2,1,0:T(8,128)(2,1)S(1)}, u32[]{:S(2)}, u32[]{:S(2)}) collective-permute-start(bf16[2,2,256,256]{3,2,1,0:T(8,128)(2,1)} %collective-permute-done.1.refs_3_), channel_id=1, source_target_pairs={{0,32},{32,64},{64,96},{96,128},{128,160},{160,192},{192,224},{224... | collective-permute-start | bytes 1572872 | tf_op jit(solution)/shard_map/ppermute | solution.py:23
  65.4 0.0 collective-permute-done.5.refs_4_
  65.4 1.9 %collective-permute-start.6 = (bf16[2,2,256,256]{3,2,1,0:T(8,128)(2,1)}, bf16[2,2,256,256]{3,2,1,0:T(8,128)(2,1)}, u32[]{:S(2)}, u32[]{:S(2)}) collective-permute-start(bf16[2,2,256,256]{3,2,1,0:T(8,128)(2,1)} %collective-permute-done.5.refs_4_), channel_id=1, source_target_pairs={{0,224},{32,0},{64,32},{96,64},{128,96},{160,128},{192,160},{224,1... | collective-permute-start | bytes 1572872 | tf_op jit(solution)/shard_map/ppermute | solution.py:23
  67.3 1.9 %collective-permute-start.12 = (bf16[512,1024]{1,0:T(8,128)(2,1)S(1)}, bf16[512,1024]{1,0:T(8,128)(2,1)}, u32[]{:S(2)}, u32[]{:S(2)}) collective-permute-start(bf16[512,1024]{1,0:T(8,128)(2,1)S(1)} %pad_maximum_fusion.refs_7_), channel_id=1, source_target_pairs={{0,4},{4,0},{1,5},{5,1},{2,6},{6,2},{3,7},{7,3},{8,12},{12,8},{9,1... | collective-permute-start | bytes 3145736 | tf_op jit(solution)/shard_map/ppermute | solution.py:23
  69.2 0.0 collective-permute-done.10.refs_10_
  69.3 0.0 copy-start.5
  69.3 2.4 %collective-permute-start.13 = (bf16[512,1024]{1,0:T(8,128)(2,1)S(1)}, bf16[512,1024]{1,0:T(8,128)(2,1)}, u32[]{:S(2)}, u32[]{:S(2)}) collective-permute-start(bf16[512,1024]{1,0:T(8,128)(2,1)S(1)} %collective-permute-done.8.refs_8_), channel_id=1, source_target_pairs={{0,4},{4,0},{1,5},{5,1},{2,6},{6,2},{3,7},{7,3},{8,12},{12,8},{9,1... | collective-permute-start | bytes 3145736 | tf_op jit(solution)/shard_map/ppermute | solution.py:23
  71.7 0.0 collective-permute-done.11.refs_11_
  71.7 0.0 copy-done.3
  71.7 0.0 copy-start.6
  71.7 1.9 %collective-permute-start.14 = (bf16[512,1024]{1,0:T(8,128)(2,1)}, bf16[512,1024]{1,0:T(8,128)(2,1)}, u32[]{:S(2)}, u32[]{:S(2)}) collective-permute-start(bf16[512,1024]{1,0:T(8,128)(2,1)} %collective-permute-done.9.refs_9_), channel_id=1, source_target_pairs={{0,4},{4,0},{1,5},{5,1},{2,6},{6,2},{3,7},{7,3},{8,12},{12,8},{9,1... | collective-permute-start | bytes 3145736 | tf_op jit(solution)/shard_map/ppermute | solution.py:23
  73.6 0.0 copy-done.4
  73.6 0.0 copy-done.5
  73.7 0.0 copy-done.6
  73.7 1.5 %collective-permute-done.2.refs_5_ = bf16[2,2,256,256]{3,2,1,0:T(8,128)(2,1)S(1)} collective-permute-done((bf16[2,2,256,256]{3,2,1,0:T(8,128)(2,1)}, bf16[2,2,256,256]{3,2,1,0:T(8,128)(2,1)S(1)}, u32[]{:S(2)}, u32[]{:S(2)}) %collective-permute-start.2) | collective-permute-done | bytes 524320 | tf_op jit(solution)/shard_map/ppermute | solution.py:23
  75.2 1.9 %collective-permute-start.15 = (bf16[256,1024]{1,0:T(8,128)(2,1)}, bf16[256,1024]{1,0:T(8,128)(2,1)S(1)}, u32[]{:S(2)}, u32[]{:S(2)}) collective-permute-start(bf16[256,1024]{1,0:T(8,128)(2,1)} %copy-done.5), channel_id=1, source_target_pairs={{0,4},{4,0},{1,5},{5,1},{2,6},{6,2},{3,7},{7,3},{8,12},{12,8},{9,1... | collective-permute-start | bytes 1572872 | tf_op jit(solution)/shard_map/ppermute | solution.py:23
  77.1 3.4 %collective-permute-done.6.refs_6_ = bf16[2,2,256,256]{3,2,1,0:T(8,128)(2,1)} collective-permute-done((bf16[2,2,256,256]{3,2,1,0:T(8,128)(2,1)}, bf16[2,2,256,256]{3,2,1,0:T(8,128)(2,1)}, u32[]{:S(2)}, u32[]{:S(2)}) %collective-permute-start.6) | collective-permute-done | bytes 524320 | tf_op jit(solution)/shard_map/ppermute | solution.py:23
  80.5 1.9 %collective-permute-start.16 = (bf16[256,1024]{1,0:T(8,128)(2,1)}, bf16[256,1024]{1,0:T(8,128)(2,1)S(1)}, u32[]{:S(2)}, u32[]{:S(2)}) collective-permute-start(bf16[256,1024]{1,0:T(8,128)(2,1)} %copy-done.6), channel_id=1, source_target_pairs={{0,4},{4,0},{1,5},{5,1},{2,6},{6,2},{3,7},{7,3},{8,12},{12,8},{9,1... | collective-permute-start | bytes 1572872 | tf_op jit(solution)/shard_map/ppermute | solution.py:23
  82.4 0.1 pad_add_fusion.where
  82.5 1.0 slice_bitcast_fusion
  83.5 0.0 copy-start
  83.5 0.0 collective-permute-done.12.refs_12_
  83.5 2.7 %collective-permute-start.3 = (bf16[2,256,256]{2,1,0:T(8,128)(2,1)S(1)}, bf16[2,256,256]{2,1,0:T(8,128)(2,1)S(1)}, u32[]{:S(2)}, u32[]{:S(2)}) collective-permute-start(bf16[2,256,256]{2,1,0:T(8,128)(2,1)S(1)} %slice_bitcast_fusion.1), channel_id=1, source_target_pairs={{0,32},{32,64},{64,96},{96,128},{128,160},{160,192},{192,224},{224... | collective-permute-start | bytes 786440 | tf_op jit(solution)/shard_map/ppermute | solution.py:23
  86.2 0.0 collective-permute-done.15.refs_15_
  86.2 3.3 %collective-permute-start.7 = (bf16[2,256,256]{2,1,0:T(8,128)(2,1)S(1)}, bf16[2,256,256]{2,1,0:T(8,128)(2,1)S(1)}, u32[]{:S(2)}, u32[]{:S(2)}) collective-permute-start(bf16[2,256,256]{2,1,0:T(8,128)(2,1)S(1)} %slice_bitcast_fusion), channel_id=1, source_target_pairs={{0,224},{32,0},{64,32},{96,64},{128,96},{160,128},{192,160},{224,1... | collective-permute-start | bytes 786440 | tf_op jit(solution)/shard_map/ppermute | solution.py:23
  89.5 0.0 collective-permute-done.16.refs_16_
  89.5 0.0 collective-permute-done.13.refs_13_
  89.5 0.0 collective-permute-done.14.refs_14_
  89.5 7.9 %project_most.1 = (f32[512,1024]{1,0:T(8,128)S(1)}, bf16[2,256,1024]{2,1,0:T(8,128)(2,1)S(1)}) custom-call(s32[3]{0:T(128)S(1)} %pad_add_fusion.where, bf16[2,2,256,256]{3,2,1,0:T(8,128)(2,1)S(1)} %bitcast.15, bf16[2,2,256,256]{3,2,1,0:T(8,128)(2,1)} %copy-done.3, bf16[2,2,256,256]{3,2,1,0:T(8,128)(2,1)} %copy-done.4, ...), custom_call_target="tpu_custom_call" | custom-call | flops 3758096384 | bytes 14680064 | tf_op jit(solution)/shard_map/project_most/pallas_call | solution.py:113
  97.4 0.0 collective-permute-done.3.first
  97.4 0.0 collective-permute-done.7.second
  97.4 0.0 copy-done
  97.4 0.7 project_rest.1
  98.2 0.0 copy-start.1
  98.2 20.9 %all_to_all.10.mine = bf16[4,320,512]{2,1,0:T(8,128)(2,1)S(1)} all-to-all(bf16[4,320,512]{2,1,0:T(8,128)(2,1)S(1)} %project_rest.1), channel_id=1, replica_groups=mesh['zh'=2,'y'=8,'x'=4,'c'=2,'mp'=4] {'x'}, dimensions={0} | all-to-all | bytes 2621440 | tf_op jit(solution)/shard_map/all_to_all | solution.py:218
  119.1 1.9 %collective-permute-start.17 = (bf16[4,320,512]{2,1,0:T(8,128)(2,1)S(1)}, bf16[4,320,512]{2,1,0:T(8,128)(2,1)S(1)}, u32[]{:S(2)}, u32[]{:S(2)}) collective-permute-start(bf16[4,320,512]{2,1,0:T(8,128)(2,1)S(1)} %all_to_all.10.mine), channel_id=1, source_target_pairs={{0,4},{4,0},{1,5},{5,1},{2,6},{6,2},{3,7},{7,3},{8,12},{12,8},{9,1... | collective-permute-start | bytes 3932168 | tf_op jit(solution)/shard_map/ppermute | solution.py:23
  121.0 3.0 %collective-permute-done.17.theirs = bf16[4,320,512]{2,1,0:T(8,128)(2,1)S(1)} collective-permute-done((bf16[4,320,512]{2,1,0:T(8,128)(2,1)S(1)}, bf16[4,320,512]{2,1,0:T(8,128)(2,1)S(1)}, u32[]{:S(2)}, u32[]{:S(2)}) %collective-permute-start.17) | collective-permute-done | bytes 1310752 | tf_op jit(solution)/shard_map/ppermute | solution.py:23
  124.0 0.0 copy-done.1
  124.0 3.7 %attend.1 = bf16[4,128,256]{2,1,0:T(8,128)(2,1)S(1)} custom-call(s32[3]{0:T(128)S(1)} %pad_add_fusion.where, s32[2]{0:T(128)S(1)} %copy-done.1, bf16[4,320,512]{2,1,0:T(8,128)(2,1)S(1)} %all_to_all.10.mine, bf16[4,320,512]{2,1,0:T(8,128)(2,1)S(1)} %collective-permute-done.17.theirs), custom_call_target="tpu_custom_call" | custom-call | flops 1073741824 | bytes 4194304 | tf_op jit(solution)/shard_map/attend/pallas_call | solution.py:194
  127.7 9.6 %all_to_all.11 = bf16[4,128,256]{2,1,0:T(8,128)(2,1)S(1)} all-to-all(bf16[4,128,256]{2,1,0:T(8,128)(2,1)S(1)} %attend.1), channel_id=1, replica_groups=mesh['zh'=2,'y'=8,'x'=4,'c'=2,'mp'=4] {'x'}, dimensions={0} | all-to-all | bytes 524288 | tf_op jit(solution)/shard_map/all_to_all | solution.py:221
  137.3 0.3 copy.7
  137.6 0.9 broadcast_in_dim_reshape.3
  (2 shorter events, 0.1 us)
Async XLA Ops:
  0.0 8.4 %copy-start.2 = (bf16[2,256,256]{2,1,0:T(8,128)(2,1)S(1)}, bf16[2,256,256]{2,1,0:T(8,128)(2,1)}, u32[]{:S(2)}) copy-start(bf16[2,256,256]{2,1,0:T(8,128)(2,1)} %param.6) | copy-start | bytes 786436
  1.4 49.9 %collective-permute-start.8 = (bf16[512,1024]{1,0:T(8,128)(2,1)S(1)}, bf16[512,1024]{1,0:T(8,128)(2,1)S(1)}, u32[]{:S(2)}, u32[]{:S(2)}) collective-permute-start(bf16[512,1024]{1,0:T(8,128)(2,1)S(1)} %pad_maximum_fusion.refs_7_), channel_id=1, source_target_pairs={{0,8},{8,16},{16,24},{24,0},{1,9},{9,17},{17,25},{25,1},{2,10},{10... | collective-permute-start | bytes 3145736 | tf_op jit(solution)/shard_map/ppermute | solution.py:23
  4.8 48.7 %collective-permute-start.9 = (bf16[512,1024]{1,0:T(8,128)(2,1)S(1)}, bf16[512,1024]{1,0:T(8,128)(2,1)}, u32[]{:S(2)}, u32[]{:S(2)}) collective-permute-start(bf16[512,1024]{1,0:T(8,128)(2,1)S(1)} %pad_maximum_fusion.refs_7_), channel_id=1, source_target_pairs={{0,24},{8,0},{16,8},{24,16},{1,25},{9,1},{17,9},{25,17},{2,26},{10... | collective-permute-start | bytes 3145736 | tf_op jit(solution)/shard_map/ppermute | solution.py:23
  27.8 15.9 %collective-permute-start = (bf16[2,2,256,256]{3,2,1,0:T(8,128)(2,1)S(1)}, bf16[2,2,256,256]{3,2,1,0:T(8,128)(2,1)S(1)}, u32[]{:S(2)}, u32[]{:S(2)}) collective-permute-start(bf16[2,2,256,256]{3,2,1,0:T(8,128)(2,1)S(1)} %bitcast.13), channel_id=1, source_target_pairs={{0,32},{32,64},{64,96},{96,128},{128,160},{160,192},{192,224},{224... | collective-permute-start | bytes 1572872 | tf_op jit(solution)/shard_map/ppermute | solution.py:23
  32.4 16.8 %collective-permute-start.4 = (bf16[2,2,256,256]{3,2,1,0:T(8,128)(2,1)S(1)}, bf16[2,2,256,256]{3,2,1,0:T(8,128)(2,1)S(1)}, u32[]{:S(2)}, u32[]{:S(2)}) collective-permute-start(bf16[2,2,256,256]{3,2,1,0:T(8,128)(2,1)S(1)} %bitcast.14), channel_id=1, source_target_pairs={{0,224},{32,0},{64,32},{96,64},{128,96},{160,128},{192,160},{224,1... | collective-permute-start | bytes 1572872 | tf_op jit(solution)/shard_map/ppermute | solution.py:23
  43.7 28.0 %copy-start.3 = (bf16[2,2,256,256]{3,2,1,0:T(8,128)(2,1)}, bf16[2,2,256,256]{3,2,1,0:T(8,128)(2,1)S(1)}, u32[]{:S(2)}) copy-start(bf16[2,2,256,256]{3,2,1,0:T(8,128)(2,1)S(1)} %collective-permute-done.refs_1_) | copy-start | bytes 1572868
  43.7 16.0 %collective-permute-start.1 = (bf16[2,2,256,256]{3,2,1,0:T(8,128)(2,1)S(1)}, bf16[2,2,256,256]{3,2,1,0:T(8,128)(2,1)}, u32[]{:S(2)}, u32[]{:S(2)}) collective-permute-start(bf16[2,2,256,256]{3,2,1,0:T(8,128)(2,1)S(1)} %collective-permute-done.refs_1_), channel_id=1, source_target_pairs={{0,32},{32,64},{64,96},{96,128},{128,160},{160,192},{192,224},{224... | collective-permute-start | bytes 1572872 | tf_op jit(solution)/shard_map/ppermute | solution.py:23
  49.3 24.3 %copy-start.4 = (bf16[2,2,256,256]{3,2,1,0:T(8,128)(2,1)}, bf16[2,2,256,256]{3,2,1,0:T(8,128)(2,1)S(1)}, u32[]{:S(2)}) copy-start(bf16[2,2,256,256]{3,2,1,0:T(8,128)(2,1)S(1)} %collective-permute-done.4.refs_2_) | copy-start | bytes 1572868
  49.3 16.1 %collective-permute-start.5 = (bf16[2,2,256,256]{3,2,1,0:T(8,128)(2,1)S(1)}, bf16[2,2,256,256]{3,2,1,0:T(8,128)(2,1)}, u32[]{:S(2)}, u32[]{:S(2)}) collective-permute-start(bf16[2,2,256,256]{3,2,1,0:T(8,128)(2,1)S(1)} %collective-permute-done.4.refs_2_), channel_id=1, source_target_pairs={{0,224},{32,0},{64,32},{96,64},{128,96},{160,128},{192,160},{224,1... | collective-permute-start | bytes 1572872 | tf_op jit(solution)/shard_map/ppermute | solution.py:23
  51.3 18.0 %collective-permute-start.10 = (bf16[256,1024]{1,0:T(8,128)(2,1)S(1)}, bf16[256,1024]{1,0:T(8,128)(2,1)S(1)}, u32[]{:S(2)}, u32[]{:S(2)}) collective-permute-start(bf16[256,1024]{1,0:T(8,128)(2,1)S(1)} %slice.18), channel_id=1, source_target_pairs={{0,8},{8,16},{16,24},{24,0},{1,9},{9,17},{17,25},{25,1},{2,10},{10... | collective-permute-start | bytes 1572872 | tf_op jit(solution)/shard_map/ppermute | solution.py:23
  54.6 17.1 %collective-permute-start.11 = (bf16[256,1024]{1,0:T(8,128)(2,1)S(1)}, bf16[256,1024]{1,0:T(8,128)(2,1)S(1)}, u32[]{:S(2)}, u32[]{:S(2)}) collective-permute-start(bf16[256,1024]{1,0:T(8,128)(2,1)S(1)} %slice.19), channel_id=1, source_target_pairs={{0,24},{8,0},{16,8},{24,16},{1,25},{9,1},{17,9},{25,17},{2,26},{10... | collective-permute-start | bytes 1572872 | tf_op jit(solution)/shard_map/ppermute | solution.py:23
  59.7 15.5 %collective-permute-start.2 = (bf16[2,2,256,256]{3,2,1,0:T(8,128)(2,1)}, bf16[2,2,256,256]{3,2,1,0:T(8,128)(2,1)S(1)}, u32[]{:S(2)}, u32[]{:S(2)}) collective-permute-start(bf16[2,2,256,256]{3,2,1,0:T(8,128)(2,1)} %collective-permute-done.1.refs_3_), channel_id=1, source_target_pairs={{0,32},{32,64},{64,96},{96,128},{128,160},{160,192},{192,224},{224... | collective-permute-start | bytes 1572872 | tf_op jit(solution)/shard_map/ppermute | solution.py:23
  65.4 15.1 %collective-permute-start.6 = (bf16[2,2,256,256]{3,2,1,0:T(8,128)(2,1)}, bf16[2,2,256,256]{3,2,1,0:T(8,128)(2,1)}, u32[]{:S(2)}, u32[]{:S(2)}) collective-permute-start(bf16[2,2,256,256]{3,2,1,0:T(8,128)(2,1)} %collective-permute-done.5.refs_4_), channel_id=1, source_target_pairs={{0,224},{32,0},{64,32},{96,64},{128,96},{160,128},{192,160},{224,1... | collective-permute-start | bytes 1572872 | tf_op jit(solution)/shard_map/ppermute | solution.py:23
  67.3 16.2 %collective-permute-start.12 = (bf16[512,1024]{1,0:T(8,128)(2,1)S(1)}, bf16[512,1024]{1,0:T(8,128)(2,1)}, u32[]{:S(2)}, u32[]{:S(2)}) collective-permute-start(bf16[512,1024]{1,0:T(8,128)(2,1)S(1)} %pad_maximum_fusion.refs_7_), channel_id=1, source_target_pairs={{0,4},{4,0},{1,5},{5,1},{2,6},{6,2},{3,7},{7,3},{8,12},{12,8},{9,1... | collective-permute-start | bytes 3145736 | tf_op jit(solution)/shard_map/ppermute | solution.py:23
  69.3 4.4 %copy-start.5 = (bf16[256,1024]{1,0:T(8,128)(2,1)}, bf16[256,1024]{1,0:T(8,128)(2,1)S(1)}, u32[]{:S(2)}) copy-start(bf16[256,1024]{1,0:T(8,128)(2,1)S(1)} %collective-permute-done.10.refs_10_) | copy-start | bytes 1572868
  69.3 20.3 %collective-permute-start.13 = (bf16[512,1024]{1,0:T(8,128)(2,1)S(1)}, bf16[512,1024]{1,0:T(8,128)(2,1)}, u32[]{:S(2)}, u32[]{:S(2)}) collective-permute-start(bf16[512,1024]{1,0:T(8,128)(2,1)S(1)} %collective-permute-done.8.refs_8_), channel_id=1, source_target_pairs={{0,4},{4,0},{1,5},{5,1},{2,6},{6,2},{3,7},{7,3},{8,12},{12,8},{9,1... | collective-permute-start | bytes 3145736 | tf_op jit(solution)/shard_map/ppermute | solution.py:23
  71.7 2.0 %copy-start.6 = (bf16[256,1024]{1,0:T(8,128)(2,1)}, bf16[256,1024]{1,0:T(8,128)(2,1)S(1)}, u32[]{:S(2)}) copy-start(bf16[256,1024]{1,0:T(8,128)(2,1)S(1)} %collective-permute-done.11.refs_11_) | copy-start | bytes 1572868
  71.7 17.8 %collective-permute-start.14 = (bf16[512,1024]{1,0:T(8,128)(2,1)}, bf16[512,1024]{1,0:T(8,128)(2,1)}, u32[]{:S(2)}, u32[]{:S(2)}) collective-permute-start(bf16[512,1024]{1,0:T(8,128)(2,1)} %collective-permute-done.9.refs_9_), channel_id=1, source_target_pairs={{0,4},{4,0},{1,5},{5,1},{2,6},{6,2},{3,7},{7,3},{8,12},{12,8},{9,1... | collective-permute-start | bytes 3145736 | tf_op jit(solution)/shard_map/ppermute | solution.py:23
  75.2 11.1 %collective-permute-start.15 = (bf16[256,1024]{1,0:T(8,128)(2,1)}, bf16[256,1024]{1,0:T(8,128)(2,1)S(1)}, u32[]{:S(2)}, u32[]{:S(2)}) collective-permute-start(bf16[256,1024]{1,0:T(8,128)(2,1)} %copy-done.5), channel_id=1, source_target_pairs={{0,4},{4,0},{1,5},{5,1},{2,6},{6,2},{3,7},{7,3},{8,12},{12,8},{9,1... | collective-permute-start | bytes 1572872 | tf_op jit(solution)/shard_map/ppermute | solution.py:23
  80.5 9.0 %collective-permute-start.16 = (bf16[256,1024]{1,0:T(8,128)(2,1)}, bf16[256,1024]{1,0:T(8,128)(2,1)S(1)}, u32[]{:S(2)}, u32[]{:S(2)}) collective-permute-start(bf16[256,1024]{1,0:T(8,128)(2,1)} %copy-done.6), channel_id=1, source_target_pairs={{0,4},{4,0},{1,5},{5,1},{2,6},{6,2},{3,7},{7,3},{8,12},{12,8},{9,1... | collective-permute-start | bytes 1572872 | tf_op jit(solution)/shard_map/ppermute | solution.py:23
  83.5 14.0 %copy-start = (bf16[1,2,128,512]{3,2,1,0:T(8,128)(2,1)S(1)}, bf16[1,2,128,512]{3,2,1,0:T(8,128)(2,1)}, u32[]{:S(2)}) copy-start(bf16[1,2,128,512]{3,2,1,0:T(8,128)(2,1)} %queries.1) | copy-start | bytes 786436
  83.5 13.9 %collective-permute-start.3 = (bf16[2,256,256]{2,1,0:T(8,128)(2,1)S(1)}, bf16[2,256,256]{2,1,0:T(8,128)(2,1)S(1)}, u32[]{:S(2)}, u32[]{:S(2)}) collective-permute-start(bf16[2,256,256]{2,1,0:T(8,128)(2,1)S(1)} %slice_bitcast_fusion.1), channel_id=1, source_target_pairs={{0,32},{32,64},{64,96},{96,128},{128,160},{160,192},{192,224},{224... | collective-permute-start | bytes 786440 | tf_op jit(solution)/shard_map/ppermute | solution.py:23
  86.2 11.2 %collective-permute-start.7 = (bf16[2,256,256]{2,1,0:T(8,128)(2,1)S(1)}, bf16[2,256,256]{2,1,0:T(8,128)(2,1)S(1)}, u32[]{:S(2)}, u32[]{:S(2)}) collective-permute-start(bf16[2,256,256]{2,1,0:T(8,128)(2,1)S(1)} %slice_bitcast_fusion), channel_id=1, source_target_pairs={{0,224},{32,0},{64,32},{96,64},{128,96},{160,128},{192,160},{224,1... | collective-permute-start | bytes 786440 | tf_op jit(solution)/shard_map/ppermute | solution.py:23
  98.2 25.8 %copy-start.1 = (s32[2]{0:T(128)S(1)}, s32[2]{0:T(128)}, u32[]{:S(2)}) copy-start(s32[2]{0:T(128)} %lengths.1) | copy-start | bytes 28
  119.1 4.9 %collective-permute-start.17 = (bf16[4,320,512]{2,1,0:T(8,128)(2,1)S(1)}, bf16[4,320,512]{2,1,0:T(8,128)(2,1)S(1)}, u32[]{:S(2)}, u32[]{:S(2)}) collective-permute-start(bf16[4,320,512]{2,1,0:T(8,128)(2,1)S(1)} %all_to_all.10.mine), channel_id=1, source_target_pairs={{0,4},{4,0},{1,5},{5,1},{2,6},{6,2},{3,7},{7,3},{8,12},{12,8},{9,1... | collective-permute-start | bytes 3932168 | tf_op jit(solution)/shard_map/ppermute | solution.py:23

commit v5 on v4

--- a/solution.py
+++ b/solution.py
@@ -163,45 +163,69 @@
     )(first, second, partial, w_left, queries)
 
 
-def attend_kernel(where, lengths, mine, theirs, out):
-    x, core = where[1], where[2]
-    length = lengths[x // 2]
-    scale = 1.0 / math.sqrt(HEAD_DIM)
-    steps = [(ref, of, p) for of, ref in ((core, mine), (1 - core, theirs)) for p in range(4)]
+def attend_half(where, lengths, ref, of, q):
+    length = lengths[where[1] // 2]
+    scores = []
+    for p in range(4):
+        s = lax.dot_general(
+            q, ref[p, :ROWS, :HEAD_DIM], (((1,), (1,)), ((), ())), preferred_element_type=jnp.float32
+        )
+        place = (p * 2 + of) * ROWS + lax.broadcasted_iota(jnp.int32, (1, ROWS), 1)
+        scores.append(jnp.where(place < length, s * (1.0 / math.sqrt(HEAD_DIM)), -jnp.inf))
+    top = jnp.maximum(jnp.maximum(scores[0], scores[1]), jnp.maximum(scores[2], scores[3]))
+    top = jnp.max(top, axis=1, keepdims=True)
+    total, summed = None, None
+    for p, s in enumerate(scores):
+        w = jnp.exp(s - top)
+        total = w if total is None else total + w
+        o = jnp.dot(w.astype(jnp.bfloat16), ref[p, :ROWS, HEAD_DIM:], preferred_element_type=jnp.float32)
+        summed = o if summed is None else summed + o
+    return top, jnp.sum(total, axis=1, keepdims=True), summed
+
+
+def query_of(mine, chunk):
+    return jnp.concatenate([mine[chunk, ROWS:, :HEAD_DIM], mine[chunk, ROWS:, HEAD_DIM:]], axis=0)
+
+
+def attend_mine_kernel(where, lengths, mine, top, total, summed):
     for chunk in range(4):
-        q = jnp.concatenate([mine[chunk, ROWS:, :HEAD_DIM], mine[chunk, ROWS:, HEAD_DIM:]], axis=0)
-        scores = []
-        for ref, of, p in steps:
-            keys = ref[p, :ROWS, :HEAD_DIM]
-            s = lax.dot_general(q, keys, (((1,), (1,)), ((), ())), preferred_element_type=jnp.float32)
-            place = (p * 2 + of) * ROWS + lax.broadcasted_iota(jnp.int32, (1, ROWS), 1)
-            scores.append(jnp.where(place < length, s * scale, -jnp.inf))
-        top = scores[0]
-        for s in scores[1:]:
-            top = jnp.maximum(top, s)
-        top = jnp.max(top, axis=1, keepdims=True)
-        total, summed = None, None
-        for s, (ref, _, p) in zip(scores, steps):
-            w = jnp.exp(s - top)
-            total = w if total is None else total + w
-            o = jnp.dot(w.astype(jnp.bfloat16), ref[p, :ROWS, HEAD_DIM:], preferred_element_type=jnp.float32)
-            summed = o if summed is None else summed + o
-        total = jnp.sum(total, axis=1, keepdims=True)
-        out[chunk] = (summed / total).astype(jnp.bfloat16)
+        t, n, o = attend_half(where, lengths, mine, where[2], query_of(mine, chunk))
+        top[chunk] = jnp.broadcast_to(t, (128, 128))
+        total[chunk] = jnp.broadcast_to(n, (128, 128))
+        summed[chunk] = o
+
+
+def attend_theirs_kernel(where, lengths, mine, theirs, top, total, summed, out):
+    for chunk in range(4):
+        t, n, o = attend_half(where, lengths, theirs, 1 - where[2], query_of(mine, chunk))
+        before = top[chunk][:, :1]
+        both = jnp.maximum(before, t)
+        old, new = jnp.exp(before - both), jnp.exp(t - both)
+        out[chunk] = ((old * summed[chunk] + new * o) / (old * total[chunk][:, :1] + new * n)).astype(jnp.bfloat16)
 
 
 def attend(where, lengths, mine, theirs):
+    cost = pl.CostEstimate(flops=2 * 512 * 2048 * 256, bytes_accessed=2 * 2**20, transcendentals=512 * 1024)
+    params = pltpu.CompilerParams(vmem_limit_bytes=32 * 2**20)
+    stat = jax.ShapeDtypeStruct((4, 128, 128), jnp.float32)
+    state = pl.pallas_call(
+        attend_mine_kernel,
+        out_shape=(stat, stat, jax.ShapeDtypeStruct((4, 128, HEAD_DIM), jnp.float32)),
+        in_specs=[SMEM, SMEM, VMEM],
+        out_specs=(VMEM, VMEM, VMEM),
+        compiler_params=params,
+        cost_estimate=cost,
+        name="attend_mine",
+    )(where, lengths, mine)
     return pl.pallas_call(
-        attend_kernel,
+        attend_theirs_kernel,
         out_shape=jax.ShapeDtypeStruct((4, 128, HEAD_DIM), jnp.bfloat16),
-        in_specs=[SMEM, SMEM, VMEM, VMEM],
+        in_specs=[SMEM, SMEM] + [VMEM] * 5,
         out_specs=VMEM,
-        compiler_params=pltpu.CompilerParams(vmem_limit_bytes=32 * 2**20),
-        cost_estimate=pl.CostEstimate(
-            flops=4 * 512 * 2048 * 256, bytes_accessed=4 * 2**20, transcendentals=512 * 2048
-        ),
-        name="attend",
-    )(where, lengths, mine, theirs)
+        compiler_params=params,
+        cost_estimate=cost,
+        name="attend_theirs",
+    )(where, lengths, mine, theirs, *state)
 
 
 def on_device(queries, enc_states, key_weight, value_weight, enc_lengths):

time: 139 us -> 138 us (level)
  waiting for transfers between devices: 17.5 us -> 15 us
  Pallas kernels: 12.3 us -> 13.7 us
    ppermute x18, waiting for transfers between devices: 17.5 us -> 15 us  [shift(): return lax.ppermute(array, axis, [(i, (i + by) % n) for i in range(n)])]
    pallas_call x1 -> x2, Pallas kernels: 3.68 us -> 5.12 us  [the longest x1 2.72 us: attend(): pl.pallas_call(attend_theirs_kernel, out_shape=jax.ShapeDtypeStruct((4, 1...]
  transfers between devices with their start and end apart: 18 -> 18, of which waited for: 5 -> 5; matrix products, arithmetic and copies ran while one was open for 2% -> 2% of each run, Pallas kernels for 6% -> 7%
where the time goes in v5:
time: 138 us; the launch traced here: 137 us
  starting transfers between devices  53.8 us (39%)
  blocking collectives  49.8 us (36%)
  waiting for transfers between devices  15 us (11%)
  Pallas kernels  13.7 us (10%)
  local copies, waits for them, and re-layouts  3.28 us (2%)
  other arithmetic  1.43 us (1%)
    ppermute x18, starting transfers between devices, shift(): return lax.ppermute(array, axis, [(i, (i + by) % n) for i in range(n)])  53.8 us
    all_to_all x1, blocking collectives, on_device(): mine = lax.all_to_all(both, 'x', 0, 0)  20.9 us
    all_gather x1, blocking collectives, on_device(): enc, (first, second) = ring_of_eight(lax.all_gather(enc_states, 'zh'))  19.3 us
    ppermute x18, waiting for transfers between devices, shift(): return lax.ppermute(array, axis, [(i, (i + by) % n) for i in range(n)])  15 us
    all_to_all x1, blocking collectives, on_device(): mixed = lax.all_to_all(mixed, 'x', 0, 0)  9.63 us
    pallas_call x1, Pallas kernels, project_most(): pl.pallas_call(project_most_kernel, out_shape=(jax.ShapeDtypeStruct((2 *...  7.87 us
  transfers between devices with their start and end apart: 18, of which 5 were waited for; matrix products, arithmetic and copies ran while one was open for 2% of the time, Pallas kernels for 7%

profile of v5, /device:TPU:152, one launch (start us, length us, event | category | flops | bytes accessed | tf_op | source)
XLA Modules:
  0.0 137.5 jit_solution(6179532293763546081)
XLA Ops:
  0.0 0.0 copy-start.2
  0.0 1.4 pad_maximum_fusion.refs_7_
  1.4 3.4 %collective-permute-start.8 = (bf16[512,1024]{1,0:T(8,128)(2,1)S(1)}, bf16[512,1024]{1,0:T(8,128)(2,1)S(1)}, u32[]{:S(2)}, u32[]{:S(2)}) collective-permute-start(bf16[512,1024]{1,0:T(8,128)(2,1)S(1)} %pad_maximum_fusion.refs_7_), channel_id=1, source_target_pairs={{0,8},{8,16},{16,24},{24,0},{1,9},{9,17},{17,25},{25,1},{2,10},{10... | collective-permute-start | bytes 3145736 | tf_op jit(solution)/shard_map/ppermute | solution.py:23
  4.8 3.7 %collective-permute-start.9 = (bf16[512,1024]{1,0:T(8,128)(2,1)S(1)}, bf16[512,1024]{1,0:T(8,128)(2,1)}, u32[]{:S(2)}, u32[]{:S(2)}) collective-permute-start(bf16[512,1024]{1,0:T(8,128)(2,1)S(1)} %pad_maximum_fusion.refs_7_), channel_id=1, source_target_pairs={{0,24},{8,0},{16,8},{24,16},{1,25},{9,1},{17,9},{25,17},{2,26},{10... | collective-permute-start | bytes 3145736 | tf_op jit(solution)/shard_map/ppermute | solution.py:23
  8.4 0.0 copy-done.2
  8.4 19.3 %all-gather = bf16[4,256,256]{2,1,0:T(8,128)(2,1)S(1)} all-gather(bf16[2,256,256]{2,1,0:T(8,128)(2,1)S(1)} %copy-done.2), channel_id=2, replica_groups=mesh['zh'=2,'y'=8,'x'=4,'c'=2,'mp'=4] {'zh'}, dimensions={0}, use_global_device_ids=true | all-gather | bytes 786432 | tf_op jit(solution)/shard_map/all_gather | solution.py:236
  27.8 4.7 %collective-permute-start = (bf16[2,2,256,256]{3,2,1,0:T(8,128)(2,1)S(1)}, bf16[2,2,256,256]{3,2,1,0:T(8,128)(2,1)S(1)}, u32[]{:S(2)}, u32[]{:S(2)}) collective-permute-start(bf16[2,2,256,256]{3,2,1,0:T(8,128)(2,1)S(1)} %bitcast.13), channel_id=1, source_target_pairs={{0,32},{32,64},{64,96},{96,128},{128,160},{160,192},{192,224},{224... | collective-permute-start | bytes 1572872 | tf_op jit(solution)/shard_map/ppermute | solution.py:23
  32.4 1.9 %collective-permute-start.4 = (bf16[2,2,256,256]{3,2,1,0:T(8,128)(2,1)S(1)}, bf16[2,2,256,256]{3,2,1,0:T(8,128)(2,1)S(1)}, u32[]{:S(2)}, u32[]{:S(2)}) collective-permute-start(bf16[2,2,256,256]{3,2,1,0:T(8,128)(2,1)S(1)} %bitcast.14), channel_id=1, source_target_pairs={{0,224},{32,0},{64,32},{96,64},{128,96},{160,128},{192,160},{224,1... | collective-permute-start | bytes 1572872 | tf_op jit(solution)/shard_map/ppermute | solution.py:23
  34.4 9.3 %collective-permute-done.refs_1_ = bf16[2,2,256,256]{3,2,1,0:T(8,128)(2,1)S(1)} collective-permute-done((bf16[2,2,256,256]{3,2,1,0:T(8,128)(2,1)S(1)}, bf16[2,2,256,256]{3,2,1,0:T(8,128)(2,1)S(1)}, u32[]{:S(2)}, u32[]{:S(2)}) %collective-permute-start) | collective-permute-done | bytes 524320 | tf_op jit(solution)/shard_map/ppermute | solution.py:23
  43.7 0.0 copy-start.3
  43.7 5.6 %collective-permute-start.1 = (bf16[2,2,256,256]{3,2,1,0:T(8,128)(2,1)S(1)}, bf16[2,2,256,256]{3,2,1,0:T(8,128)(2,1)}, u32[]{:S(2)}, u32[]{:S(2)}) collective-permute-start(bf16[2,2,256,256]{3,2,1,0:T(8,128)(2,1)S(1)} %collective-permute-done.refs_1_), channel_id=1, source_target_pairs={{0,32},{32,64},{64,96},{96,128},{128,160},{160,192},{192,224},{224... | collective-permute-start | bytes 1572872 | tf_op jit(solution)/shard_map/ppermute | solution.py:23
  49.3 0.0 collective-permute-done.4.refs_2_
  49.3 0.0 copy-start.4
  49.3 1.9 %collective-permute-start.5 = (bf16[2,2,256,256]{3,2,1,0:T(8,128)(2,1)S(1)}, bf16[2,2,256,256]{3,2,1,0:T(8,128)(2,1)}, u32[]{:S(2)}, u32[]{:S(2)}) collective-permute-start(bf16[2,2,256,256]{3,2,1,0:T(8,128)(2,1)S(1)} %collective-permute-done.4.refs_2_), channel_id=1, source_target_pairs={{0,224},{32,0},{64,32},{96,64},{128,96},{160,128},{192,160},{224,1... | collective-permute-start | bytes 1572872 | tf_op jit(solution)/shard_map/ppermute | solution.py:23
  51.2 0.0 collective-permute-done.8.refs_8_
  51.3 2.2 %collective-permute-start.10 = (bf16[256,1024]{1,0:T(8,128)(2,1)S(1)}, bf16[256,1024]{1,0:T(8,128)(2,1)S(1)}, u32[]{:S(2)}, u32[]{:S(2)}) collective-permute-start(bf16[256,1024]{1,0:T(8,128)(2,1)S(1)} %slice.18), channel_id=1, source_target_pairs={{0,8},{8,16},{16,24},{24,0},{1,9},{9,17},{17,25},{25,1},{2,10},{10... | collective-permute-start | bytes 1572872 | tf_op jit(solution)/shard_map/ppermute | solution.py:23
  53.5 0.0 collective-permute-done.9.refs_9_
  53.5 1.1 slice.19
  54.6 4.9 %collective-permute-start.11 = (bf16[256,1024]{1,0:T(8,128)(2,1)S(1)}, bf16[256,1024]{1,0:T(8,128)(2,1)S(1)}, u32[]{:S(2)}, u32[]{:S(2)}) collective-permute-start(bf16[256,1024]{1,0:T(8,128)(2,1)S(1)} %slice.19), channel_id=1, source_target_pairs={{0,24},{8,0},{16,8},{24,16},{1,25},{9,1},{17,9},{25,17},{2,26},{10... | collective-permute-start | bytes 1572872 | tf_op jit(solution)/shard_map/ppermute | solution.py:23
  59.5 0.2 collective-permute-done.1.refs_3_
  59.7 5.7 %collective-permute-start.2 = (bf16[2,2,256,256]{3,2,1,0:T(8,128)(2,1)}, bf16[2,2,256,256]{3,2,1,0:T(8,128)(2,1)S(1)}, u32[]{:S(2)}, u32[]{:S(2)}) collective-permute-start(bf16[2,2,256,256]{3,2,1,0:T(8,128)(2,1)} %collective-permute-done.1.refs_3_), channel_id=1, source_target_pairs={{0,32},{32,64},{64,96},{96,128},{128,160},{160,192},{192,224},{224... | collective-permute-start | bytes 1572872 | tf_op jit(solution)/shard_map/ppermute | solution.py:23
  65.4 0.0 collective-permute-done.5.refs_4_
  65.4 1.9 %collective-permute-start.6 = (bf16[2,2,256,256]{3,2,1,0:T(8,128)(2,1)}, bf16[2,2,256,256]{3,2,1,0:T(8,128)(2,1)}, u32[]{:S(2)}, u32[]{:S(2)}) collective-permute-start(bf16[2,2,256,256]{3,2,1,0:T(8,128)(2,1)} %collective-permute-done.5.refs_4_), channel_id=1, source_target_pairs={{0,224},{32,0},{64,32},{96,64},{128,96},{160,128},{192,160},{224,1... | collective-permute-start | bytes 1572872 | tf_op jit(solution)/shard_map/ppermute | solution.py:23
  67.3 1.9 %collective-permute-start.12 = (bf16[512,1024]{1,0:T(8,128)(2,1)S(1)}, bf16[512,1024]{1,0:T(8,128)(2,1)}, u32[]{:S(2)}, u32[]{:S(2)}) collective-permute-start(bf16[512,1024]{1,0:T(8,128)(2,1)S(1)} %pad_maximum_fusion.refs_7_), channel_id=1, source_target_pairs={{0,4},{4,0},{1,5},{5,1},{2,6},{6,2},{3,7},{7,3},{8,12},{12,8},{9,1... | collective-permute-start | bytes 3145736 | tf_op jit(solution)/shard_map/ppermute | solution.py:23
  69.2 0.0 collective-permute-done.10.refs_10_
  69.3 0.0 copy-start.5
  69.3 2.4 %collective-permute-start.13 = (bf16[512,1024]{1,0:T(8,128)(2,1)S(1)}, bf16[512,1024]{1,0:T(8,128)(2,1)}, u32[]{:S(2)}, u32[]{:S(2)}) collective-permute-start(bf16[512,1024]{1,0:T(8,128)(2,1)S(1)} %collective-permute-done.8.refs_8_), channel_id=1, source_target_pairs={{0,4},{4,0},{1,5},{5,1},{2,6},{6,2},{3,7},{7,3},{8,12},{12,8},{9,1... | collective-permute-start | bytes 3145736 | tf_op jit(solution)/shard_map/ppermute | solution.py:23
  71.7 0.0 collective-permute-done.11.refs_11_
  71.7 0.0 copy-done.3
  71.7 0.0 copy-start.6
  71.7 1.9 %collective-permute-start.14 = (bf16[512,1024]{1,0:T(8,128)(2,1)}, bf16[512,1024]{1,0:T(8,128)(2,1)}, u32[]{:S(2)}, u32[]{:S(2)}) collective-permute-start(bf16[512,1024]{1,0:T(8,128)(2,1)} %collective-permute-done.9.refs_9_), channel_id=1, source_target_pairs={{0,4},{4,0},{1,5},{5,1},{2,6},{6,2},{3,7},{7,3},{8,12},{12,8},{9,1... | collective-permute-start | bytes 3145736 | tf_op jit(solution)/shard_map/ppermute | solution.py:23
  73.6 0.0 copy-done.4
  73.6 0.0 copy-done.5
  73.7 0.0 copy-done.6
  73.7 1.5 %collective-permute-done.2.refs_5_ = bf16[2,2,256,256]{3,2,1,0:T(8,128)(2,1)S(1)} collective-permute-done((bf16[2,2,256,256]{3,2,1,0:T(8,128)(2,1)}, bf16[2,2,256,256]{3,2,1,0:T(8,128)(2,1)S(1)}, u32[]{:S(2)}, u32[]{:S(2)}) %collective-permute-start.2) | collective-permute-done | bytes 524320 | tf_op jit(solution)/shard_map/ppermute | solution.py:23
  75.2 1.9 %collective-permute-start.15 = (bf16[256,1024]{1,0:T(8,128)(2,1)}, bf16[256,1024]{1,0:T(8,128)(2,1)S(1)}, u32[]{:S(2)}, u32[]{:S(2)}) collective-permute-start(bf16[256,1024]{1,0:T(8,128)(2,1)} %copy-done.5), channel_id=1, source_target_pairs={{0,4},{4,0},{1,5},{5,1},{2,6},{6,2},{3,7},{7,3},{8,12},{12,8},{9,1... | collective-permute-start | bytes 1572872 | tf_op jit(solution)/shard_map/ppermute | solution.py:23
  77.1 3.4 %collective-permute-done.6.refs_6_ = bf16[2,2,256,256]{3,2,1,0:T(8,128)(2,1)} collective-permute-done((bf16[2,2,256,256]{3,2,1,0:T(8,128)(2,1)}, bf16[2,2,256,256]{3,2,1,0:T(8,128)(2,1)}, u32[]{:S(2)}, u32[]{:S(2)}) %collective-permute-start.6) | collective-permute-done | bytes 524320 | tf_op jit(solution)/shard_map/ppermute | solution.py:23
  80.5 1.9 %collective-permute-start.16 = (bf16[256,1024]{1,0:T(8,128)(2,1)}, bf16[256,1024]{1,0:T(8,128)(2,1)S(1)}, u32[]{:S(2)}, u32[]{:S(2)}) collective-permute-start(bf16[256,1024]{1,0:T(8,128)(2,1)} %copy-done.6), channel_id=1, source_target_pairs={{0,4},{4,0},{1,5},{5,1},{2,6},{6,2},{3,7},{7,3},{8,12},{12,8},{9,1... | collective-permute-start | bytes 1572872 | tf_op jit(solution)/shard_map/ppermute | solution.py:23
  82.4 0.1 pad_add_fusion.where
  82.5 1.0 slice_bitcast_fusion
  83.5 0.0 copy-start
  83.5 0.0 collective-permute-done.12.refs_12_
  83.5 2.7 %collective-permute-start.3 = (bf16[2,256,256]{2,1,0:T(8,128)(2,1)S(1)}, bf16[2,256,256]{2,1,0:T(8,128)(2,1)S(1)}, u32[]{:S(2)}, u32[]{:S(2)}) collective-permute-start(bf16[2,256,256]{2,1,0:T(8,128)(2,1)S(1)} %slice_bitcast_fusion.1), channel_id=1, source_target_pairs={{0,32},{32,64},{64,96},{96,128},{128,160},{160,192},{192,224},{224... | collective-permute-start | bytes 786440 | tf_op jit(solution)/shard_map/ppermute | solution.py:23
  86.2 0.0 collective-permute-done.15.refs_15_
  86.2 3.3 %collective-permute-start.7 = (bf16[2,256,256]{2,1,0:T(8,128)(2,1)S(1)}, bf16[2,256,256]{2,1,0:T(8,128)(2,1)S(1)}, u32[]{:S(2)}, u32[]{:S(2)}) collective-permute-start(bf16[2,256,256]{2,1,0:T(8,128)(2,1)S(1)} %slice_bitcast_fusion), channel_id=1, source_target_pairs={{0,224},{32,0},{64,32},{96,64},{128,96},{160,128},{192,160},{224,1... | collective-permute-start | bytes 786440 | tf_op jit(solution)/shard_map/ppermute | solution.py:23
  89.5 0.0 collective-permute-done.16.refs_16_
  89.5 0.0 collective-permute-done.13.refs_13_
  89.5 0.0 collective-permute-done.14.refs_14_
  89.5 7.9 %project_most.1 = (f32[512,1024]{1,0:T(8,128)S(1)}, bf16[2,256,1024]{2,1,0:T(8,128)(2,1)S(1)}) custom-call(s32[3]{0:T(128)S(1)} %pad_add_fusion.where, bf16[2,2,256,256]{3,2,1,0:T(8,128)(2,1)S(1)} %bitcast.15, bf16[2,2,256,256]{3,2,1,0:T(8,128)(2,1)} %copy-done.3, bf16[2,2,256,256]{3,2,1,0:T(8,128)(2,1)} %copy-done.4, ...), custom_call_target="tpu_custom_call" | custom-call | flops 3758096384 | bytes 14680064 | tf_op jit(solution)/shard_map/project_most/pallas_call | solution.py:113
  97.4 0.0 collective-permute-done.3.first
  97.4 0.0 collective-permute-done.7.second
  97.4 0.0 copy-done
  97.4 0.7 project_rest.1
  98.2 0.0 copy-start.1
  98.2 20.9 %all_to_all.10.mine = bf16[4,320,512]{2,1,0:T(8,128)(2,1)S(1)} all-to-all(bf16[4,320,512]{2,1,0:T(8,128)(2,1)S(1)} %project_rest.1), channel_id=1, replica_groups=mesh['zh'=2,'y'=8,'x'=4,'c'=2,'mp'=4] {'x'}, dimensions={0} | all-to-all | bytes 2621440 | tf_op jit(solution)/shard_map/all_to_all | solution.py:242
  119.1 1.9 %collective-permute-start.17 = (bf16[4,320,512]{2,1,0:T(8,128)(2,1)S(1)}, bf16[4,320,512]{2,1,0:T(8,128)(2,1)S(1)}, u32[]{:S(2)}, u32[]{:S(2)}) collective-permute-start(bf16[4,320,512]{2,1,0:T(8,128)(2,1)S(1)} %all_to_all.10.mine), channel_id=1, source_target_pairs={{0,4},{4,0},{1,5},{5,1},{2,6},{6,2},{3,7},{7,3},{8,12},{12,8},{9,1... | collective-permute-start | bytes 3932168 | tf_op jit(solution)/shard_map/ppermute | solution.py:23
  121.0 0.0 copy-done.1
  121.0 2.4 %attend_mine.1 = (f32[4,128,128]{2,1,0:T(8,128)S(1)}, f32[4,128,128]{2,1,0:T(8,128)S(1)}, f32[4,128,256]{2,1,0:T(8,128)S(1)}) custom-call(s32[3]{0:T(128)S(1)} %pad_add_fusion.where, s32[2]{0:T(128)S(1)} %copy-done.1, bf16[4,320,512]{2,1,0:T(8,128)(2,1)S(1)} %all_to_all.10.mine), custom_call_target="tpu_custom_call" | custom-call | flops 536870912 | bytes 2097152 | tf_op jit(solution)/shard_map/attend_mine/pallas_call | solution.py:211
  123.4 0.6 collective-permute-done.17.theirs
  124.0 2.7 %attend_theirs.1 = bf16[4,128,256]{2,1,0:T(8,128)(2,1)S(1)} custom-call(s32[3]{0:T(128)S(1)} %pad_add_fusion.where, s32[2]{0:T(128)S(1)} %copy-done.1, bf16[4,320,512]{2,1,0:T(8,128)(2,1)S(1)} %all_to_all.10.mine, bf16[4,320,512]{2,1,0:T(8,128)(2,1)S(1)} %collective-permute-done.17.theirs, f32[4,128,128]{2,1,0:T(8,128)S(1)} %get-tuple-element.12.top, ...), custom_call_target="tpu_custom_call" | custom-call | flops 536870912 | bytes 2097152 | tf_op jit(solution)/shard_map/attend_theirs/pallas_call | solution.py:220
  126.7 9.6 %all_to_all.11 = bf16[4,128,256]{2,1,0:T(8,128)(2,1)S(1)} all-to-all(bf16[4,128,256]{2,1,0:T(8,128)(2,1)S(1)} %attend_theirs.1), channel_id=1, replica_groups=mesh['zh'=2,'y'=8,'x'=4,'c'=2,'mp'=4] {'x'}, dimensions={0} | all-to-all | bytes 524288 | tf_op jit(solution)/shard_map/all_to_all | solution.py:245
  136.3 0.3 copy.7
  136.6 0.9 broadcast_in_dim_reshape.3
  (2 shorter events, 0.1 us)
Async XLA Ops:
  0.0 8.4 %copy-start.2 = (bf16[2,256,256]{2,1,0:T(8,128)(2,1)S(1)}, bf16[2,256,256]{2,1,0:T(8,128)(2,1)}, u32[]{:S(2)}) copy-start(bf16[2,256,256]{2,1,0:T(8,128)(2,1)} %param.6) | copy-start | bytes 786436
  1.4 49.9 %collective-permute-start.8 = (bf16[512,1024]{1,0:T(8,128)(2,1)S(1)}, bf16[512,1024]{1,0:T(8,128)(2,1)S(1)}, u32[]{:S(2)}, u32[]{:S(2)}) collective-permute-start(bf16[512,1024]{1,0:T(8,128)(2,1)S(1)} %pad_maximum_fusion.refs_7_), channel_id=1, source_target_pairs={{0,8},{8,16},{16,24},{24,0},{1,9},{9,17},{17,25},{25,1},{2,10},{10... | collective-permute-start | bytes 3145736 | tf_op jit(solution)/shard_map/ppermute | solution.py:23
  4.8 48.7 %collective-permute-start.9 = (bf16[512,1024]{1,0:T(8,128)(2,1)S(1)}, bf16[512,1024]{1,0:T(8,128)(2,1)}, u32[]{:S(2)}, u32[]{:S(2)}) collective-permute-start(bf16[512,1024]{1,0:T(8,128)(2,1)S(1)} %pad_maximum_fusion.refs_7_), channel_id=1, source_target_pairs={{0,24},{8,0},{16,8},{24,16},{1,25},{9,1},{17,9},{25,17},{2,26},{10... | collective-permute-start | bytes 3145736 | tf_op jit(solution)/shard_map/ppermute | solution.py:23
  27.8 15.9 %collective-permute-start = (bf16[2,2,256,256]{3,2,1,0:T(8,128)(2,1)S(1)}, bf16[2,2,256,256]{3,2,1,0:T(8,128)(2,1)S(1)}, u32[]{:S(2)}, u32[]{:S(2)}) collective-permute-start(bf16[2,2,256,256]{3,2,1,0:T(8,128)(2,1)S(1)} %bitcast.13), channel_id=1, source_target_pairs={{0,32},{32,64},{64,96},{96,128},{128,160},{160,192},{192,224},{224... | collective-permute-start | bytes 1572872 | tf_op jit(solution)/shard_map/ppermute | solution.py:23
  32.4 16.8 %collective-permute-start.4 = (bf16[2,2,256,256]{3,2,1,0:T(8,128)(2,1)S(1)}, bf16[2,2,256,256]{3,2,1,0:T(8,128)(2,1)S(1)}, u32[]{:S(2)}, u32[]{:S(2)}) collective-permute-start(bf16[2,2,256,256]{3,2,1,0:T(8,128)(2,1)S(1)} %bitcast.14), channel_id=1, source_target_pairs={{0,224},{32,0},{64,32},{96,64},{128,96},{160,128},{192,160},{224,1... | collective-permute-start | bytes 1572872 | tf_op jit(solution)/shard_map/ppermute | solution.py:23
  43.7 28.0 %copy-start.3 = (bf16[2,2,256,256]{3,2,1,0:T(8,128)(2,1)}, bf16[2,2,256,256]{3,2,1,0:T(8,128)(2,1)S(1)}, u32[]{:S(2)}) copy-start(bf16[2,2,256,256]{3,2,1,0:T(8,128)(2,1)S(1)} %collective-permute-done.refs_1_) | copy-start | bytes 1572868
  43.7 16.0 %collective-permute-start.1 = (bf16[2,2,256,256]{3,2,1,0:T(8,128)(2,1)S(1)}, bf16[2,2,256,256]{3,2,1,0:T(8,128)(2,1)}, u32[]{:S(2)}, u32[]{:S(2)}) collective-permute-start(bf16[2,2,256,256]{3,2,1,0:T(8,128)(2,1)S(1)} %collective-permute-done.refs_1_), channel_id=1, source_target_pairs={{0,32},{32,64},{64,96},{96,128},{128,160},{160,192},{192,224},{224... | collective-permute-start | bytes 1572872 | tf_op jit(solution)/shard_map/ppermute | solution.py:23
  49.3 24.3 %copy-start.4 = (bf16[2,2,256,256]{3,2,1,0:T(8,128)(2,1)}, bf16[2,2,256,256]{3,2,1,0:T(8,128)(2,1)S(1)}, u32[]{:S(2)}) copy-start(bf16[2,2,256,256]{3,2,1,0:T(8,128)(2,1)S(1)} %collective-permute-done.4.refs_2_) | copy-start | bytes 1572868
  49.3 16.1 %collective-permute-start.5 = (bf16[2,2,256,256]{3,2,1,0:T(8,128)(2,1)S(1)}, bf16[2,2,256,256]{3,2,1,0:T(8,128)(2,1)}, u32[]{:S(2)}, u32[]{:S(2)}) collective-permute-start(bf16[2,2,256,256]{3,2,1,0:T(8,128)(2,1)S(1)} %collective-permute-done.4.refs_2_), channel_id=1, source_target_pairs={{0,224},{32,0},{64,32},{96,64},{128,96},{160,128},{192,160},{224,1... | collective-permute-start | bytes 1572872 | tf_op jit(solution)/shard_map/ppermute | solution.py:23
  51.3 18.0 %collective-permute-start.10 = (bf16[256,1024]{1,0:T(8,128)(2,1)S(1)}, bf16[256,1024]{1,0:T(8,128)(2,1)S(1)}, u32[]{:S(2)}, u32[]{:S(2)}) collective-permute-start(bf16[256,1024]{1,0:T(8,128)(2,1)S(1)} %slice.18), channel_id=1, source_target_pairs={{0,8},{8,16},{16,24},{24,0},{1,9},{9,17},{17,25},{25,1},{2,10},{10... | collective-permute-start | bytes 1572872 | tf_op jit(solution)/shard_map/ppermute | solution.py:23
  54.6 17.1 %collective-permute-start.11 = (bf16[256,1024]{1,0:T(8,128)(2,1)S(1)}, bf16[256,1024]{1,0:T(8,128)(2,1)S(1)}, u32[]{:S(2)}, u32[]{:S(2)}) collective-permute-start(bf16[256,1024]{1,0:T(8,128)(2,1)S(1)} %slice.19), channel_id=1, source_target_pairs={{0,24},{8,0},{16,8},{24,16},{1,25},{9,1},{17,9},{25,17},{2,26},{10... | collective-permute-start | bytes 1572872 | tf_op jit(solution)/shard_map/ppermute | solution.py:23
  59.7 15.5 %collective-permute-start.2 = (bf16[2,2,256,256]{3,2,1,0:T(8,128)(2,1)}, bf16[2,2,256,256]{3,2,1,0:T(8,128)(2,1)S(1)}, u32[]{:S(2)}, u32[]{:S(2)}) collective-permute-start(bf16[2,2,256,256]{3,2,1,0:T(8,128)(2,1)} %collective-permute-done.1.refs_3_), channel_id=1, source_target_pairs={{0,32},{32,64},{64,96},{96,128},{128,160},{160,192},{192,224},{224... | collective-permute-start | bytes 1572872 | tf_op jit(solution)/shard_map/ppermute | solution.py:23
  65.4 15.1 %collective-permute-start.6 = (bf16[2,2,256,256]{3,2,1,0:T(8,128)(2,1)}, bf16[2,2,256,256]{3,2,1,0:T(8,128)(2,1)}, u32[]{:S(2)}, u32[]{:S(2)}) collective-permute-start(bf16[2,2,256,256]{3,2,1,0:T(8,128)(2,1)} %collective-permute-done.5.refs_4_), channel_id=1, source_target_pairs={{0,224},{32,0},{64,32},{96,64},{128,96},{160,128},{192,160},{224,1... | collective-permute-start | bytes 1572872 | tf_op jit(solution)/shard_map/ppermute | solution.py:23
  67.3 16.2 %collective-permute-start.12 = (bf16[512,1024]{1,0:T(8,128)(2,1)S(1)}, bf16[512,1024]{1,0:T(8,128)(2,1)}, u32[]{:S(2)}, u32[]{:S(2)}) collective-permute-start(bf16[512,1024]{1,0:T(8,128)(2,1)S(1)} %pad_maximum_fusion.refs_7_), channel_id=1, source_target_pairs={{0,4},{4,0},{1,5},{5,1},{2,6},{6,2},{3,7},{7,3},{8,12},{12,8},{9,1... | collective-permute-start | bytes 3145736 | tf_op jit(solution)/shard_map/ppermute | solution.py:23
  69.3 4.4 %copy-start.5 = (bf16[256,1024]{1,0:T(8,128)(2,1)}, bf16[256,1024]{1,0:T(8,128)(2,1)S(1)}, u32[]{:S(2)}) copy-start(bf16[256,1024]{1,0:T(8,128)(2,1)S(1)} %collective-permute-done.10.refs_10_) | copy-start | bytes 1572868
  69.3 20.3 %collective-permute-start.13 = (bf16[512,1024]{1,0:T(8,128)(2,1)S(1)}, bf16[512,1024]{1,0:T(8,128)(2,1)}, u32[]{:S(2)}, u32[]{:S(2)}) collective-permute-start(bf16[512,1024]{1,0:T(8,128)(2,1)S(1)} %collective-permute-done.8.refs_8_), channel_id=1, source_target_pairs={{0,4},{4,0},{1,5},{5,1},{2,6},{6,2},{3,7},{7,3},{8,12},{12,8},{9,1... | collective-permute-start | bytes 3145736 | tf_op jit(solution)/shard_map/ppermute | solution.py:23
  71.7 2.0 %copy-start.6 = (bf16[256,1024]{1,0:T(8,128)(2,1)}, bf16[256,1024]{1,0:T(8,128)(2,1)S(1)}, u32[]{:S(2)}) copy-start(bf16[256,1024]{1,0:T(8,128)(2,1)S(1)} %collective-permute-done.11.refs_11_) | copy-start | bytes 1572868
  71.7 17.8 %collective-permute-start.14 = (bf16[512,1024]{1,0:T(8,128)(2,1)}, bf16[512,1024]{1,0:T(8,128)(2,1)}, u32[]{:S(2)}, u32[]{:S(2)}) collective-permute-start(bf16[512,1024]{1,0:T(8,128)(2,1)} %collective-permute-done.9.refs_9_), channel_id=1, source_target_pairs={{0,4},{4,0},{1,5},{5,1},{2,6},{6,2},{3,7},{7,3},{8,12},{12,8},{9,1... | collective-permute-start | bytes 3145736 | tf_op jit(solution)/shard_map/ppermute | solution.py:23
  75.2 11.1 %collective-permute-start.15 = (bf16[256,1024]{1,0:T(8,128)(2,1)}, bf16[256,1024]{1,0:T(8,128)(2,1)S(1)}, u32[]{:S(2)}, u32[]{:S(2)}) collective-permute-start(bf16[256,1024]{1,0:T(8,128)(2,1)} %copy-done.5), channel_id=1, source_target_pairs={{0,4},{4,0},{1,5},{5,1},{2,6},{6,2},{3,7},{7,3},{8,12},{12,8},{9,1... | collective-permute-start | bytes 1572872 | tf_op jit(solution)/shard_map/ppermute | solution.py:23
  80.5 9.0 %collective-permute-start.16 = (bf16[256,1024]{1,0:T(8,128)(2,1)}, bf16[256,1024]{1,0:T(8,128)(2,1)S(1)}, u32[]{:S(2)}, u32[]{:S(2)}) collective-permute-start(bf16[256,1024]{1,0:T(8,128)(2,1)} %copy-done.6), channel_id=1, source_target_pairs={{0,4},{4,0},{1,5},{5,1},{2,6},{6,2},{3,7},{7,3},{8,12},{12,8},{9,1... | collective-permute-start | bytes 1572872 | tf_op jit(solution)/shard_map/ppermute | solution.py:23
  83.5 14.0 %copy-start = (bf16[1,2,128,512]{3,2,1,0:T(8,128)(2,1)S(1)}, bf16[1,2,128,512]{3,2,1,0:T(8,128)(2,1)}, u32[]{:S(2)}) copy-start(bf16[1,2,128,512]{3,2,1,0:T(8,128)(2,1)} %queries.1) | copy-start | bytes 786436
  83.5 13.9 %collective-permute-start.3 = (bf16[2,256,256]{2,1,0:T(8,128)(2,1)S(1)}, bf16[2,256,256]{2,1,0:T(8,128)(2,1)S(1)}, u32[]{:S(2)}, u32[]{:S(2)}) collective-permute-start(bf16[2,256,256]{2,1,0:T(8,128)(2,1)S(1)} %slice_bitcast_fusion.1), channel_id=1, source_target_pairs={{0,32},{32,64},{64,96},{96,128},{128,160},{160,192},{192,224},{224... | collective-permute-start | bytes 786440 | tf_op jit(solution)/shard_map/ppermute | solution.py:23
  86.2 11.2 %collective-permute-start.7 = (bf16[2,256,256]{2,1,0:T(8,128)(2,1)S(1)}, bf16[2,256,256]{2,1,0:T(8,128)(2,1)S(1)}, u32[]{:S(2)}, u32[]{:S(2)}) collective-permute-start(bf16[2,256,256]{2,1,0:T(8,128)(2,1)S(1)} %slice_bitcast_fusion), channel_id=1, source_target_pairs={{0,224},{32,0},{64,32},{96,64},{128,96},{160,128},{192,160},{224,1... | collective-permute-start | bytes 786440 | tf_op jit(solution)/shard_map/ppermute | solution.py:23
  98.2 22.8 %copy-start.1 = (s32[2]{0:T(128)S(1)}, s32[2]{0:T(128)}, u32[]{:S(2)}) copy-start(s32[2]{0:T(128)} %lengths.3) | copy-start | bytes 28
  119.1 4.9 %collective-permute-start.17 = (bf16[4,320,512]{2,1,0:T(8,128)(2,1)S(1)}, bf16[4,320,512]{2,1,0:T(8,128)(2,1)S(1)}, u32[]{:S(2)}, u32[]{:S(2)}) collective-permute-start(bf16[4,320,512]{2,1,0:T(8,128)(2,1)S(1)} %all_to_all.10.mine), channel_id=1, source_target_pairs={{0,4},{4,0},{1,5},{5,1},{2,6},{6,2},{3,7},{7,3},{8,12},{12,8},{9,1... | collective-permute-start | bytes 3932168 | tf_op jit(solution)/shard_map/ppermute | solution.py:23

commit v6 on v5

--- a/solution.py
+++ b/solution.py
@@ -228,6 +228,22 @@
     )(where, lengths, mine, theirs, *state)
 
 
+def side_by_side_kernel(parts, out):
+    for doc in range(2):
+        for head in range(2):
+            out[0, doc, :, head * HEAD_DIM : (head + 1) * HEAD_DIM] = parts[doc * 2 + head]
+
+
+def side_by_side(parts):
+    return pl.pallas_call(
+        side_by_side_kernel,
+        out_shape=jax.ShapeDtypeStruct((1, 2, 128, 2 * HEAD_DIM), jnp.bfloat16),
+        in_specs=[VMEM],
+        out_specs=VMEM,
+        name="side_by_side",
+    )(parts)
+
+
 def on_device(queries, enc_states, key_weight, value_weight, enc_lengths):
     where = jnp.stack([lax.axis_index("y"), lax.axis_index("x"), lax.axis_index("c")])
     weight = jnp.concatenate([key_weight[0], value_weight[0]], axis=1)
@@ -242,9 +258,7 @@
     mine = lax.all_to_all(both, "x", 0, 0)
     theirs = shift(mine, "c", 1)
     mixed = attend(where, enc_lengths, mine, theirs)
-    mixed = lax.all_to_all(mixed, "x", 0, 0)
-    mixed = mixed.reshape(2, 2, 128, HEAD_DIM).transpose(0, 2, 1, 3).reshape(2, 128, 2 * HEAD_DIM)
-    return mixed[None]
+    return side_by_side(lax.all_to_all(mixed, "x", 0, 0))
 
 
 def solution(mesh):

time: 138 us -> 140 us (1.014)
  Pallas kernels: 13.7 us -> 15.4 us
    pallas_call x0 -> x1, Pallas kernels: none -> 1.67 us  [side_by_side(): pl.pallas_call(side_by_side_kernel, out_shape=jax.ShapeDtypeStruct((1, 2,...]
where the time goes in v6:
time: 140 us; the launch traced here: 139 us
  starting transfers between devices  53.8 us (38%)
  blocking collectives  50.5 us (36%)
  Pallas kernels  15.4 us (11%)
  waiting for transfers between devices  15 us (11%)
  local copies, waits for them, and re-layouts  2.13 us (2%)
  other arithmetic  1.43 us (1%)
    ppermute x18, starting transfers between devices, shift(): return lax.ppermute(array, axis, [(i, (i + by) % n) for i in range(n)])  53.8 us
    all_to_all x1, blocking collectives, on_device(): mine = lax.all_to_all(both, 'x', 0, 0)  20.9 us
    all_gather x1, blocking collectives, on_device(): enc, (first, second) = ring_of_eight(lax.all_gather(enc_states, 'zh'))  19.3 us
    ppermute x18, waiting for transfers between devices, shift(): return lax.ppermute(array, axis, [(i, (i + by) % n) for i in range(n)])  15 us
    all_to_all x1, blocking collectives, on_device(): return side_by_side(lax.all_to_all(mixed, 'x', 0, 0))  10.3 us
    pallas_call x1, Pallas kernels, project_most(): pl.pallas_call(project_most_kernel, out_shape=(jax.ShapeDtypeStruct((2 *...  7.87 us
  transfers between devices with their start and end apart: 18, of which 5 were waited for; matrix products, arithmetic and copies ran while one was open for 2% of the time, Pallas kernels for 7%

profile of v6, /device:TPU:152, one launch (start us, length us, event | category | flops | bytes accessed | tf_op | source)
XLA Modules:
  0.0 138.7 jit_solution(16628834539899230663)
XLA Ops:
  0.0 0.0 copy-start.2
  0.0 1.4 pad_maximum_fusion.refs_7_
  1.4 3.4 %collective-permute-start.8 = (bf16[512,1024]{1,0:T(8,128)(2,1)S(1)}, bf16[512,1024]{1,0:T(8,128)(2,1)S(1)}, u32[]{:S(2)}, u32[]{:S(2)}) collective-permute-start(bf16[512,1024]{1,0:T(8,128)(2,1)S(1)} %pad_maximum_fusion.refs_7_), channel_id=1, source_target_pairs={{0,8},{8,16},{16,24},{24,0},{1,9},{9,17},{17,25},{25,1},{2,10},{10... | collective-permute-start | bytes 3145736 | tf_op jit(solution)/shard_map/ppermute | solution.py:23
  4.8 3.7 %collective-permute-start.9 = (bf16[512,1024]{1,0:T(8,128)(2,1)S(1)}, bf16[512,1024]{1,0:T(8,128)(2,1)}, u32[]{:S(2)}, u32[]{:S(2)}) collective-permute-start(bf16[512,1024]{1,0:T(8,128)(2,1)S(1)} %pad_maximum_fusion.refs_7_), channel_id=1, source_target_pairs={{0,24},{8,0},{16,8},{24,16},{1,25},{9,1},{17,9},{25,17},{2,26},{10... | collective-permute-start | bytes 3145736 | tf_op jit(solution)/shard_map/ppermute | solution.py:23
  8.4 0.0 copy-done.2
  8.4 19.3 %all-gather = bf16[4,256,256]{2,1,0:T(8,128)(2,1)S(1)} all-gather(bf16[2,256,256]{2,1,0:T(8,128)(2,1)S(1)} %copy-done.2), channel_id=2, replica_groups=mesh['zh'=2,'y'=8,'x'=4,'c'=2,'mp'=4] {'zh'}, dimensions={0}, use_global_device_ids=true | all-gather | bytes 786432 | tf_op jit(solution)/shard_map/all_gather | solution.py:252
  27.8 4.7 %collective-permute-start = (bf16[2,2,256,256]{3,2,1,0:T(8,128)(2,1)S(1)}, bf16[2,2,256,256]{3,2,1,0:T(8,128)(2,1)S(1)}, u32[]{:S(2)}, u32[]{:S(2)}) collective-permute-start(bf16[2,2,256,256]{3,2,1,0:T(8,128)(2,1)S(1)} %bitcast.10), channel_id=1, source_target_pairs={{0,32},{32,64},{64,96},{96,128},{128,160},{160,192},{192,224},{224... | collective-permute-start | bytes 1572872 | tf_op jit(solution)/shard_map/ppermute | solution.py:23
  32.4 1.9 %collective-permute-start.4 = (bf16[2,2,256,256]{3,2,1,0:T(8,128)(2,1)S(1)}, bf16[2,2,256,256]{3,2,1,0:T(8,128)(2,1)S(1)}, u32[]{:S(2)}, u32[]{:S(2)}) collective-permute-start(bf16[2,2,256,256]{3,2,1,0:T(8,128)(2,1)S(1)} %bitcast.11), channel_id=1, source_target_pairs={{0,224},{32,0},{64,32},{96,64},{128,96},{160,128},{192,160},{224,1... | collective-permute-start | bytes 1572872 | tf_op jit(solution)/shard_map/ppermute | solution.py:23
  34.4 9.3 %collective-permute-done.refs_1_ = bf16[2,2,256,256]{3,2,1,0:T(8,128)(2,1)S(1)} collective-permute-done((bf16[2,2,256,256]{3,2,1,0:T(8,128)(2,1)S(1)}, bf16[2,2,256,256]{3,2,1,0:T(8,128)(2,1)S(1)}, u32[]{:S(2)}, u32[]{:S(2)}) %collective-permute-start) | collective-permute-done | bytes 524320 | tf_op jit(solution)/shard_map/ppermute | solution.py:23
  43.7 0.0 copy-start.3
  43.7 5.6 %collective-permute-start.1 = (bf16[2,2,256,256]{3,2,1,0:T(8,128)(2,1)S(1)}, bf16[2,2,256,256]{3,2,1,0:T(8,128)(2,1)}, u32[]{:S(2)}, u32[]{:S(2)}) collective-permute-start(bf16[2,2,256,256]{3,2,1,0:T(8,128)(2,1)S(1)} %collective-permute-done.refs_1_), channel_id=1, source_target_pairs={{0,32},{32,64},{64,96},{96,128},{128,160},{160,192},{192,224},{224... | collective-permute-start | bytes 1572872 | tf_op jit(solution)/shard_map/ppermute | solution.py:23
  49.3 0.0 collective-permute-done.4.refs_2_
  49.3 0.0 copy-start.4
  49.3 1.9 %collective-permute-start.5 = (bf16[2,2,256,256]{3,2,1,0:T(8,128)(2,1)S(1)}, bf16[2,2,256,256]{3,2,1,0:T(8,128)(2,1)}, u32[]{:S(2)}, u32[]{:S(2)}) collective-permute-start(bf16[2,2,256,256]{3,2,1,0:T(8,128)(2,1)S(1)} %collective-permute-done.4.refs_2_), channel_id=1, source_target_pairs={{0,224},{32,0},{64,32},{96,64},{128,96},{160,128},{192,160},{224,1... | collective-permute-start | bytes 1572872 | tf_op jit(solution)/shard_map/ppermute | solution.py:23
  51.2 0.0 collective-permute-done.8.refs_8_
  51.3 2.2 %collective-permute-start.10 = (bf16[256,1024]{1,0:T(8,128)(2,1)S(1)}, bf16[256,1024]{1,0:T(8,128)(2,1)S(1)}, u32[]{:S(2)}, u32[]{:S(2)}) collective-permute-start(bf16[256,1024]{1,0:T(8,128)(2,1)S(1)} %slice.18), channel_id=1, source_target_pairs={{0,8},{8,16},{16,24},{24,0},{1,9},{9,17},{17,25},{25,1},{2,10},{10... | collective-permute-start | bytes 1572872 | tf_op jit(solution)/shard_map/ppermute | solution.py:23
  53.5 0.0 collective-permute-done.9.refs_9_
  53.5 1.1 slice.19
  54.6 4.9 %collective-permute-start.11 = (bf16[256,1024]{1,0:T(8,128)(2,1)S(1)}, bf16[256,1024]{1,0:T(8,128)(2,1)S(1)}, u32[]{:S(2)}, u32[]{:S(2)}) collective-permute-start(bf16[256,1024]{1,0:T(8,128)(2,1)S(1)} %slice.19), channel_id=1, source_target_pairs={{0,24},{8,0},{16,8},{24,16},{1,25},{9,1},{17,9},{25,17},{2,26},{10... | collective-permute-start | bytes 1572872 | tf_op jit(solution)/shard_map/ppermute | solution.py:23
  59.5 0.2 collective-permute-done.1.refs_3_
  59.7 5.7 %collective-permute-start.2 = (bf16[2,2,256,256]{3,2,1,0:T(8,128)(2,1)}, bf16[2,2,256,256]{3,2,1,0:T(8,128)(2,1)S(1)}, u32[]{:S(2)}, u32[]{:S(2)}) collective-permute-start(bf16[2,2,256,256]{3,2,1,0:T(8,128)(2,1)} %collective-permute-done.1.refs_3_), channel_id=1, source_target_pairs={{0,32},{32,64},{64,96},{96,128},{128,160},{160,192},{192,224},{224... | collective-permute-start | bytes 1572872 | tf_op jit(solution)/shard_map/ppermute | solution.py:23
  65.4 0.0 collective-permute-done.5.refs_4_
  65.4 1.9 %collective-permute-start.6 = (bf16[2,2,256,256]{3,2,1,0:T(8,128)(2,1)}, bf16[2,2,256,256]{3,2,1,0:T(8,128)(2,1)}, u32[]{:S(2)}, u32[]{:S(2)}) collective-permute-start(bf16[2,2,256,256]{3,2,1,0:T(8,128)(2,1)} %collective-permute-done.5.refs_4_), channel_id=1, source_target_pairs={{0,224},{32,0},{64,32},{96,64},{128,96},{160,128},{192,160},{224,1... | collective-permute-start | bytes 1572872 | tf_op jit(solution)/shard_map/ppermute | solution.py:23
  67.3 1.9 %collective-permute-start.12 = (bf16[512,1024]{1,0:T(8,128)(2,1)S(1)}, bf16[512,1024]{1,0:T(8,128)(2,1)}, u32[]{:S(2)}, u32[]{:S(2)}) collective-permute-start(bf16[512,1024]{1,0:T(8,128)(2,1)S(1)} %pad_maximum_fusion.refs_7_), channel_id=1, source_target_pairs={{0,4},{4,0},{1,5},{5,1},{2,6},{6,2},{3,7},{7,3},{8,12},{12,8},{9,1... | collective-permute-start | bytes 3145736 | tf_op jit(solution)/shard_map/ppermute | solution.py:23
  69.2 0.0 collective-permute-done.10.refs_10_
  69.3 0.0 copy-start.5
  69.3 2.4 %collective-permute-start.13 = (bf16[512,1024]{1,0:T(8,128)(2,1)S(1)}, bf16[512,1024]{1,0:T(8,128)(2,1)}, u32[]{:S(2)}, u32[]{:S(2)}) collective-permute-start(bf16[512,1024]{1,0:T(8,128)(2,1)S(1)} %collective-permute-done.8.refs_8_), channel_id=1, source_target_pairs={{0,4},{4,0},{1,5},{5,1},{2,6},{6,2},{3,7},{7,3},{8,12},{12,8},{9,1... | collective-permute-start | bytes 3145736 | tf_op jit(solution)/shard_map/ppermute | solution.py:23
  71.7 0.0 collective-permute-done.11.refs_11_
  71.7 0.0 copy-done.3
  71.7 0.0 copy-start.6
  71.7 1.9 %collective-permute-start.14 = (bf16[512,1024]{1,0:T(8,128)(2,1)}, bf16[512,1024]{1,0:T(8,128)(2,1)}, u32[]{:S(2)}, u32[]{:S(2)}) collective-permute-start(bf16[512,1024]{1,0:T(8,128)(2,1)} %collective-permute-done.9.refs_9_), channel_id=1, source_target_pairs={{0,4},{4,0},{1,5},{5,1},{2,6},{6,2},{3,7},{7,3},{8,12},{12,8},{9,1... | collective-permute-start | bytes 3145736 | tf_op jit(solution)/shard_map/ppermute | solution.py:23
  73.6 0.0 copy-done.4
  73.6 0.0 copy-done.5
  73.7 0.0 copy-done.6
  73.7 1.5 %collective-permute-done.2.refs_5_ = bf16[2,2,256,256]{3,2,1,0:T(8,128)(2,1)S(1)} collective-permute-done((bf16[2,2,256,256]{3,2,1,0:T(8,128)(2,1)}, bf16[2,2,256,256]{3,2,1,0:T(8,128)(2,1)S(1)}, u32[]{:S(2)}, u32[]{:S(2)}) %collective-permute-start.2) | collective-permute-done | bytes 524320 | tf_op jit(solution)/shard_map/ppermute | solution.py:23
  75.2 1.9 %collective-permute-start.15 = (bf16[256,1024]{1,0:T(8,128)(2,1)}, bf16[256,1024]{1,0:T(8,128)(2,1)S(1)}, u32[]{:S(2)}, u32[]{:S(2)}) collective-permute-start(bf16[256,1024]{1,0:T(8,128)(2,1)} %copy-done.5), channel_id=1, source_target_pairs={{0,4},{4,0},{1,5},{5,1},{2,6},{6,2},{3,7},{7,3},{8,12},{12,8},{9,1... | collective-permute-start | bytes 1572872 | tf_op jit(solution)/shard_map/ppermute | solution.py:23
  77.1 3.4 %collective-permute-done.6.refs_6_ = bf16[2,2,256,256]{3,2,1,0:T(8,128)(2,1)} collective-permute-done((bf16[2,2,256,256]{3,2,1,0:T(8,128)(2,1)}, bf16[2,2,256,256]{3,2,1,0:T(8,128)(2,1)}, u32[]{:S(2)}, u32[]{:S(2)}) %collective-permute-start.6) | collective-permute-done | bytes 524320 | tf_op jit(solution)/shard_map/ppermute | solution.py:23
  80.5 1.9 %collective-permute-start.16 = (bf16[256,1024]{1,0:T(8,128)(2,1)}, bf16[256,1024]{1,0:T(8,128)(2,1)S(1)}, u32[]{:S(2)}, u32[]{:S(2)}) collective-permute-start(bf16[256,1024]{1,0:T(8,128)(2,1)} %copy-done.6), channel_id=1, source_target_pairs={{0,4},{4,0},{1,5},{5,1},{2,6},{6,2},{3,7},{7,3},{8,12},{12,8},{9,1... | collective-permute-start | bytes 1572872 | tf_op jit(solution)/shard_map/ppermute | solution.py:23
  82.4 0.1 pad_add_fusion.where
  82.5 1.0 slice_bitcast_fusion
  83.5 0.0 copy-start
  83.5 0.0 collective-permute-done.12.refs_12_
  83.5 2.7 %collective-permute-start.3 = (bf16[2,256,256]{2,1,0:T(8,128)(2,1)S(1)}, bf16[2,256,256]{2,1,0:T(8,128)(2,1)S(1)}, u32[]{:S(2)}, u32[]{:S(2)}) collective-permute-start(bf16[2,256,256]{2,1,0:T(8,128)(2,1)S(1)} %slice_bitcast_fusion.1), channel_id=1, source_target_pairs={{0,32},{32,64},{64,96},{96,128},{128,160},{160,192},{192,224},{224... | collective-permute-start | bytes 786440 | tf_op jit(solution)/shard_map/ppermute | solution.py:23
  86.2 0.0 collective-permute-done.15.refs_15_
  86.2 3.3 %collective-permute-start.7 = (bf16[2,256,256]{2,1,0:T(8,128)(2,1)S(1)}, bf16[2,256,256]{2,1,0:T(8,128)(2,1)S(1)}, u32[]{:S(2)}, u32[]{:S(2)}) collective-permute-start(bf16[2,256,256]{2,1,0:T(8,128)(2,1)S(1)} %slice_bitcast_fusion), channel_id=1, source_target_pairs={{0,224},{32,0},{64,32},{96,64},{128,96},{160,128},{192,160},{224,1... | collective-permute-start | bytes 786440 | tf_op jit(solution)/shard_map/ppermute | solution.py:23
  89.5 0.0 collective-permute-done.16.refs_16_
  89.5 0.0 collective-permute-done.13.refs_13_
  89.5 0.0 collective-permute-done.14.refs_14_
  89.5 7.9 %project_most.1 = (f32[512,1024]{1,0:T(8,128)S(1)}, bf16[2,256,1024]{2,1,0:T(8,128)(2,1)S(1)}) custom-call(s32[3]{0:T(128)S(1)} %pad_add_fusion.where, bf16[2,2,256,256]{3,2,1,0:T(8,128)(2,1)S(1)} %bitcast.12, bf16[2,2,256,256]{3,2,1,0:T(8,128)(2,1)} %copy-done.3, bf16[2,2,256,256]{3,2,1,0:T(8,128)(2,1)} %copy-done.4, ...), custom_call_target="tpu_custom_call" | custom-call | flops 3758096384 | bytes 14680064 | tf_op jit(solution)/shard_map/project_most/pallas_call | solution.py:113
  97.4 0.0 collective-permute-done.3.first
  97.4 0.0 collective-permute-done.7.second
  97.4 0.0 copy-done
  97.4 0.7 project_rest.1
  98.2 0.0 copy-start.1
  98.2 20.9 %all_to_all.10.mine = bf16[4,320,512]{2,1,0:T(8,128)(2,1)S(1)} all-to-all(bf16[4,320,512]{2,1,0:T(8,128)(2,1)S(1)} %project_rest.1), channel_id=1, replica_groups=mesh['zh'=2,'y'=8,'x'=4,'c'=2,'mp'=4] {'x'}, dimensions={0} | all-to-all | bytes 2621440 | tf_op jit(solution)/shard_map/all_to_all | solution.py:258
  119.1 1.9 %collective-permute-start.17 = (bf16[4,320,512]{2,1,0:T(8,128)(2,1)S(1)}, bf16[4,320,512]{2,1,0:T(8,128)(2,1)S(1)}, u32[]{:S(2)}, u32[]{:S(2)}) collective-permute-start(bf16[4,320,512]{2,1,0:T(8,128)(2,1)S(1)} %all_to_all.10.mine), channel_id=1, source_target_pairs={{0,4},{4,0},{1,5},{5,1},{2,6},{6,2},{3,7},{7,3},{8,12},{12,8},{9,1... | collective-permute-start | bytes 3932168 | tf_op jit(solution)/shard_map/ppermute | solution.py:23
  121.0 0.0 copy-done.1
  121.0 2.4 %attend_mine.1 = (f32[4,128,128]{2,1,0:T(8,128)S(1)}, f32[4,128,128]{2,1,0:T(8,128)S(1)}, f32[4,128,256]{2,1,0:T(8,128)S(1)}) custom-call(s32[3]{0:T(128)S(1)} %pad_add_fusion.where, s32[2]{0:T(128)S(1)} %copy-done.1, bf16[4,320,512]{2,1,0:T(8,128)(2,1)S(1)} %all_to_all.10.mine), custom_call_target="tpu_custom_call" | custom-call | flops 536870912 | bytes 2097152 | tf_op jit(solution)/shard_map/attend_mine/pallas_call | solution.py:211
  123.4 0.6 collective-permute-done.17.theirs
  124.0 2.7 %attend_theirs.1 = bf16[4,128,256]{2,1,0:T(8,128)(2,1)S(1)} custom-call(s32[3]{0:T(128)S(1)} %pad_add_fusion.where, s32[2]{0:T(128)S(1)} %copy-done.1, bf16[4,320,512]{2,1,0:T(8,128)(2,1)S(1)} %all_to_all.10.mine, bf16[4,320,512]{2,1,0:T(8,128)(2,1)S(1)} %collective-permute-done.17.theirs, f32[4,128,128]{2,1,0:T(8,128)S(1)} %get-tuple-element.12.top, ...), custom_call_target="tpu_custom_call" | custom-call | flops 536870912 | bytes 2097152 | tf_op jit(solution)/shard_map/attend_theirs/pallas_call | solution.py:220
  126.7 10.3 %all_to_all.11.parts = bf16[4,128,256]{2,1,0:T(8,128)(2,1)} all-to-all(bf16[4,128,256]{2,1,0:T(8,128)(2,1)S(1)} %attend_theirs.1), channel_id=1, replica_groups=mesh['zh'=2,'y'=8,'x'=4,'c'=2,'mp'=4] {'x'}, dimensions={0} | all-to-all | bytes 524288 | tf_op jit(solution)/shard_map/all_to_all | solution.py:261
  137.0 1.7 %side_by_side.1 = bf16[1,2,128,512]{3,2,1,0:T(8,128)(2,1)} custom-call(bf16[4,128,256]{2,1,0:T(8,128)(2,1)} %all_to_all.11.parts), custom_call_target="tpu_custom_call" | custom-call | tf_op jit(solution)/shard_map/side_by_side/pallas_call | solution.py:238
  (2 shorter events, 0.1 us)
Async XLA Ops:
  0.0 8.4 %copy-start.2 = (bf16[2,256,256]{2,1,0:T(8,128)(2,1)S(1)}, bf16[2,256,256]{2,1,0:T(8,128)(2,1)}, u32[]{:S(2)}) copy-start(bf16[2,256,256]{2,1,0:T(8,128)(2,1)} %param.6) | copy-start | bytes 786436
  1.4 49.9 %collective-permute-start.8 = (bf16[512,1024]{1,0:T(8,128)(2,1)S(1)}, bf16[512,1024]{1,0:T(8,128)(2,1)S(1)}, u32[]{:S(2)}, u32[]{:S(2)}) collective-permute-start(bf16[512,1024]{1,0:T(8,128)(2,1)S(1)} %pad_maximum_fusion.refs_7_), channel_id=1, source_target_pairs={{0,8},{8,16},{16,24},{24,0},{1,9},{9,17},{17,25},{25,1},{2,10},{10... | collective-permute-start | bytes 3145736 | tf_op jit(solution)/shard_map/ppermute | solution.py:23
  4.8 48.7 %collective-permute-start.9 = (bf16[512,1024]{1,0:T(8,128)(2,1)S(1)}, bf16[512,1024]{1,0:T(8,128)(2,1)}, u32[]{:S(2)}, u32[]{:S(2)}) collective-permute-start(bf16[512,1024]{1,0:T(8,128)(2,1)S(1)} %pad_maximum_fusion.refs_7_), channel_id=1, source_target_pairs={{0,24},{8,0},{16,8},{24,16},{1,25},{9,1},{17,9},{25,17},{2,26},{10... | collective-permute-start | bytes 3145736 | tf_op jit(solution)/shard_map/ppermute | solution.py:23
  27.8 15.9 %collective-permute-start = (bf16[2,2,256,256]{3,2,1,0:T(8,128)(2,1)S(1)}, bf16[2,2,256,256]{3,2,1,0:T(8,128)(2,1)S(1)}, u32[]{:S(2)}, u32[]{:S(2)}) collective-permute-start(bf16[2,2,256,256]{3,2,1,0:T(8,128)(2,1)S(1)} %bitcast.10), channel_id=1, source_target_pairs={{0,32},{32,64},{64,96},{96,128},{128,160},{160,192},{192,224},{224... | collective-permute-start | bytes 1572872 | tf_op jit(solution)/shard_map/ppermute | solution.py:23
  32.4 16.8 %collective-permute-start.4 = (bf16[2,2,256,256]{3,2,1,0:T(8,128)(2,1)S(1)}, bf16[2,2,256,256]{3,2,1,0:T(8,128)(2,1)S(1)}, u32[]{:S(2)}, u32[]{:S(2)}) collective-permute-start(bf16[2,2,256,256]{3,2,1,0:T(8,128)(2,1)S(1)} %bitcast.11), channel_id=1, source_target_pairs={{0,224},{32,0},{64,32},{96,64},{128,96},{160,128},{192,160},{224,1... | collective-permute-start | bytes 1572872 | tf_op jit(solution)/shard_map/ppermute | solution.py:23
  43.7 28.0 %copy-start.3 = (bf16[2,2,256,256]{3,2,1,0:T(8,128)(2,1)}, bf16[2,2,256,256]{3,2,1,0:T(8,128)(2,1)S(1)}, u32[]{:S(2)}) copy-start(bf16[2,2,256,256]{3,2,1,0:T(8,128)(2,1)S(1)} %collective-permute-done.refs_1_) | copy-start | bytes 1572868
  43.7 16.0 %collective-permute-start.1 = (bf16[2,2,256,256]{3,2,1,0:T(8,128)(2,1)S(1)}, bf16[2,2,256,256]{3,2,1,0:T(8,128)(2,1)}, u32[]{:S(2)}, u32[]{:S(2)}) collective-permute-start(bf16[2,2,256,256]{3,2,1,0:T(8,128)(2,1)S(1)} %collective-permute-done.refs_1_), channel_id=1, source_target_pairs={{0,32},{32,64},{64,96},{96,128},{128,160},{160,192},{192,224},{224... | collective-permute-start | bytes 1572872 | tf_op jit(solution)/shard_map/ppermute | solution.py:23
  49.3 24.3 %copy-start.4 = (bf16[2,2,256,256]{3,2,1,0:T(8,128)(2,1)}, bf16[2,2,256,256]{3,2,1,0:T(8,128)(2,1)S(1)}, u32[]{:S(2)}) copy-start(bf16[2,2,256,256]{3,2,1,0:T(8,128)(2,1)S(1)} %collective-permute-done.4.refs_2_) | copy-start | bytes 1572868
  49.3 16.1 %collective-permute-start.5 = (bf16[2,2,256,256]{3,2,1,0:T(8,128)(2,1)S(1)}, bf16[2,2,256,256]{3,2,1,0:T(8,128)(2,1)}, u32[]{:S(2)}, u32[]{:S(2)}) collective-permute-start(bf16[2,2,256,256]{3,2,1,0:T(8,128)(2,1)S(1)} %collective-permute-done.4.refs_2_), channel_id=1, source_target_pairs={{0,224},{32,0},{64,32},{96,64},{128,96},{160,128},{192,160},{224,1... | collective-permute-start | bytes 1572872 | tf_op jit(solution)/shard_map/ppermute | solution.py:23
  51.3 18.0 %collective-permute-start.10 = (bf16[256,1024]{1,0:T(8,128)(2,1)S(1)}, bf16[256,1024]{1,0:T(8,128)(2,1)S(1)}, u32[]{:S(2)}, u32[]{:S(2)}) collective-permute-start(bf16[256,1024]{1,0:T(8,128)(2,1)S(1)} %slice.18), channel_id=1, source_target_pairs={{0,8},{8,16},{16,24},{24,0},{1,9},{9,17},{17,25},{25,1},{2,10},{10... | collective-permute-start | bytes 1572872 | tf_op jit(solution)/shard_map/ppermute | solution.py:23
  54.6 17.1 %collective-permute-start.11 = (bf16[256,1024]{1,0:T(8,128)(2,1)S(1)}, bf16[256,1024]{1,0:T(8,128)(2,1)S(1)}, u32[]{:S(2)}, u32[]{:S(2)}) collective-permute-start(bf16[256,1024]{1,0:T(8,128)(2,1)S(1)} %slice.19), channel_id=1, source_target_pairs={{0,24},{8,0},{16,8},{24,16},{1,25},{9,1},{17,9},{25,17},{2,26},{10... | collective-permute-start | bytes 1572872 | tf_op jit(solution)/shard_map/ppermute | solution.py:23
  59.7 15.5 %collective-permute-start.2 = (bf16[2,2,256,256]{3,2,1,0:T(8,128)(2,1)}, bf16[2,2,256,256]{3,2,1,0:T(8,128)(2,1)S(1)}, u32[]{:S(2)}, u32[]{:S(2)}) collective-permute-start(bf16[2,2,256,256]{3,2,1,0:T(8,128)(2,1)} %collective-permute-done.1.refs_3_), channel_id=1, source_target_pairs={{0,32},{32,64},{64,96},{96,128},{128,160},{160,192},{192,224},{224... | collective-permute-start | bytes 1572872 | tf_op jit(solution)/shard_map/ppermute | solution.py:23
  65.4 15.1 %collective-permute-start.6 = (bf16[2,2,256,256]{3,2,1,0:T(8,128)(2,1)}, bf16[2,2,256,256]{3,2,1,0:T(8,128)(2,1)}, u32[]{:S(2)}, u32[]{:S(2)}) collective-permute-start(bf16[2,2,256,256]{3,2,1,0:T(8,128)(2,1)} %collective-permute-done.5.refs_4_), channel_id=1, source_target_pairs={{0,224},{32,0},{64,32},{96,64},{128,96},{160,128},{192,160},{224,1... | collective-permute-start | bytes 1572872 | tf_op jit(solution)/shard_map/ppermute | solution.py:23
  67.3 16.2 %collective-permute-start.12 = (bf16[512,1024]{1,0:T(8,128)(2,1)S(1)}, bf16[512,1024]{1,0:T(8,128)(2,1)}, u32[]{:S(2)}, u32[]{:S(2)}) collective-permute-start(bf16[512,1024]{1,0:T(8,128)(2,1)S(1)} %pad_maximum_fusion.refs_7_), channel_id=1, source_target_pairs={{0,4},{4,0},{1,5},{5,1},{2,6},{6,2},{3,7},{7,3},{8,12},{12,8},{9,1... | collective-permute-start | bytes 3145736 | tf_op jit(solution)/shard_map/ppermute | solution.py:23
  69.3 4.4 %copy-start.5 = (bf16[256,1024]{1,0:T(8,128)(2,1)}, bf16[256,1024]{1,0:T(8,128)(2,1)S(1)}, u32[]{:S(2)}) copy-start(bf16[256,1024]{1,0:T(8,128)(2,1)S(1)} %collective-permute-done.10.refs_10_) | copy-start | bytes 1572868
  69.3 20.3 %collective-permute-start.13 = (bf16[512,1024]{1,0:T(8,128)(2,1)S(1)}, bf16[512,1024]{1,0:T(8,128)(2,1)}, u32[]{:S(2)}, u32[]{:S(2)}) collective-permute-start(bf16[512,1024]{1,0:T(8,128)(2,1)S(1)} %collective-permute-done.8.refs_8_), channel_id=1, source_target_pairs={{0,4},{4,0},{1,5},{5,1},{2,6},{6,2},{3,7},{7,3},{8,12},{12,8},{9,1... | collective-permute-start | bytes 3145736 | tf_op jit(solution)/shard_map/ppermute | solution.py:23
  71.7 2.0 %copy-start.6 = (bf16[256,1024]{1,0:T(8,128)(2,1)}, bf16[256,1024]{1,0:T(8,128)(2,1)S(1)}, u32[]{:S(2)}) copy-start(bf16[256,1024]{1,0:T(8,128)(2,1)S(1)} %collective-permute-done.11.refs_11_) | copy-start | bytes 1572868
  71.7 17.8 %collective-permute-start.14 = (bf16[512,1024]{1,0:T(8,128)(2,1)}, bf16[512,1024]{1,0:T(8,128)(2,1)}, u32[]{:S(2)}, u32[]{:S(2)}) collective-permute-start(bf16[512,1024]{1,0:T(8,128)(2,1)} %collective-permute-done.9.refs_9_), channel_id=1, source_target_pairs={{0,4},{4,0},{1,5},{5,1},{2,6},{6,2},{3,7},{7,3},{8,12},{12,8},{9,1... | collective-permute-start | bytes 3145736 | tf_op jit(solution)/shard_map/ppermute | solution.py:23
  75.2 11.1 %collective-permute-start.15 = (bf16[256,1024]{1,0:T(8,128)(2,1)}, bf16[256,1024]{1,0:T(8,128)(2,1)S(1)}, u32[]{:S(2)}, u32[]{:S(2)}) collective-permute-start(bf16[256,1024]{1,0:T(8,128)(2,1)} %copy-done.5), channel_id=1, source_target_pairs={{0,4},{4,0},{1,5},{5,1},{2,6},{6,2},{3,7},{7,3},{8,12},{12,8},{9,1... | collective-permute-start | bytes 1572872 | tf_op jit(solution)/shard_map/ppermute | solution.py:23
  80.5 9.0 %collective-permute-start.16 = (bf16[256,1024]{1,0:T(8,128)(2,1)}, bf16[256,1024]{1,0:T(8,128)(2,1)S(1)}, u32[]{:S(2)}, u32[]{:S(2)}) collective-permute-start(bf16[256,1024]{1,0:T(8,128)(2,1)} %copy-done.6), channel_id=1, source_target_pairs={{0,4},{4,0},{1,5},{5,1},{2,6},{6,2},{3,7},{7,3},{8,12},{12,8},{9,1... | collective-permute-start | bytes 1572872 | tf_op jit(solution)/shard_map/ppermute | solution.py:23
  83.5 14.0 %copy-start = (bf16[1,2,128,512]{3,2,1,0:T(8,128)(2,1)S(1)}, bf16[1,2,128,512]{3,2,1,0:T(8,128)(2,1)}, u32[]{:S(2)}) copy-start(bf16[1,2,128,512]{3,2,1,0:T(8,128)(2,1)} %queries.1) | copy-start | bytes 786436
  83.5 13.9 %collective-permute-start.3 = (bf16[2,256,256]{2,1,0:T(8,128)(2,1)S(1)}, bf16[2,256,256]{2,1,0:T(8,128)(2,1)S(1)}, u32[]{:S(2)}, u32[]{:S(2)}) collective-permute-start(bf16[2,256,256]{2,1,0:T(8,128)(2,1)S(1)} %slice_bitcast_fusion.1), channel_id=1, source_target_pairs={{0,32},{32,64},{64,96},{96,128},{128,160},{160,192},{192,224},{224... | collective-permute-start | bytes 786440 | tf_op jit(solution)/shard_map/ppermute | solution.py:23
  86.2 11.2 %collective-permute-start.7 = (bf16[2,256,256]{2,1,0:T(8,128)(2,1)S(1)}, bf16[2,256,256]{2,1,0:T(8,128)(2,1)S(1)}, u32[]{:S(2)}, u32[]{:S(2)}) collective-permute-start(bf16[2,256,256]{2,1,0:T(8,128)(2,1)S(1)} %slice_bitcast_fusion), channel_id=1, source_target_pairs={{0,224},{32,0},{64,32},{96,64},{128,96},{160,128},{192,160},{224,1... | collective-permute-start | bytes 786440 | tf_op jit(solution)/shard_map/ppermute | solution.py:23
  98.2 22.8 %copy-start.1 = (s32[2]{0:T(128)S(1)}, s32[2]{0:T(128)}, u32[]{:S(2)}) copy-start(s32[2]{0:T(128)} %lengths.3) | copy-start | bytes 28
  119.1 4.9 %collective-permute-start.17 = (bf16[4,320,512]{2,1,0:T(8,128)(2,1)S(1)}, bf16[4,320,512]{2,1,0:T(8,128)(2,1)S(1)}, u32[]{:S(2)}, u32[]{:S(2)}) collective-permute-start(bf16[4,320,512]{2,1,0:T(8,128)(2,1)S(1)} %all_to_all.10.mine), channel_id=1, source_target_pairs={{0,4},{4,0},{1,5},{5,1},{2,6},{6,2},{3,7},{7,3},{8,12},{12,8},{9,1... | collective-permute-start | bytes 3932168 | tf_op jit(solution)/shard_map/ppermute | solution.py:23
